TPU v7x, 32 devices: a whole 2x2x4 slice. The times are simulated.
32 devices in a mesh: dp: 8 (over z, core), seq: 4 (over y, x).
Axes of the slice: x: 2, y: 2, z: 4, core: 2. Of those that a mesh axis runs over, the one named last changes fastest.
Arguments:
- tokens: bfloat16 [8, 64, 16, 1152], P('dp', None, 'seq'), may hold values from -6 to 6
- slot_owner: int32 [8, 64], P('dp'), may hold values from 0 to 7, as said below
- clip_pieces: int32 [8, 4, 16], P('dp'), may hold values from 0 to 63, as said below
- clip_length: int32 [8, 4], P('dp'), may hold values from 64 to 256, as said below
- modulation: bfloat16 [8, 4, 3, 1152], P('dp'), may hold values from -4 to 4
- qkv_weight: bfloat16 [1152, 3, 1152], P(None, None, 'seq'), may hold values from -0.1875 to 0.1875
- qk_gain: float32 [2, 72], replicated, may hold values from 0.1 to 1.9
- proj_weight: bfloat16 [1152, 1152], P('seq'), may hold values from -0.1875 to 0.1875
Outputs:
- block_output: bfloat16 [8, 64, 16, 1152], P('dp', None, 'seq')
Inputs may be any that keep to these rules, and one draw needn't show every extreme that they name: `slot_owner`: each row names every owner exactly 8 times. `clip_pieces`: each owner's table holds every arrival index 0 to 63 exactly once. `clip_length`: every owner has one clip of 256 tokens.
All inputs are finite; a program needn't handle non-finite values.
Results may differ from a plain program's by a relative error of at most 0.0045.
Values may be sent and summed in bfloat16 or wider, within the bound.
No kernel may reach another device: no remote copies, remote signals or barrier semaphores. Data moves between devices by JAX's collectives and lax.ppermute only.
A program may use at most 64 MiB of HBM per device.

v0:
```python
import functools
import math

import jax
import jax.numpy as jnp
from jax import lax
from jax.experimental import pallas as pl
from jax.experimental.pallas import tpu as pltpu
from jax.sharding import PartitionSpec as P

HEADS = 16
EPSILON = 1e-06
BF16 = jnp.bfloat16
F32 = jnp.float32


def send(array, axis, mask):
    if mask == 0:
        return array
    count = lax.axis_size(axis)
    return lax.ppermute(array, axis, [(i, i ^ mask) for i in range(count)])


def route_kernel(per_peer, piece_rows, place_ref, owner_hbm, token_hbm, *refs):
    slot_ref, own_ref, other_ref, filled_ref, owner_ref, token_ref, sems = refs
    peers = filled_ref.shape[0]
    owner_copy = pltpu.make_async_copy(owner_hbm, owner_ref, sems.at[0])
    token_copy = pltpu.make_async_copy(token_hbm, token_ref, sems.at[1])
    owner_copy.start()
    token_copy.start()
    for peer in range(peers):
        filled_ref[peer] = peer * per_peer
    owner_copy.wait()

    @pl.loop(0, peers * per_peer, unroll=8)
    def _(slot):
        peer = jnp.bitwise_xor(owner_ref[0, slot], place_ref[0])
        at = filled_ref[peer]
        filled_ref[peer] = at + 1
        slot_ref[at] = slot

    token_copy.wait()
    for peer in range(peers):
        ref = own_ref if peer % 2 == 0 else other_ref
        for m in range(per_peer):
            at = (peer // 2 * per_peer + m) * piece_rows
            ref[at : at + piece_rows, :] = token_ref[0, slot_ref[peer * per_peer + m]]


def merge_kernel(rows, own_hbm, other_ref, *refs):
    refs, own_ref, sem = refs[:-2], refs[-2], refs[-1]
    copy = pltpu.make_async_copy(own_hbm, own_ref, sem)
    copy.start()
    for index, ref in enumerate(refs):
        ref[rows:] = other_ref[index * rows : (index + 1) * rows]
    copy.wait()
    for index, ref in enumerate(refs):
        ref[:rows] = own_ref[index * rows : (index + 1) * rows]


def sides_kernel(*refs):
    count = len(refs) // 2
    for index in range(count):
        rows = refs[count + index].shape[0]
        start = 0 if index < count // 2 else rows
        refs[count + index][...] = refs[index][start : start + rows]


def half_kernel(core_ref, weight_hbm, out_ref, sem):
    rows = out_ref.shape[0]
    start = pl.multiple_of(core_ref[0] * rows, 16)
    copy = pltpu.make_async_copy(weight_hbm.at[pl.ds(start, rows), :], out_ref, sem)
    copy.start()
    copy.wait()


def place_kernel(per_peer, piece_rows, places, slot_ref, *refs):
    block_refs, out_ref = refs[:-1], refs[-1]
    for peer, (block, first) in enumerate(places):
        for m in range(per_peer):
            slot = slot_ref[peer * per_peer + m]
            start = first + m * piece_rows
            out_ref[0, slot] = block_refs[block][start : start + piece_rows, :]


def stack_kernel(*refs):
    start = 0
    for ref in refs[:-1]:
        refs[-1][start : start + ref.shape[0]] = ref[...]
        start += ref.shape[0]


def crossing_kernel(rows, own_ref, *refs):
    refs[-1][:rows] = own_ref[...]
    for index, ref in enumerate(refs[:-1]):
        refs[-1][(index + 1) * rows : (index + 2) * rows] = ref[rows:]


def arrival_of(piece, per_peer, owner_place):
    source = jnp.bitwise_xor(lax.div(piece, per_peer), owner_place)
    return source * per_peer + lax.rem(piece, per_peer)


def row_codes(rows, first_piece, per_peer, piece_rows, token_rows, owner_place, place, table):
    row = lax.broadcasted_iota(jnp.int32, (rows, 1), 0)
    arrival = arrival_of(first_piece + lax.div(row, piece_rows), per_peer, owner_place)
    lane = lax.broadcasted_iota(jnp.int32, (1, table.shape[1]), 1)
    found = jnp.zeros((rows, 1), jnp.int32)
    for clip in range(table.shape[0]):
        number = jnp.where(
            arrival == table[clip : clip + 1], lane + clip * table.shape[1], 0
        )
        found += jnp.sum(number, axis=1, keepdims=True)
    return found * token_rows + place * piece_rows + lax.rem(row, piece_rows)


def pick(clip, table):
    rows = jnp.broadcast_to(table[0:1], (clip.shape[0], table.shape[1]))
    for index in range(1, table.shape[0]):
        rows = jnp.where(clip == index, table[index : index + 1], rows)
    return rows


def norm_kernel(
    clip_tokens, codes_of, owner_ref, place_ref, table_ref, modulation_ref, *refs
):
    block_refs, out_ref = refs[:-1], refs[-1]
    code = codes_of(out_ref.shape[0], owner_ref[0], place_ref[0], table_ref[0])
    clip = lax.div(code, clip_tokens)
    rows = jnp.concatenate([ref[...].astype(F32) for ref in block_refs], axis=0)
    average = jnp.mean(rows, axis=-1, keepdims=True)
    centered = rows - average
    variance = jnp.mean(centered * centered, axis=-1, keepdims=True)
    normed = centered * lax.rsqrt(variance + EPSILON)
    shift = pick(clip, modulation_ref[0].astype(F32))
    scale = pick(clip, modulation_ref[1].astype(F32))
    out_ref[...] = (normed * (1.0 + scale) + shift).astype(BF16)


def project_kernel(head_size, weight_ref, gain_ref, *refs):
    hidden_refs, out_ref = refs[:-1], refs[-1]
    hidden = jnp.concatenate([ref[...] for ref in hidden_refs], axis=0)
    projected = lax.dot_general(
        weight_ref[...], hidden, (((1,), (1,)), ((), ())), preferred_element_type=F32
    )
    width = weight_ref.shape[0] // 3
    shape = (head_size, head_size)
    diagonal = lax.broadcasted_iota(jnp.int32, shape, 0) == lax.broadcasted_iota(
        jnp.int32, shape, 1
    )
    found = []
    for part in range(2):
        gain = jnp.sum(
            jnp.where(diagonal, gain_ref[part : part + 1, :], 0.0), axis=1, keepdims=True
        )
        for start in range(part * width, (part + 1) * width, head_size):
            value = projected[start : start + head_size]
            square = jnp.sum(value * value, axis=0, keepdims=True) * (1.0 / head_size)
            found.append(value * lax.rsqrt(square + EPSILON) * gain)
    found.append(projected[2 * width :])
    out_ref[...] = jnp.concatenate(found, axis=0).astype(BF16)


def token_codes(tokens, group_rows, per_peer, piece_rows, owner_ref, place_ref, table_ref):
    clips, per_clip = table_ref.shape[1:]
    seq_count = tokens // 2 // group_rows
    token = lax.broadcasted_iota(jnp.int32, (1, tokens), 1)
    row = lax.rem(token, group_rows)
    block = lax.div(token, group_rows)
    piece = lax.div(block, seq_count) * (group_rows // piece_rows) + lax.div(row, piece_rows)
    arrival = arrival_of(piece, per_peer, owner_ref[0])
    found = jnp.zeros_like(token)
    for clip in range(clips):
        for p in range(per_clip):
            found = jnp.where(arrival == table_ref[0, clip, p], clip * per_clip + p, found)
    source = jnp.bitwise_xor(lax.rem(block, seq_count), place_ref[0])
    return found * (piece_rows * seq_count) + source * piece_rows + lax.rem(row, piece_rows)


def gather_kernel(
    first, group_rows, per_peer, piece_rows, owner_ref, place_ref, table_ref, stacked_ref, *refs
):
    out_ref = refs[-1]
    clips, _, clip_tokens = out_ref.shape
    code = token_codes(
        clips * clip_tokens, group_rows, per_peer, piece_rows, owner_ref, place_ref, table_ref
    )[:, first : first + stacked_ref.shape[1]]
    position = lax.broadcasted_iota(jnp.int32, (clip_tokens, 1), 0)
    for clip in range(clips):
        chosen = jnp.where(code == position + clip * clip_tokens, 1.0, 0.0).astype(BF16)
        picked = lax.dot_general(
            stacked_ref[...], chosen, (((1,), (1,)), ((), ())), preferred_element_type=F32
        )
        if len(refs) > 1:
            picked += refs[0][clip].astype(F32)
        out_ref[clip] = picked.astype(BF16)


def attention_kernel(
    head_size, per_peer, piece_rows, length_ref, owner_ref, place_ref, table_ref, *refs
):
    early_ref, late_ref, out_refs, all_ref = refs[0], refs[1], refs[2:-1], refs[-1]
    clips, features, clip_tokens = early_ref.shape
    width, tokens = features // 3, clips * clip_tokens
    seq_count = len(out_refs)
    group_rows = tokens // 2 // seq_count
    code = token_codes(
        tokens, group_rows, per_peer, piece_rows, owner_ref, place_ref, table_ref
    )
    position = lax.broadcasted_iota(jnp.int32, (clip_tokens, 1), 0)
    key = lax.broadcasted_iota(jnp.int32, (8, clip_tokens), 1)
    heads = range(0, width, head_size)
    scale = math.log2(math.e) / math.sqrt(head_size)
    for clip in range(clips):
        chosen = jnp.where(code == position + clip * clip_tokens, 1.0, 0.0).astype(BF16)
        picked = early_ref[clip].astype(F32) + lax.dot_general(
            late_ref[...],
            chosen[:, tokens - late_ref.shape[1] :],
            (((1,), (1,)), ((), ())),
            preferred_element_type=F32,
        )
        in_clip = jnp.where(key < length_ref[0, clip], 1.0, 0.0)
        scores = [
            jnp.dot(
                jnp.transpose(picked[width + head : width + head + head_size]).astype(BF16),
                picked[head : head + head_size].astype(BF16),
                preferred_element_type=F32,
            )
            for head in heads
        ]
        unscaled = [jnp.exp2(score * scale).astype(BF16) for score in scores]
        outs = []
        for head, weights in zip(heads, unscaled):
            values = picked[2 * width + head : 2 * width + head + head_size] * in_clip[:1]
            values = jnp.concatenate([values, in_clip], axis=0).astype(BF16)
            summed = jnp.dot(values, weights, preferred_element_type=F32)
            outs.append(summed[:head_size] * (1.0 / summed[head_size : head_size + 1]))
        attended = jnp.concatenate(outs, axis=0).astype(BF16)
        back = jnp.dot(attended, chosen, preferred_element_type=F32)
        if clip == 0:
            all_ref[...] = back
        else:
            all_ref[...] += back
    for index, ref in enumerate(out_refs):
        for group in range(2):
            start = (group * seq_count + index) * group_rows
            ref[:, group * group_rows : (group + 1) * group_rows] = all_ref[
                :, start : start + group_rows
            ].astype(BF16)


def projected_rows(masks, halves, core_ref, head_refs, weight_refs):
    branch = None
    for mask, head_ref in zip(masks, head_refs):
        parts = [weight_refs[0][...]]
        if mask > 0:
            parts = [ref[...] for ref in weight_refs[:halves]]
            weight_refs = weight_refs[halves:]
            if halves == 2:
                first = core_ref[0] == 0
                parts = [
                    jnp.where(first, parts[0], parts[1]),
                    jnp.where(first, parts[1], parts[0]),
                ]
        else:
            weight_refs = weight_refs[1:]
        term = lax.dot_general(
            head_ref[...],
            jnp.concatenate(parts, axis=0),
            (((0,), (0,)), ((), ())),
            preferred_element_type=F32,
        )
        branch = term if branch is None else branch + term
    return branch


def sides_output_kernel(masks, halves, core_ref, *refs):
    refs[-1][...] = projected_rows(
        masks, halves, core_ref, refs[: len(masks)], refs[len(masks) : -1]
    )


def output_kernel(
    masks,
    halves,
    clip_tokens,
    codes_of,
    owner_masks,
    core_ref,
    length_ref,
    owner_ref,
    place_ref,
    table_ref,
    modulation_ref,
    partial_ref,
    *refs,
):
    head_refs, refs = refs[: len(masks)], refs[len(masks) :]
    weight_refs, refs = refs[: len(masks) * halves], refs[len(masks) * halves :]
    count = len(owner_masks) // 2
    block_refs, out_refs = refs[:count], refs[count:]
    rows = block_refs[0].shape[0] // 2
    branch = partial_ref[...] + projected_rows(masks, halves, core_ref, head_refs, weight_refs)
    code = codes_of(branch.shape[0], owner_ref[0], place_ref[0], table_ref[0])
    clip = lax.div(code, clip_tokens)
    limit = jnp.zeros_like(code)
    for index in range(length_ref.shape[1]):
        limit = jnp.where(clip == index, length_ref[0, index], limit)
    kept = lax.rem(code, clip_tokens) < limit
    branch = pick(clip, modulation_ref[2].astype(F32)) * branch
    for index, (out, first) in enumerate(owner_masks):
        at = slice(index * rows, (index + 1) * rows)
        side = slice(index % 2 * rows, (index % 2 + 1) * rows)
        result = block_refs[index // 2][side].astype(F32) + branch[at]
        out_refs[out][first : first + rows] = jnp.where(kept[at], result, 0.0).astype(BF16)


def body(
    tokens, slot_owner, clip_pieces, clip_length, modulation, qkv_weight, qk_gain, proj_weight
):
    dp_count = lax.axis_size("dp")
    seq_count = lax.axis_size("seq")
    pieces_here = tokens.shape[1]
    piece_rows = tokens.shape[2]
    model_width = tokens.shape[3]
    per_peer = pieces_here // dp_count
    head_size = qk_gain.shape[1]
    heads = HEADS // seq_count
    head_width = heads * head_size
    clips_here, per_clip = clip_pieces.shape[1:]
    clip_tokens = per_clip * piece_rows * seq_count
    block_rows = per_peer * piece_rows
    rows_here = pieces_here * piece_rows
    group_rows = rows_here // 2
    chips = dp_count // 2
    owner_place = lax.axis_index("dp").astype(jnp.int32)
    place = lax.axis_index("seq").astype(jnp.int32).reshape(1)
    core = lax.rem(owner_place, 2).reshape(1)
    owner_place = owner_place.reshape(1)
    halves = 2 if heads % 2 == 0 else 1

    smem = pl.BlockSpec(memory_space=pltpu.SMEM)
    vmem = pl.BlockSpec(memory_space=pltpu.VMEM)

    def call(
        kernel, scalars, inputs, outputs, scratch=(), out_scalars=0, limit=16, flops=10**9, where=vmem
    ):
        return pl.pallas_call(
            kernel,
            in_specs=[smem] * len(scalars)
            + (where if isinstance(where, list) else [where] * len(inputs)),
            out_specs=[smem] * out_scalars + [vmem] * (len(outputs) - out_scalars),
            out_shape=[jax.ShapeDtypeStruct(shape, dtype) for shape, dtype in outputs],
            scratch_shapes=list(scratch),
            compiler_params=pltpu.CompilerParams(vmem_limit_bytes=int(limit * 2**20)),
            cost_estimate=pl.CostEstimate(
                flops=flops, bytes_accessed=2**20, transcendentals=0
            ),
        )(*scalars, *inputs)

    x_count = math.isqrt(seq_count)
    anywhere = pl.BlockSpec(memory_space=pltpu.HBM)
    along_x = list(range(1, x_count))
    along_y = list(range(x_count, seq_count, x_count))

    proj_own = proj_weight
    if halves == 2:
        (proj_own,) = call(
            half_kernel,
            [core],
            [proj_weight],
            [((head_width // 2, model_width), BF16)],
            scratch=[pltpu.SemaphoreType.DMA],
            where=anywhere,
        )
    proj_parts = {mask: send(proj_own, "seq", mask) for mask in along_y + along_x}

    slots, own, other = call(
        functools.partial(route_kernel, per_peer, piece_rows),
        [owner_place],
        [slot_owner, tokens],
        [((pieces_here,), jnp.int32)] + [((chips * block_rows, model_width), BF16)] * 2,
        scratch=[
            pltpu.SMEM((dp_count,), jnp.int32),
            pltpu.SMEM(slot_owner.shape, jnp.int32),
            pltpu.VMEM(tokens.shape, BF16),
            pltpu.SemaphoreType.DMA((2,)),
        ],
        out_scalars=1,
        limit=59,
        flops=3 * 10**10,
        where=anywhere,
    )
    payloads = call(
        functools.partial(merge_kernel, block_rows),
        [],
        [own, send(other, "dp", 1)],
        [((2 * block_rows, model_width), BF16)] * chips,
        scratch=[pltpu.VMEM(own.shape, BF16), pltpu.SemaphoreType.DMA],
        where=[anywhere, vmem],
    )
    arrived = [send(payload, "dp", 2 * mask) for mask, payload in enumerate(payloads)]

    def codes_of(group):
        return lambda rows, *places: row_codes(
            rows,
            group * (pieces_here // 2),
            per_peer,
            piece_rows,
            piece_rows * seq_count,
            *places,
        )

    weight = jnp.transpose(qkv_weight, (1, 2, 0)).reshape(3 * head_width, model_width)
    factors = jnp.transpose(modulation[0], (1, 0, 2))
    def project(blocks, flops=3 * 10**9):
        (projected,) = call(
            functools.partial(project_kernel, head_size),
            [],
            [weight, qk_gain] + blocks,
            [((3 * head_width, sum(block.shape[0] for block in blocks)), BF16)],
            flops=flops,
        )
        return projected

    near, far = [
        call(
            functools.partial(norm_kernel, clip_tokens, codes_of(group)),
            [owner_place, place],
            [clip_pieces, factors] + arrived[group * chips // 2 : (group + 1) * chips // 2],
            [((group_rows, model_width), BF16)],
            flops=(1 + 9 * group) * 10**9,
        )[0]
        for group in range(2)
    ]
    near, proj_parts = lax.optimization_barrier((near, proj_parts))
    near, proj_parts = lax.optimization_barrier((near, proj_parts))
    sides = {mask: send(near, "seq", mask) for mask in along_y + along_x}
    far, sides = lax.optimization_barrier((far, sides))
    far_blocks = [send(far, "seq", mask) for mask in range(seq_count)]
    halved = call(
        sides_kernel,
        [],
        [sides[mask] for mask in along_y + along_x],
        [((group_rows // 2, model_width), BF16)] * len(sides),
    )
    halved = dict(zip(along_y + along_x, halved))
    near_blocks = []
    for mask in range(seq_count):
        mx = mask % x_count
        my = mask - mx
        if mx > 0 and my > 0:
            near_blocks += [send(halved[my], "seq", mx), send(halved[mx], "seq", my)]
        else:
            near_blocks.append(sides[mask] if mask > 0 else near)
    stacked_near = project(near_blocks)
    def gather(first, *arrays):
        (gathered,) = call(
            functools.partial(gather_kernel, first, group_rows, per_peer, piece_rows),
            [owner_place, place, clip_pieces],
            list(arrays),
            [((clips_here, 3 * head_width, clip_tokens), BF16)],
            limit=16 if clip_tokens <= 256 else 48,
            flops=3 * 10**9,
        )
        return gathered

    gathered = gather(0, stacked_near)
    gathered, proj_parts = lax.optimization_barrier((gathered, proj_parts))
    early_blocks, late_blocks = far_blocks[: seq_count // 2], far_blocks[seq_count // 2 :]
    early_blocks, gathered = lax.optimization_barrier((early_blocks, gathered))
    gathered = gather(seq_count * group_rows, project(early_blocks), gathered)
    swapped = {mask: send(proj_parts[mask], "dp", 1) for mask in proj_parts} if halves == 2 else {}
    gathered, proj_parts = lax.optimization_barrier((gathered, proj_parts))
    for my in along_y:
        for mx in along_x:
            proj_parts[my + mx] = send(proj_parts[my], "seq", mx)
    late_blocks, gathered = lax.optimization_barrier((late_blocks, gathered))
    stacked_late, swapped = lax.optimization_barrier((project(late_blocks, 10**8), swapped))

    attended = call(
        functools.partial(attention_kernel, head_size, per_peer, piece_rows),
        [clip_length, owner_place, place, clip_pieces],
        [gathered, stacked_late],
        [((head_width, rows_here), BF16)] * seq_count,
        scratch=[pltpu.VMEM((head_width, seq_count * rows_here), F32)],
        limit=16 if clip_tokens <= 256 else 48,
        flops=10**8,
    )
    returned = [send(array, "seq", mask) for mask, array in enumerate(attended)]
    if halves == 2:
        _, late = lax.optimization_barrier((attended[0], proj_parts))
        swapped |= {mask: send(late[mask], "dp", 1) for mask in late if mask not in swapped}
    proj_parts = proj_parts | {seq_count + mask: swapped[mask] for mask in swapped}

    half_count = dp_count // 2
    far_masks = list(range(half_count, dp_count))
    outs = {mask: (index, 0) for index, mask in enumerate(far_masks)}
    for mask in range(2, half_count):
        outs[mask] = (half_count + mask // 2 - 1, mask % 2 * block_rows)
    outs[0], outs[1] = [(half_count + half_count // 2 - 1 + core_of, 0) for core_of in range(2)]

    def weights_of(masks):
        return [
            part
            for mask in masks
            for part in (
                [proj_weight]
                if mask == 0
                else [proj_parts[mask + half * seq_count] for half in range(halves)]
            )
        ]

    beside = [0] + along_x + along_y
    across = [mask for mask in range(seq_count) if mask not in beside]
    (partial,) = call(
        functools.partial(sides_output_kernel, beside, halves),
        [core],
        [returned[mask] for mask in beside] + weights_of(beside),
        [((rows_here, model_width), F32)],
        flops=10**10,
    )
    results = call(
        functools.partial(
            output_kernel,
            across,
            halves,
            clip_tokens,
            codes_of(0),
            [outs[mask] for mask in range(dp_count)],
        ),
        [core, clip_length, owner_place, place],
        [clip_pieces, factors, partial]
        + [returned[mask] for mask in across]
        + weights_of(across)
        + arrived,
        [((block_rows, model_width), BF16)] * half_count
        + [((2 * block_rows, model_width), BF16)] * (half_count // 2 - 1)
        + [((block_rows, model_width), BF16)] * 2,
        flops=3 * 10**9,
    )
    near_back = [
        send(block, "dp", 2 * (index + 1)) for index, block in enumerate(results[half_count:-2])
    ]
    far_back = [send(block, "dp", mask) for block, mask in zip(results, far_masks)]
    (crossing,) = call(
        functools.partial(crossing_kernel, block_rows),
        [],
        [results[-1]] + near_back,
        [((half_count // 2 * block_rows, model_width), BF16)],
    )
    crossed = send(crossing, "dp", 1)
    (far_back,) = call(
        stack_kernel,
        [],
        far_back,
        [((half_count * block_rows, model_width), BF16)],
        flops=10**10,
    )
    came_back = [far_back, crossed, results[-2]] + near_back
    places = {mask: (0, index * block_rows) for index, mask in enumerate(far_masks)}
    places[0] = (2, 0)
    for index in range(half_count // 2):
        places[2 * index + 1] = (1, index * block_rows)
        if index > 0:
            places[2 * index] = (2 + index, 0)
    (out,) = call(
        functools.partial(
            place_kernel, per_peer, piece_rows, [places[mask] for mask in range(dp_count)]
        ),
        [slots],
        came_back,
        [(tokens.shape, BF16)],
    )
    return out


def solution(mesh):
    return jax.shard_map(
        body,
        mesh=mesh,
        in_specs=(
            P("dp", None, "seq", None),
            P("dp", None),
            P("dp", None, None),
            P("dp", None),
            P("dp", None, None, None),
            P(None, None, "seq"),
            P(),
            P("seq", None),
        ),
        out_specs=P("dp", None, "seq", None),
        check_vma=False,
    )
```

profile of v0, /device:TPU:0, one launch (start us, length us, event | category | flops | bytes accessed | tf_op | source)
XLA Modules:
  0.0 74.0 jit_solution(11387885250038537458)
XLA Ops:
  0.0 2.1 %shard_map.82 = (s32[64]{0:T(128)}, bf16[128,1152]{1,0:T(8,128)(2,1)}, bf16[128,1152]{1,0:T(8,128)(2,1)}) custom-call(s32[1]{0:T(128)} %bitcast.place_ref.owner_ref, s32[1,64]{1,0:T(1,128)} %owner_hbm.1, bf16[1,64,4,1152]{3,2,1,0:T(4,128)(2,1)} %token_hbm.1), custom_call_target="tpu_custom_call" | custom-call | flops 30000001024 | bytes 1048576 | tf_op jit(solution)/shard_map/pallas_call | solution.py:348
  2.2 0.5 collective-permute-start
  2.7 0.1 shard_map.86
  2.8 2.6 %collective-permute-start.4 = (bf16[144,1152]{1,0:T(8,128)(2,1)S(1)}, bf16[144,1152]{1,0:T(8,128)(2,1)S(1)}, u32[]{:S(2)}, u32[]{:S(2)}) collective-permute-start(bf16[144,1152]{1,0:T(8,128)(2,1)S(1)} %shard_map.86), channel_id=1, source_target_pairs={{0,1},{1,0},{2,3},{3,2},{4,5},{5,4},{6,7},{7,6},{8,9},{9,8},{10,11... | collective-permute-start | bytes 995336 | tf_op jit(solution)/shard_map/ppermute | solution.py:21
  5.4 1.5 %collective-permute-start.5 = (bf16[144,1152]{1,0:T(8,128)(2,1)S(1)}, bf16[144,1152]{1,0:T(8,128)(2,1)S(1)}, u32[]{:S(2)}, u32[]{:S(2)}) collective-permute-start(bf16[144,1152]{1,0:T(8,128)(2,1)S(1)} %shard_map.86), channel_id=1, source_target_pairs={{0,2},{1,3},{2,0},{3,1},{4,6},{5,7},{6,4},{7,5},{8,10},{9,11},{10,... | collective-permute-start | bytes 995336 | tf_op jit(solution)/shard_map/ppermute | solution.py:21
  6.9 0.0 collective-permute-done.other_ref
  6.9 0.1 shard_map.83
  7.0 1.6 %collective-permute-start.3 = (bf16[64,1152]{1,0:T(8,128)(2,1)S(1)}, bf16[64,1152]{1,0:T(8,128)(2,1)S(1)}, u32[]{:S(2)}, u32[]{:S(2)}) collective-permute-start(bf16[64,1152]{1,0:T(8,128)(2,1)S(1)} %get-tuple-element.53), channel_id=1, source_target_pairs={{0,8},{4,12},{8,0},{12,4},{16,24},{20,28},{24,16},{28,20},{1,9},{5... | collective-permute-start | bytes 442376 | tf_op jit(solution)/shard_map/ppermute | solution.py:21
  8.7 2.6 %collective-permute-start.1 = (bf16[64,1152]{1,0:T(8,128)(2,1)S(1)}, bf16[64,1152]{1,0:T(8,128)(2,1)S(1)}, u32[]{:S(2)}, u32[]{:S(2)}) collective-permute-start(bf16[64,1152]{1,0:T(8,128)(2,1)S(1)} %get-tuple-element.50), channel_id=1, source_target_pairs={{0,16},{4,20},{8,24},{12,28},{16,0},{20,4},{24,8},{28,12},{1,17},{... | collective-permute-start | bytes 442376 | tf_op jit(solution)/shard_map/ppermute | solution.py:21
  11.3 0.2 collective-permute-start.2
  11.5 3.4 %collective-permute-done.3.refs_1_.refs_4_ = bf16[64,1152]{1,0:T(8,128)(2,1)S(1)} collective-permute-done((bf16[64,1152]{1,0:T(8,128)(2,1)S(1)}, bf16[64,1152]{1,0:T(8,128)(2,1)S(1)}, u32[]{:S(2)}, u32[]{:S(2)}) %collective-permute-start.3) | collective-permute-done | bytes 147488 | tf_op jit(solution)/shard_map/ppermute | solution.py:21
  14.9 0.6 shard_map.85.refs_0_
  15.5 0.0 collective-permute-done.4.refs_4_
  15.5 0.0 collective-permute-done.5.refs_6_
  15.5 0.6 collective-permute-start.6
  16.1 1.5 %collective-permute-start.7 = (bf16[128,1152]{1,0:T(8,128)(2,1)S(1)}, bf16[128,1152]{1,0:T(8,128)(2,1)S(1)}, u32[]{:S(2)}, u32[]{:S(2)}) collective-permute-start(bf16[128,1152]{1,0:T(8,128)(2,1)S(1)} %shard_map.85.refs_0_), channel_id=1, source_target_pairs={{0,2},{1,3},{2,0},{3,1},{4,6},{5,7},{6,4},{7,5},{8,10},{9,11},{10,... | collective-permute-start | bytes 884744 | tf_op jit(solution)/shard_map/ppermute | solution.py:21
  17.6 5.1 %collective-permute-done.1.refs_0_.refs_5_ = bf16[64,1152]{1,0:T(8,128)(2,1)S(1)} collective-permute-done((bf16[64,1152]{1,0:T(8,128)(2,1)S(1)}, bf16[64,1152]{1,0:T(8,128)(2,1)S(1)}, u32[]{:S(2)}, u32[]{:S(2)}) %collective-permute-start.1) | collective-permute-done | bytes 147488 | tf_op jit(solution)/shard_map/ppermute | solution.py:21
  22.7 0.6 shard_map.84.refs_0_
  23.2 0.0 copy-start
  23.3 0.0 copy-start.2
  23.3 0.3 collective-permute-done.6.refs_1_
  23.6 0.4 collective-permute-done.7.refs_0_.refs_2_
  24.0 1.4 %collective-permute-start.11 = (bf16[64,1152]{1,0:T(8,128)(2,1)S(1)}, bf16[64,1152]{1,0:T(8,128)(2,1)S(1)}, u32[]{:S(2)}, u32[]{:S(2)}) collective-permute-start(bf16[64,1152]{1,0:T(8,128)(2,1)S(1)} %get-tuple-element.58), channel_id=1, source_target_pairs={{0,1},{1,0},{2,3},{3,2},{4,5},{5,4},{6,7},{7,6},{8,9},{9,8},{10,11... | collective-permute-start | bytes 442376 | tf_op jit(solution)/shard_map/ppermute | solution.py:21
  25.4 1.5 %collective-permute-start.12 = (bf16[64,1152]{1,0:T(8,128)(2,1)S(1)}, bf16[64,1152]{1,0:T(8,128)(2,1)S(1)}, u32[]{:S(2)}, u32[]{:S(2)}) collective-permute-start(bf16[64,1152]{1,0:T(8,128)(2,1)S(1)} %get-tuple-element.59), channel_id=1, source_target_pairs={{0,2},{1,3},{2,0},{3,1},{4,6},{5,7},{6,4},{7,5},{8,10},{9,11},{10,... | collective-permute-start | bytes 442376 | tf_op jit(solution)/shard_map/ppermute | solution.py:21
  26.9 0.6 collective-permute-start.10
  27.5 0.6 collective-permute-start.8
  28.1 2.3 %collective-permute-start.9 = (bf16[128,1152]{1,0:T(8,128)(2,1)S(1)}, bf16[128,1152]{1,0:T(8,128)(2,1)S(1)}, u32[]{:S(2)}, u32[]{:S(2)}) collective-permute-start(bf16[128,1152]{1,0:T(8,128)(2,1)S(1)} %shard_map.84.refs_0_), channel_id=1, source_target_pairs={{0,3},{1,2},{2,1},{3,0},{4,7},{5,6},{6,5},{7,4},{8,11},{9,10},{10,... | collective-permute-start | bytes 884744 | tf_op jit(solution)/shard_map/ppermute | solution.py:21
  30.4 0.3 collective-permute-done.11.refs_3_
  30.7 1.4 %collective-permute-done.12.refs_4_ = bf16[64,1152]{1,0:T(8,128)(2,1)S(1)} collective-permute-done((bf16[64,1152]{1,0:T(8,128)(2,1)S(1)}, bf16[64,1152]{1,0:T(8,128)(2,1)S(1)}, u32[]{:S(2)}, u32[]{:S(2)}) %collective-permute-start.12) | collective-permute-done | bytes 147488 | tf_op jit(solution)/shard_map/ppermute | solution.py:21
  32.1 1.4 %shard_map.88.stacked_ref = bf16[864,512]{1,0:T(8,128)(2,1)S(1)} custom-call(bf16[864,1152]{1,0:T(8,128)(2,1)S(1)} %bitcast.9, f32[2,72]{1,0:T(2,128)S(1)} %copy-done.2, bf16[128,1152]{1,0:T(8,128)(2,1)S(1)} %shard_map.85.refs_0_, bf16[128,1152]{1,0:T(8,128)(2,1)S(1)} %collective-permute-done.6.refs_1_, ...), custom_call_target="tpu_custom_call" | custom-call | flops 3000000000 | bytes 1048576 | tf_op jit(solution)/shard_map/pallas_call | solution.py:348
  33.5 1.8 %shard_map.89.refs_0_ = bf16[4,864,256]{2,1,0:T(8,128)(2,1)S(1)} custom-call(s32[1]{0:T(128)} %bitcast.place_ref.owner_ref, s32[1]{0:T(128)} %bitcast.2.place_ref, s32[1,4,16]{2,1,0:T(4,128)S(1)} %copy-done.1, bf16[864,512]{1,0:T(8,128)(2,1)S(1)} %shard_map.88.stacked_ref), custom_call_target="tpu_custom_call" | custom-call | flops 3000000000 | bytes 1048576 | tf_op jit(solution)/shard_map/pallas_call | solution.py:348
  35.3 0.1 collective-permute-start.13
  35.4 0.5 collective-permute-start.14
  35.9 1.1 %collective-permute-done.10.refs_1_ = bf16[128,1152]{1,0:T(8,128)(2,1)S(1)} collective-permute-done((bf16[128,1152]{1,0:T(8,128)(2,1)S(1)}, bf16[128,1152]{1,0:T(8,128)(2,1)S(1)}, u32[]{:S(2)}, u32[]{:S(2)}) %collective-permute-start.10) | collective-permute-done | bytes 294944 | tf_op jit(solution)/shard_map/ppermute | solution.py:21
  37.0 0.8 %shard_map.90.stacked_ref = bf16[864,256]{1,0:T(8,128)(2,1)S(1)} custom-call(bf16[864,1152]{1,0:T(8,128)(2,1)S(1)} %bitcast.10, f32[2,72]{1,0:T(2,128)S(1)} %copy-done.2, bf16[128,1152]{1,0:T(8,128)(2,1)S(1)} %shard_map.84.refs_0_, bf16[128,1152]{1,0:T(8,128)(2,1)S(1)} %collective-permute-done.10.refs_1_), custom_call_target="tpu_custom_call" | custom-call | flops 3000000000 | bytes 1048576 | tf_op jit(solution)/shard_map/pallas_call | solution.py:348
  37.8 1.3 %shard_map.91.refs_0_ = bf16[4,864,256]{2,1,0:T(8,128)(2,1)S(1)} custom-call(s32[1]{0:T(128)} %bitcast.place_ref.owner_ref, s32[1]{0:T(128)} %bitcast.2.place_ref, s32[1,4,16]{2,1,0:T(4,128)S(1)} %copy-done.1, bf16[864,256]{1,0:T(8,128)(2,1)S(1)} %shard_map.90.stacked_ref, bf16[4,864,256]{2,1,0:T(8,128)(2,1)S(1)} %shard_map.89.refs_0_), custom_call_target="tpu_custom_call" | custom-call | flops 3000000000 | bytes 1048576 | tf_op jit(solution)/shard_map/pallas_call | solution.py:348
  39.1 0.0 copy-start.3
  39.1 1.5 %collective-permute-start.18 = (bf16[144,1152]{1,0:T(8,128)(2,1)S(1)}, bf16[144,1152]{1,0:T(8,128)(2,1)S(1)}, u32[]{:S(2)}, u32[]{:S(2)}) collective-permute-start(bf16[144,1152]{1,0:T(8,128)(2,1)S(1)} %collective-permute-done.5.refs_6_), channel_id=1, source_target_pairs={{0,1},{1,0},{2,3},{3,2},{4,5},{5,4},{6,7},{7,6},{8,9},{9,8},{10,11... | collective-permute-start | bytes 995336 | tf_op jit(solution)/shard_map/ppermute | solution.py:21
  40.7 1.0 %collective-permute-done.8.refs_0_ = bf16[128,1152]{1,0:T(8,128)(2,1)S(1)} collective-permute-done((bf16[128,1152]{1,0:T(8,128)(2,1)S(1)}, bf16[128,1152]{1,0:T(8,128)(2,1)S(1)}, u32[]{:S(2)}, u32[]{:S(2)}) %collective-permute-start.8) | collective-permute-done | bytes 294944 | tf_op jit(solution)/shard_map/ppermute | solution.py:21
  41.6 0.0 collective-permute-done.9.refs_1_
  41.6 0.8 %shard_map.92.refs_1_ = bf16[864,256]{1,0:T(8,128)(2,1)S(1)} custom-call(bf16[864,1152]{1,0:T(8,128)(2,1)S(1)} %bitcast.11, f32[2,72]{1,0:T(2,128)S(1)} %copy-done.2, bf16[128,1152]{1,0:T(8,128)(2,1)S(1)} %collective-permute-done.8.refs_0_, bf16[128,1152]{1,0:T(8,128)(2,1)S(1)} %collective-permute-done.9.refs_1_), custom_call_target="tpu_custom_call" | custom-call | flops 100000000 | bytes 1048576 | tf_op jit(solution)/shard_map/pallas_call | solution.py:348
  42.4 0.0 collective-permute-done.13.refs_5_
  42.4 0.0 collective-permute-done.14.refs_7_
  42.4 4.6 %shard_map.93 = (bf16[288,256]{1,0:T(8,128)(2,1)S(1)}, bf16[288,256]{1,0:T(8,128)(2,1)S(1)}, bf16[288,256]{1,0:T(8,128)(2,1)S(1)}, bf16[288,256]{1,0:T(8,128)(2,1)S(1)}) custom-call(s32[1,4]{1,0:T(1,128)S(1)} %copy-done.3, s32[1]{0:T(128)} %bitcast.place_ref.owner_ref, s32[1]{0:T(128)} %bitcast.2.place_ref, s32[1,4,16]{2,1,0:T(4,128)S(1)} %copy-done.1, ...), custom_call_target="tpu_custom_call" | custom-call | flops 100000000 | bytes 1048576 | tf_op jit(solution)/shard_map/pallas_call | solution.py:348
  47.0 1.8 %collective-permute-start.15 = (bf16[288,256]{1,0:T(8,128)(2,1)S(1)}, bf16[288,256]{1,0:T(8,128)(2,1)S(1)}, u32[]{:S(2)}, u32[]{:S(2)}) collective-permute-start(bf16[288,256]{1,0:T(8,128)(2,1)S(1)} %get-tuple-element.74), channel_id=1, source_target_pairs={{0,1},{1,0},{2,3},{3,2},{4,5},{5,4},{6,7},{7,6},{8,9},{9,8},{10,11... | collective-permute-start | bytes 442376 | tf_op jit(solution)/shard_map/ppermute | solution.py:21
  48.9 0.5 collective-permute-start.16
  49.4 1.2 %collective-permute-start.17 = (bf16[288,256]{1,0:T(8,128)(2,1)S(1)}, bf16[288,256]{1,0:T(8,128)(2,1)S(1)}, u32[]{:S(2)}, u32[]{:S(2)}) collective-permute-start(bf16[288,256]{1,0:T(8,128)(2,1)S(1)} %get-tuple-element.80), channel_id=1, source_target_pairs={{0,3},{1,2},{2,1},{3,0},{4,7},{5,6},{6,5},{7,4},{8,11},{9,10},{10,... | collective-permute-start | bytes 442376 | tf_op jit(solution)/shard_map/ppermute | solution.py:21
  50.6 0.0 collective-permute-done.18.refs_1_
  50.6 2.6 %collective-permute-done.15.refs_1_ = bf16[288,256]{1,0:T(8,128)(2,1)S(1)} collective-permute-done((bf16[288,256]{1,0:T(8,128)(2,1)S(1)}, bf16[288,256]{1,0:T(8,128)(2,1)S(1)}, u32[]{:S(2)}, u32[]{:S(2)}) %collective-permute-start.15) | collective-permute-done | bytes 147488 | tf_op jit(solution)/shard_map/ppermute | solution.py:21
  53.2 2.4 %collective-permute-done.16.refs_2_ = bf16[288,256]{1,0:T(8,128)(2,1)S(1)} collective-permute-done((bf16[288,256]{1,0:T(8,128)(2,1)S(1)}, bf16[288,256]{1,0:T(8,128)(2,1)S(1)}, u32[]{:S(2)}, u32[]{:S(2)}) %collective-permute-start.16) | collective-permute-done | bytes 147488 | tf_op jit(solution)/shard_map/ppermute | solution.py:21
  55.6 1.2 %shard_map.94.partial_ref = f32[256,1152]{1,0:T(8,128)S(1)} custom-call(s32[1]{0:T(128)} %bitcast.1.core_ref, bf16[288,256]{1,0:T(8,128)(2,1)S(1)} %get-tuple-element.73.refs_0_, bf16[288,256]{1,0:T(8,128)(2,1)S(1)} %collective-permute-done.15.refs_1_, bf16[288,256]{1,0:T(8,128)(2,1)S(1)} %collective-permute-done.16.refs_2_, ...), custom_call_target="tpu_custom_call" | custom-call | flops 10000000000 | bytes 1048576 | tf_op jit(solution)/shard_map/pallas_call | solution.py:348
  56.8 0.0 collective-permute-done.19.refs_2_
  56.8 1.5 %shard_map.95 = (bf16[32,1152]{1,0:T(8,128)(2,1)S(1)}, bf16[32,1152]{1,0:T(8,128)(2,1)S(1)}, bf16[32,1152]{1,0:T(8,128)(2,1)S(1)}, bf16[32,1152]{1,0:T(8,128)(2,...) custom-call(s32[1]{0:T(128)} %bitcast.1.core_ref, ...), custom_call_target="tpu_custom_call" | custom-call | flops 3000000000 | bytes 1048576 | tf_op jit(solution)/shard_map/pallas_call | solution.py:348
  58.3 1.7 %collective-permute-start.24 = (bf16[64,1152]{1,0:T(8,128)(2,1)S(1)}, bf16[64,1152]{1,0:T(8,128)(2,1)S(1)}, u32[]{:S(2)}, u32[]{:S(2)}) collective-permute-start(bf16[64,1152]{1,0:T(8,128)(2,1)S(1)} %get-tuple-element.87), channel_id=1, source_target_pairs={{0,8},{4,12},{8,0},{12,4},{16,24},{20,28},{24,16},{28,20},{1,9},{5... | collective-permute-start | bytes 442376 | tf_op jit(solution)/shard_map/ppermute | solution.py:21
  60.0 1.4 %collective-permute-start.20 = (bf16[32,1152]{1,0:T(8,128)(2,1)S(1)}, bf16[32,1152]{1,0:T(8,128)(2,1)S(1)}, u32[]{:S(2)}, u32[]{:S(2)}) collective-permute-start(bf16[32,1152]{1,0:T(8,128)(2,1)S(1)} %get-tuple-element.82), channel_id=1, source_target_pairs={{0,16},{4,20},{8,24},{12,28},{16,0},{20,4},{24,8},{28,12},{1,17},{... | collective-permute-start | bytes 221192 | tf_op jit(solution)/shard_map/ppermute | solution.py:21
  61.4 0.0 collective-permute-start.21
  61.4 1.3 %collective-permute-start.22 = (bf16[32,1152]{1,0:T(8,128)(2,1)S(1)}, bf16[32,1152]{1,0:T(8,128)(2,1)S(1)}, u32[]{:S(2)}, u32[]{:S(2)}) collective-permute-start(bf16[32,1152]{1,0:T(8,128)(2,1)S(1)} %get-tuple-element.84), channel_id=1, source_target_pairs={{0,24},{4,28},{8,16},{12,20},{16,8},{20,12},{24,0},{28,4},{1,25},{... | collective-permute-start | bytes 221192 | tf_op jit(solution)/shard_map/ppermute | solution.py:21
  62.7 3.5 %collective-permute-start.23 = (bf16[32,1152]{1,0:T(8,128)(2,1)S(1)}, bf16[32,1152]{1,0:T(8,128)(2,1)S(1)}, u32[]{:S(2)}, u32[]{:S(2)}) collective-permute-start(bf16[32,1152]{1,0:T(8,128)(2,1)S(1)} %get-tuple-element.85), channel_id=1, source_target_pairs={{0,28},{4,24},{8,20},{12,16},{16,12},{20,8},{24,4},{28,0},{1,29},{... | collective-permute-start | bytes 221192 | tf_op jit(solution)/shard_map/ppermute | solution.py:21
  66.2 0.0 collective-permute-done.24.refs_0_.refs_3_
  66.2 0.1 collective-permute-start.25
  66.3 0.0 collective-permute-done.20.refs_0_
  66.3 6.1 %collective-permute-done.21.refs_1_ = bf16[32,1152]{1,0:T(8,128)(2,1)S(1)} collective-permute-done((bf16[32,1152]{1,0:T(8,128)(2,1)S(1)}, bf16[32,1152]{1,0:T(8,128)(2,1)S(1)}, u32[]{:S(2)}, u32[]{:S(2)}) %collective-permute-start.21) | collective-permute-done | bytes 73760 | tf_op jit(solution)/shard_map/ppermute | solution.py:21
  72.4 0.0 collective-permute-done.25.refs_1_
  72.5 1.5 %shard_map.98 = bf16[1,64,4,1152]{3,2,1,0:T(4,128)(2,1)} custom-call(s32[64]{0:T(128)S(1)} %copy-done.7, bf16[128,1152]{1,0:T(8,128)(2,1)S(1)} %shard_map.96.refs_0_, bf16[64,1152]{1,0:T(8,128)(2,1)S(1)} %collective-permute-done.25.refs_1_, bf16[32,1152]{1,0:T(8,128)(2,1)S(1)} %get-tuple-element.88.refs_2_, ...), custom_call_target="tpu_custom_call" | custom-call | flops 1000000000 | bytes 1048576 | tf_op jit(solution)/shard_map/pallas_call | solution.py:348
  (21 shorter events, 0.1 us)
Async XLA Ops:
  0.0 2.7 %copy-start.4 = (bf16[288,1152]{1,0:T(8,128)(2,1)S(1)}, bf16[288,1152]{1,0:T(8,128)(2,1)}, u32[]{:S(2)}) copy-start(bf16[288,1152]{1,0:T(8,128)(2,1)} %refs_3_.1) | copy-start | bytes 1990660
  2.2 4.8 %collective-permute-start = (bf16[128,1152]{1,0:T(8,128)(2,1)}, bf16[128,1152]{1,0:T(8,128)(2,1)S(1)}, u32[]{:S(2)}, u32[]{:S(2)}) collective-permute-start(bf16[128,1152]{1,0:T(8,128)(2,1)} %get-tuple-element.49), channel_id=1, source_target_pairs={{0,4},{4,0},{8,12},{12,8},{16,20},{20,16},{24,28},{28,24},{1,5},{5... | collective-permute-start | bytes 884744 | tf_op jit(solution)/shard_map/ppermute | solution.py:21
  2.7 4.2 %copy-start.6 = (bf16[128,1152]{1,0:T(8,128)(2,1)S(1)}, bf16[128,1152]{1,0:T(8,128)(2,1)}, u32[]{:S(2)}) copy-start(bf16[128,1152]{1,0:T(8,128)(2,1)} %get-tuple-element.48.own_hbm) | copy-start | bytes 884740
  2.8 12.7 %collective-permute-start.4 = (bf16[144,1152]{1,0:T(8,128)(2,1)S(1)}, bf16[144,1152]{1,0:T(8,128)(2,1)S(1)}, u32[]{:S(2)}, u32[]{:S(2)}) collective-permute-start(bf16[144,1152]{1,0:T(8,128)(2,1)S(1)} %shard_map.86), channel_id=1, source_target_pairs={{0,1},{1,0},{2,3},{3,2},{4,5},{5,4},{6,7},{7,6},{8,9},{9,8},{10,11... | collective-permute-start | bytes 995336 | tf_op jit(solution)/shard_map/ppermute | solution.py:21
  5.4 10.1 %collective-permute-start.5 = (bf16[144,1152]{1,0:T(8,128)(2,1)S(1)}, bf16[144,1152]{1,0:T(8,128)(2,1)S(1)}, u32[]{:S(2)}, u32[]{:S(2)}) collective-permute-start(bf16[144,1152]{1,0:T(8,128)(2,1)S(1)} %shard_map.86), channel_id=1, source_target_pairs={{0,2},{1,3},{2,0},{3,1},{4,6},{5,7},{6,4},{7,5},{8,10},{9,11},{10,... | collective-permute-start | bytes 995336 | tf_op jit(solution)/shard_map/ppermute | solution.py:21
  6.9 8.0 %copy-start.1 = (s32[1,4,16]{2,1,0:T(4,128)S(1)}, s32[1,4,16]{2,1,0:T(4,128)}, u32[]{:S(2)}) copy-start(s32[1,4,16]{2,1,0:T(4,128)} %table_ref.11) | copy-start | bytes 772
  6.9 8.0 %copy-start.5 = (bf16[1,4,3,1152]{3,1,2,0:T(4,128)(2,1)S(1)}, bf16[1,4,3,1152]{3,1,2,0:T(4,128)(2,1)}, u32[]{:S(2)}) copy-start(bf16[1,4,3,1152]{3,1,2,0:T(4,128)(2,1)} %param.12) | copy-start | bytes 82948
  7.0 7.9 %collective-permute-start.3 = (bf16[64,1152]{1,0:T(8,128)(2,1)S(1)}, bf16[64,1152]{1,0:T(8,128)(2,1)S(1)}, u32[]{:S(2)}, u32[]{:S(2)}) collective-permute-start(bf16[64,1152]{1,0:T(8,128)(2,1)S(1)} %get-tuple-element.53), channel_id=1, source_target_pairs={{0,8},{4,12},{8,0},{12,4},{16,24},{20,28},{24,16},{28,20},{1,9},{5... | collective-permute-start | bytes 442376 | tf_op jit(solution)/shard_map/ppermute | solution.py:21
  8.7 14.0 %collective-permute-start.1 = (bf16[64,1152]{1,0:T(8,128)(2,1)S(1)}, bf16[64,1152]{1,0:T(8,128)(2,1)S(1)}, u32[]{:S(2)}, u32[]{:S(2)}) collective-permute-start(bf16[64,1152]{1,0:T(8,128)(2,1)S(1)} %get-tuple-element.50), channel_id=1, source_target_pairs={{0,16},{4,20},{8,24},{12,28},{16,0},{20,4},{24,8},{28,12},{1,17},{... | collective-permute-start | bytes 442376 | tf_op jit(solution)/shard_map/ppermute | solution.py:21
  11.3 11.4 %collective-permute-start.2 = (bf16[64,1152]{1,0:T(8,128)(2,1)S(1)}, bf16[64,1152]{1,0:T(8,128)(2,1)S(1)}, u32[]{:S(2)}, u32[]{:S(2)}) collective-permute-start(bf16[64,1152]{1,0:T(8,128)(2,1)S(1)} %get-tuple-element.51), channel_id=1, source_target_pairs={{0,24},{4,28},{8,16},{12,20},{16,8},{20,12},{24,0},{28,4},{1,25},{... | collective-permute-start | bytes 442376 | tf_op jit(solution)/shard_map/ppermute | solution.py:21
  15.5 8.1 %collective-permute-start.6 = (bf16[128,1152]{1,0:T(8,128)(2,1)S(1)}, bf16[128,1152]{1,0:T(8,128)(2,1)S(1)}, u32[]{:S(2)}, u32[]{:S(2)}) collective-permute-start(bf16[128,1152]{1,0:T(8,128)(2,1)S(1)} %shard_map.85.refs_0_), channel_id=1, source_target_pairs={{0,1},{1,0},{2,3},{3,2},{4,5},{5,4},{6,7},{7,6},{8,9},{9,8},{10,11... | collective-permute-start | bytes 884744 | tf_op jit(solution)/shard_map/ppermute | solution.py:21
  16.1 7.9 %collective-permute-start.7 = (bf16[128,1152]{1,0:T(8,128)(2,1)S(1)}, bf16[128,1152]{1,0:T(8,128)(2,1)S(1)}, u32[]{:S(2)}, u32[]{:S(2)}) collective-permute-start(bf16[128,1152]{1,0:T(8,128)(2,1)S(1)} %shard_map.85.refs_0_), channel_id=1, source_target_pairs={{0,2},{1,3},{2,0},{3,1},{4,6},{5,7},{6,4},{7,5},{8,10},{9,11},{10,... | collective-permute-start | bytes 884744 | tf_op jit(solution)/shard_map/ppermute | solution.py:21
  23.2 8.9 %copy-start = (bf16[1152,3,288]{0,2,1:T(8,128)(2,1)S(1)}, bf16[1152,3,288]{0,2,1:T(8,128)(2,1)}, u32[]{:S(2)}) copy-start(bf16[1152,3,288]{0,2,1:T(8,128)(2,1)} %param.13) | copy-start | bytes 5971972
  23.3 8.9 %copy-start.2 = (f32[2,72]{1,0:T(2,128)S(1)}, f32[2,72]{1,0:T(2,128)}, u32[]{:S(2)}) copy-start(f32[2,72]{1,0:T(2,128)} %gain_ref.5) | copy-start | bytes 1732
  24.0 6.7 %collective-permute-start.11 = (bf16[64,1152]{1,0:T(8,128)(2,1)S(1)}, bf16[64,1152]{1,0:T(8,128)(2,1)S(1)}, u32[]{:S(2)}, u32[]{:S(2)}) collective-permute-start(bf16[64,1152]{1,0:T(8,128)(2,1)S(1)} %get-tuple-element.58), channel_id=1, source_target_pairs={{0,1},{1,0},{2,3},{3,2},{4,5},{5,4},{6,7},{7,6},{8,9},{9,8},{10,11... | collective-permute-start | bytes 442376 | tf_op jit(solution)/shard_map/ppermute | solution.py:21
  25.4 6.7 %collective-permute-start.12 = (bf16[64,1152]{1,0:T(8,128)(2,1)S(1)}, bf16[64,1152]{1,0:T(8,128)(2,1)S(1)}, u32[]{:S(2)}, u32[]{:S(2)}) collective-permute-start(bf16[64,1152]{1,0:T(8,128)(2,1)S(1)} %get-tuple-element.59), channel_id=1, source_target_pairs={{0,2},{1,3},{2,0},{3,1},{4,6},{5,7},{6,4},{7,5},{8,10},{9,11},{10,... | collective-permute-start | bytes 442376 | tf_op jit(solution)/shard_map/ppermute | solution.py:21
  26.9 10.1 %collective-permute-start.10 = (bf16[128,1152]{1,0:T(8,128)(2,1)S(1)}, bf16[128,1152]{1,0:T(8,128)(2,1)S(1)}, u32[]{:S(2)}, u32[]{:S(2)}) collective-permute-start(bf16[128,1152]{1,0:T(8,128)(2,1)S(1)} %shard_map.84.refs_0_), channel_id=1, source_target_pairs={{0,1},{1,0},{2,3},{3,2},{4,5},{5,4},{6,7},{7,6},{8,9},{9,8},{10,11... | collective-permute-start | bytes 884744 | tf_op jit(solution)/shard_map/ppermute | solution.py:21
  27.5 14.1 %collective-permute-start.8 = (bf16[128,1152]{1,0:T(8,128)(2,1)S(1)}, bf16[128,1152]{1,0:T(8,128)(2,1)S(1)}, u32[]{:S(2)}, u32[]{:S(2)}) collective-permute-start(bf16[128,1152]{1,0:T(8,128)(2,1)S(1)} %shard_map.84.refs_0_), channel_id=1, source_target_pairs={{0,2},{1,3},{2,0},{3,1},{4,6},{5,7},{6,4},{7,5},{8,10},{9,11},{10,... | collective-permute-start | bytes 884744 | tf_op jit(solution)/shard_map/ppermute | solution.py:21
  28.1 13.5 %collective-permute-start.9 = (bf16[128,1152]{1,0:T(8,128)(2,1)S(1)}, bf16[128,1152]{1,0:T(8,128)(2,1)S(1)}, u32[]{:S(2)}, u32[]{:S(2)}) collective-permute-start(bf16[128,1152]{1,0:T(8,128)(2,1)S(1)} %shard_map.84.refs_0_), channel_id=1, source_target_pairs={{0,3},{1,2},{2,1},{3,0},{4,7},{5,6},{6,5},{7,4},{8,11},{9,10},{10,... | collective-permute-start | bytes 884744 | tf_op jit(solution)/shard_map/ppermute | solution.py:21
  35.3 7.1 %collective-permute-start.13 = (bf16[144,1152]{1,0:T(8,128)(2,1)S(1)}, bf16[144,1152]{1,0:T(8,128)(2,1)S(1)}, u32[]{:S(2)}, u32[]{:S(2)}) collective-permute-start(bf16[144,1152]{1,0:T(8,128)(2,1)S(1)} %collective-permute-done.4.refs_4_), channel_id=1, source_target_pairs={{0,4},{4,0},{8,12},{12,8},{16,20},{20,16},{24,28},{28,24},{1,5},{5... | collective-permute-start | bytes 995336 | tf_op jit(solution)/shard_map/ppermute | solution.py:21
  35.4 7.0 %collective-permute-start.14 = (bf16[144,1152]{1,0:T(8,128)(2,1)S(1)}, bf16[144,1152]{1,0:T(8,128)(2,1)S(1)}, u32[]{:S(2)}, u32[]{:S(2)}) collective-permute-start(bf16[144,1152]{1,0:T(8,128)(2,1)S(1)} %collective-permute-done.5.refs_6_), channel_id=1, source_target_pairs={{0,4},{4,0},{8,12},{12,8},{16,20},{20,16},{24,28},{28,24},{1,5},{5... | collective-permute-start | bytes 995336 | tf_op jit(solution)/shard_map/ppermute | solution.py:21
  39.1 3.3 %copy-start.3 = (s32[1,4]{1,0:T(1,128)S(1)}, s32[1,4]{1,0:T(1,128)}, u32[]{:S(2)}) copy-start(s32[1,4]{1,0:T(1,128)} %length_ref.3) | copy-start | bytes 52
  39.1 11.5 %collective-permute-start.18 = (bf16[144,1152]{1,0:T(8,128)(2,1)S(1)}, bf16[144,1152]{1,0:T(8,128)(2,1)S(1)}, u32[]{:S(2)}, u32[]{:S(2)}) collective-permute-start(bf16[144,1152]{1,0:T(8,128)(2,1)S(1)} %collective-permute-done.5.refs_6_), channel_id=1, source_target_pairs={{0,1},{1,0},{2,3},{3,2},{4,5},{5,4},{6,7},{7,6},{8,9},{9,8},{10,11... | collective-permute-start | bytes 995336 | tf_op jit(solution)/shard_map/ppermute | solution.py:21
  47.0 6.2 %collective-permute-start.15 = (bf16[288,256]{1,0:T(8,128)(2,1)S(1)}, bf16[288,256]{1,0:T(8,128)(2,1)S(1)}, u32[]{:S(2)}, u32[]{:S(2)}) collective-permute-start(bf16[288,256]{1,0:T(8,128)(2,1)S(1)} %get-tuple-element.74), channel_id=1, source_target_pairs={{0,1},{1,0},{2,3},{3,2},{4,5},{5,4},{6,7},{7,6},{8,9},{9,8},{10,11... | collective-permute-start | bytes 442376 | tf_op jit(solution)/shard_map/ppermute | solution.py:21
  48.9 6.7 %collective-permute-start.16 = (bf16[288,256]{1,0:T(8,128)(2,1)S(1)}, bf16[288,256]{1,0:T(8,128)(2,1)S(1)}, u32[]{:S(2)}, u32[]{:S(2)}) collective-permute-start(bf16[288,256]{1,0:T(8,128)(2,1)S(1)} %get-tuple-element.75), channel_id=1, source_target_pairs={{0,2},{1,3},{2,0},{3,1},{4,6},{5,7},{6,4},{7,5},{8,10},{9,11},{10,... | collective-permute-start | bytes 442376 | tf_op jit(solution)/shard_map/ppermute | solution.py:21
  49.4 7.4 %collective-permute-start.17 = (bf16[288,256]{1,0:T(8,128)(2,1)S(1)}, bf16[288,256]{1,0:T(8,128)(2,1)S(1)}, u32[]{:S(2)}, u32[]{:S(2)}) collective-permute-start(bf16[288,256]{1,0:T(8,128)(2,1)S(1)} %get-tuple-element.80), channel_id=1, source_target_pairs={{0,3},{1,2},{2,1},{3,0},{4,7},{5,6},{6,5},{7,4},{8,11},{9,10},{10,... | collective-permute-start | bytes 442376 | tf_op jit(solution)/shard_map/ppermute | solution.py:21
  50.6 6.2 %collective-permute-start.19 = (bf16[144,1152]{1,0:T(8,128)(2,1)S(1)}, bf16[144,1152]{1,0:T(8,128)(2,1)S(1)}, u32[]{:S(2)}, u32[]{:S(2)}) collective-permute-start(bf16[144,1152]{1,0:T(8,128)(2,1)S(1)} %collective-permute-done.18.refs_1_), channel_id=1, source_target_pairs={{0,4},{4,0},{8,12},{12,8},{16,20},{20,16},{24,28},{28,24},{1,5},{5... | collective-permute-start | bytes 995336 | tf_op jit(solution)/shard_map/ppermute | solution.py:21
  58.3 7.9 %collective-permute-start.24 = (bf16[64,1152]{1,0:T(8,128)(2,1)S(1)}, bf16[64,1152]{1,0:T(8,128)(2,1)S(1)}, u32[]{:S(2)}, u32[]{:S(2)}) collective-permute-start(bf16[64,1152]{1,0:T(8,128)(2,1)S(1)} %get-tuple-element.87), channel_id=1, source_target_pairs={{0,8},{4,12},{8,0},{12,4},{16,24},{20,28},{24,16},{28,20},{1,9},{5... | collective-permute-start | bytes 442376 | tf_op jit(solution)/shard_map/ppermute | solution.py:21
  60.0 6.3 %collective-permute-start.20 = (bf16[32,1152]{1,0:T(8,128)(2,1)S(1)}, bf16[32,1152]{1,0:T(8,128)(2,1)S(1)}, u32[]{:S(2)}, u32[]{:S(2)}) collective-permute-start(bf16[32,1152]{1,0:T(8,128)(2,1)S(1)} %get-tuple-element.82), channel_id=1, source_target_pairs={{0,16},{4,20},{8,24},{12,28},{16,0},{20,4},{24,8},{28,12},{1,17},{... | collective-permute-start | bytes 221192 | tf_op jit(solution)/shard_map/ppermute | solution.py:21
  61.4 11.0 %collective-permute-start.21 = (bf16[32,1152]{1,0:T(8,128)(2,1)S(1)}, bf16[32,1152]{1,0:T(8,128)(2,1)S(1)}, u32[]{:S(2)}, u32[]{:S(2)}) collective-permute-start(bf16[32,1152]{1,0:T(8,128)(2,1)S(1)} %get-tuple-element.83), channel_id=1, source_target_pairs={{0,20},{4,16},{8,28},{12,24},{16,4},{20,0},{24,12},{28,8},{1,21},{... | collective-permute-start | bytes 221192 | tf_op jit(solution)/shard_map/ppermute | solution.py:21
  61.4 11.0 %collective-permute-start.22 = (bf16[32,1152]{1,0:T(8,128)(2,1)S(1)}, bf16[32,1152]{1,0:T(8,128)(2,1)S(1)}, u32[]{:S(2)}, u32[]{:S(2)}) collective-permute-start(bf16[32,1152]{1,0:T(8,128)(2,1)S(1)} %get-tuple-element.84), channel_id=1, source_target_pairs={{0,24},{4,28},{8,16},{12,20},{16,8},{20,12},{24,0},{28,4},{1,25},{... | collective-permute-start | bytes 221192 | tf_op jit(solution)/shard_map/ppermute | solution.py:21
  62.7 9.7 %collective-permute-start.23 = (bf16[32,1152]{1,0:T(8,128)(2,1)S(1)}, bf16[32,1152]{1,0:T(8,128)(2,1)S(1)}, u32[]{:S(2)}, u32[]{:S(2)}) collective-permute-start(bf16[32,1152]{1,0:T(8,128)(2,1)S(1)} %get-tuple-element.85), channel_id=1, source_target_pairs={{0,28},{4,24},{8,20},{12,16},{16,12},{20,8},{24,4},{28,0},{1,29},{... | collective-permute-start | bytes 221192 | tf_op jit(solution)/shard_map/ppermute | solution.py:21
  66.2 6.2 %copy-start.7 = (s32[64]{0:T(128)S(1)}, s32[64]{0:T(128)}, u32[]{:S(2)}) copy-start(s32[64]{0:T(128)} %get-tuple-element.47.slot_ref) | copy-start | bytes 772
  66.2 6.2 %collective-permute-start.25 = (bf16[64,1152]{1,0:T(8,128)(2,1)S(1)}, bf16[64,1152]{1,0:T(8,128)(2,1)S(1)}, u32[]{:S(2)}, u32[]{:S(2)}) collective-permute-start(bf16[64,1152]{1,0:T(8,128)(2,1)S(1)} %shard_map.97), channel_id=1, source_target_pairs={{0,4},{4,0},{8,12},{12,8},{16,20},{20,16},{24,28},{28,24},{1,5},{5... | collective-permute-start | bytes 442376 | tf_op jit(solution)/shard_map/ppermute | solution.py:21
where the time goes:
time: 75 us; the launch traced here: 74 us
  starting transfers between devices  31.3 us (42%)
  waiting for transfers between devices  24.1 us (32%)
  Pallas kernels  18.3 us (24%)
    ppermute x26, starting transfers between devices, send(): return lax.ppermute(array, axis, [(i, i ^ mask) for i in range(count)])  31.3 us
    ppermute x26, waiting for transfers between devices, send(): return lax.ppermute(array, axis, [(i, i ^ mask) for i in range(count)])  24.1 us
    pallas_call x17, Pallas kernels, call(): pl.pallas_call(kernel, in_specs=[smem] * len(scalars) + (where if isinsta...  18.3 us
  transfers between devices with their start and end apart: 26, of which 11 were waited for; matrix products, arithmetic and copies ran while one was open for 0% of the time, Pallas kernels for 18%

commit v1 on v0

--- a/solution.py
+++ b/solution.py
@@ -199,7 +199,7 @@
 def attention_kernel(
     head_size, per_peer, piece_rows, length_ref, owner_ref, place_ref, table_ref, *refs
 ):
-    early_ref, late_ref, out_refs, all_ref = refs[0], refs[1], refs[2:-1], refs[-1]
+    early_ref, late_ref, out_refs = refs[0], refs[1], refs[2:]
     clips, features, clip_tokens = early_ref.shape
     width, tokens = features // 3, clips * clip_tokens
     seq_count = len(out_refs)
@@ -211,6 +211,7 @@
     key = lax.broadcasted_iota(jnp.int32, (8, clip_tokens), 1)
     heads = range(0, width, head_size)
     scale = math.log2(math.e) / math.sqrt(head_size)
+    attended, chosen_by_clip = [], []
     for clip in range(clips):
         chosen = jnp.where(code == position + clip * clip_tokens, 1.0, 0.0).astype(BF16)
         picked = early_ref[clip].astype(F32) + lax.dot_general(
@@ -235,42 +236,37 @@
             values = jnp.concatenate([values, in_clip], axis=0).astype(BF16)
             summed = jnp.dot(values, weights, preferred_element_type=F32)
             outs.append(summed[:head_size] * (1.0 / summed[head_size : head_size + 1]))
-        attended = jnp.concatenate(outs, axis=0).astype(BF16)
-        back = jnp.dot(attended, chosen, preferred_element_type=F32)
-        if clip == 0:
-            all_ref[...] = back
-        else:
-            all_ref[...] += back
+        attended.append(jnp.concatenate(outs, axis=0).astype(BF16))
+        chosen_by_clip.append(chosen)
+    back = jnp.dot(
+        jnp.concatenate(attended, axis=1),
+        jnp.concatenate(chosen_by_clip, axis=0),
+        preferred_element_type=F32,
+    ).astype(BF16)
     for index, ref in enumerate(out_refs):
         for group in range(2):
             start = (group * seq_count + index) * group_rows
-            ref[:, group * group_rows : (group + 1) * group_rows] = all_ref[
+            ref[:, group * group_rows : (group + 1) * group_rows] = back[
                 :, start : start + group_rows
-            ].astype(BF16)
+            ]
 
 
 def projected_rows(masks, halves, core_ref, head_refs, weight_refs):
     branch = None
     for mask, head_ref in zip(masks, head_refs):
-        parts = [weight_refs[0][...]]
-        if mask > 0:
-            parts = [ref[...] for ref in weight_refs[:halves]]
-            weight_refs = weight_refs[halves:]
-            if halves == 2:
-                first = core_ref[0] == 0
-                parts = [
-                    jnp.where(first, parts[0], parts[1]),
-                    jnp.where(first, parts[1], parts[0]),
-                ]
-        else:
-            weight_refs = weight_refs[1:]
-        term = lax.dot_general(
-            head_ref[...],
-            jnp.concatenate(parts, axis=0),
-            (((0,), (0,)), ((), ())),
-            preferred_element_type=F32,
-        )
-        branch = term if branch is None else branch + term
+        parts = 1 if mask == 0 else halves
+        for part in range(parts):
+            weight = weight_refs[part][...]
+            head = head_ref[...]
+            if parts == 2:
+                rows = weight.shape[0]
+                start = jnp.bitwise_xor(core_ref[0], part) * rows
+                head = head_ref[pl.ds(pl.multiple_of(start, 16), rows), :]
+            term = lax.dot_general(
+                head, weight, (((0,), (0,)), ((), ())), preferred_element_type=F32
+            )
+            branch = term if branch is None else branch + term
+        weight_refs = weight_refs[parts:]
     return branch
 
 
@@ -280,39 +276,32 @@
     )
 
 
-def output_kernel(
-    masks,
-    halves,
-    clip_tokens,
-    codes_of,
-    owner_masks,
-    core_ref,
-    length_ref,
-    owner_ref,
-    place_ref,
-    table_ref,
-    modulation_ref,
-    partial_ref,
-    *refs,
+def residual_kernel(
+    clip_tokens, codes_of, length_ref, owner_ref, place_ref, table_ref, modulation_ref, *refs
 ):
-    head_refs, refs = refs[: len(masks)], refs[len(masks) :]
-    weight_refs, refs = refs[: len(masks) * halves], refs[len(masks) * halves :]
-    count = len(owner_masks) // 2
-    block_refs, out_refs = refs[:count], refs[count:]
-    rows = block_refs[0].shape[0] // 2
-    branch = partial_ref[...] + projected_rows(masks, halves, core_ref, head_refs, weight_refs)
-    code = codes_of(branch.shape[0], owner_ref[0], place_ref[0], table_ref[0])
+    block_refs, (base_ref, gate_ref) = refs[:-2], refs[-2:]
+    code = codes_of(base_ref.shape[0], owner_ref[0], place_ref[0], table_ref[0])
     clip = lax.div(code, clip_tokens)
     limit = jnp.zeros_like(code)
     for index in range(length_ref.shape[1]):
         limit = jnp.where(clip == index, length_ref[0, index], limit)
     kept = lax.rem(code, clip_tokens) < limit
-    branch = pick(clip, modulation_ref[2].astype(F32)) * branch
+    rows = jnp.concatenate([ref[...].astype(F32) for ref in block_refs], axis=0)
+    base_ref[...] = jnp.where(kept, rows, 0.0).astype(BF16)
+    gate = pick(clip, modulation_ref[2].astype(F32))
+    gate_ref[...] = jnp.where(kept, gate, 0.0).astype(BF16)
+
+
+def output_kernel(masks, halves, owner_masks, core_ref, base_ref, gate_ref, partial_ref, *refs):
+    head_refs, refs = refs[: len(masks)], refs[len(masks) :]
+    weight_refs, out_refs = refs[: len(masks) * halves], refs[len(masks) * halves :]
+    branch = partial_ref[...] + projected_rows(masks, halves, core_ref, head_refs, weight_refs)
+    result = base_ref[...].astype(F32) + gate_ref[...].astype(F32) * branch
+    rows = result.shape[0] // len(owner_masks)
     for index, (out, first) in enumerate(owner_masks):
-        at = slice(index * rows, (index + 1) * rows)
-        side = slice(index % 2 * rows, (index % 2 + 1) * rows)
-        result = block_refs[index // 2][side].astype(F32) + branch[at]
-        out_refs[out][first : first + rows] = jnp.where(kept[at], result, 0.0).astype(BF16)
+        out_refs[out][first : first + rows] = result[index * rows : (index + 1) * rows].astype(
+            BF16
+        )
 
 
 def body(
@@ -468,7 +457,15 @@
     gathered = gather(0, stacked_near)
     gathered, proj_parts = lax.optimization_barrier((gathered, proj_parts))
     early_blocks, late_blocks = far_blocks[: seq_count // 2], far_blocks[seq_count // 2 :]
-    early_blocks, gathered = lax.optimization_barrier((early_blocks, gathered))
+    residual = call(
+        functools.partial(residual_kernel, clip_tokens, codes_of(0)),
+        [clip_length, owner_place, place],
+        [clip_pieces, factors] + arrived,
+        [((rows_here, model_width), BF16)] * 2,
+    )
+    early_blocks, gathered, residual = lax.optimization_barrier(
+        (early_blocks, gathered, list(residual))
+    )
     gathered = gather(seq_count * group_rows, project(early_blocks), gathered)
     swapped = {mask: send(proj_parts[mask], "dp", 1) for mask in proj_parts} if halves == 2 else {}
     gathered, proj_parts = lax.optimization_barrier((gathered, proj_parts))
@@ -483,7 +480,6 @@
         [clip_length, owner_place, place, clip_pieces],
         [gathered, stacked_late],
         [((head_width, rows_here), BF16)] * seq_count,
-        scratch=[pltpu.VMEM((head_width, seq_count * rows_here), F32)],
         limit=16 if clip_tokens <= 256 else 48,
         flops=10**8,
     )
@@ -521,19 +517,9 @@
         flops=10**10,
     )
     results = call(
-        functools.partial(
-            output_kernel,
-            across,
-            halves,
-            clip_tokens,
-            codes_of(0),
-            [outs[mask] for mask in range(dp_count)],
-        ),
-        [core, clip_length, owner_place, place],
-        [clip_pieces, factors, partial]
-        + [returned[mask] for mask in across]
-        + weights_of(across)
-        + arrived,
+        functools.partial(output_kernel, across, halves, [outs[mask] for mask in range(dp_count)]),
+        [core],
+        residual + [partial] + [returned[mask] for mask in across] + weights_of(across),
         [((block_rows, model_width), BF16)] * half_count
         + [((2 * block_rows, model_width), BF16)] * (half_count // 2 - 1)
         + [((block_rows, model_width), BF16)] * 2,

time: 75 us -> 76.2 us (1.016)
  starting transfers between devices: 31.3 us -> 33 us
    ppermute x26, starting transfers between devices: 31.3 us -> 33 us  [send(): return lax.ppermute(array, axis, [(i, i ^ mask) for i in range(count)])]
    pallas_call x17 -> x18, Pallas kernels: 18.3 us -> 18.3 us  [call(): pl.pallas_call(kernel, in_specs=[smem] * len(scalars) + (where if isinsta...]
  transfers between devices with their start and end apart: 26 -> 26, of which waited for: 11 -> 10; matrix products, arithmetic and copies ran while one was open for 0% -> 0% of each run, Pallas kernels for 18% -> 19%
where the time goes in v1:
time: 76.2 us; the launch traced here: 75.1 us
  starting transfers between devices  33 us (43%)
  waiting for transfers between devices  23.5 us (31%)
  Pallas kernels  18.3 us (24%)
    ppermute x26, starting transfers between devices, send(): return lax.ppermute(array, axis, [(i, i ^ mask) for i in range(count)])  33 us
    ppermute x26, waiting for transfers between devices, send(): return lax.ppermute(array, axis, [(i, i ^ mask) for i in range(count)])  23.5 us
    pallas_call x18, Pallas kernels, call(): pl.pallas_call(kernel, in_specs=[smem] * len(scalars) + (where if isinsta...  18.3 us
  transfers between devices with their start and end apart: 26, of which 10 were waited for; matrix products, arithmetic and copies ran while one was open for 0% of the time, Pallas kernels for 19%

profile of v1, /device:TPU:0, one launch (start us, length us, event | category | flops | bytes accessed | tf_op | source)
XLA Modules:
  0.0 75.1 jit_solution(4264068836990842094)
XLA Ops:
  0.0 2.1 %shard_map.82 = (s32[64]{0:T(128)}, bf16[128,1152]{1,0:T(8,128)(2,1)}, bf16[128,1152]{1,0:T(8,128)(2,1)}) custom-call(s32[1]{0:T(128)} %bitcast.place_ref.owner_ref, s32[1,64]{1,0:T(1,128)} %owner_hbm.1, bf16[1,64,4,1152]{3,2,1,0:T(4,128)(2,1)} %token_hbm.1), custom_call_target="tpu_custom_call" | custom-call | flops 30000001024 | bytes 1048576 | tf_op jit(solution)/shard_map/pallas_call | solution.py:337
  2.1 0.5 collective-permute-start
  2.7 0.1 shard_map.86
  2.8 2.6 %collective-permute-start.4 = (bf16[144,1152]{1,0:T(8,128)(2,1)S(1)}, bf16[144,1152]{1,0:T(8,128)(2,1)S(1)}, u32[]{:S(2)}, u32[]{:S(2)}) collective-permute-start(bf16[144,1152]{1,0:T(8,128)(2,1)S(1)} %shard_map.86), channel_id=1, source_target_pairs={{0,1},{1,0},{2,3},{3,2},{4,5},{5,4},{6,7},{7,6},{8,9},{9,8},{10,11... | collective-permute-start | bytes 995336 | tf_op jit(solution)/shard_map/ppermute | solution.py:21
  5.4 1.5 %collective-permute-start.5 = (bf16[144,1152]{1,0:T(8,128)(2,1)S(1)}, bf16[144,1152]{1,0:T(8,128)(2,1)S(1)}, u32[]{:S(2)}, u32[]{:S(2)}) collective-permute-start(bf16[144,1152]{1,0:T(8,128)(2,1)S(1)} %shard_map.86), channel_id=1, source_target_pairs={{0,2},{1,3},{2,0},{3,1},{4,6},{5,7},{6,4},{7,5},{8,10},{9,11},{10,... | collective-permute-start | bytes 995336 | tf_op jit(solution)/shard_map/ppermute | solution.py:21
  6.9 0.0 collective-permute-done.other_ref
  6.9 0.1 shard_map.83
  7.0 1.6 %collective-permute-start.3 = (bf16[64,1152]{1,0:T(8,128)(2,1)S(1)}, bf16[64,1152]{1,0:T(8,128)(2,1)S(1)}, u32[]{:S(2)}, u32[]{:S(2)}) collective-permute-start(bf16[64,1152]{1,0:T(8,128)(2,1)S(1)} %get-tuple-element.57), channel_id=1, source_target_pairs={{0,8},{4,12},{8,0},{12,4},{16,24},{20,28},{24,16},{28,20},{1,9},{5... | collective-permute-start | bytes 442376 | tf_op jit(solution)/shard_map/ppermute | solution.py:21
  8.7 2.6 %collective-permute-start.1 = (bf16[64,1152]{1,0:T(8,128)(2,1)S(1)}, bf16[64,1152]{1,0:T(8,128)(2,1)S(1)}, u32[]{:S(2)}, u32[]{:S(2)}) collective-permute-start(bf16[64,1152]{1,0:T(8,128)(2,1)S(1)} %get-tuple-element.54), channel_id=1, source_target_pairs={{0,16},{4,20},{8,24},{12,28},{16,0},{20,4},{24,8},{28,12},{1,17},{... | collective-permute-start | bytes 442376 | tf_op jit(solution)/shard_map/ppermute | solution.py:21
  11.3 0.2 collective-permute-start.2
  11.5 3.4 %collective-permute-done.3.refs_1_ = bf16[64,1152]{1,0:T(8,128)(2,1)S(1)} collective-permute-done((bf16[64,1152]{1,0:T(8,128)(2,1)S(1)}, bf16[64,1152]{1,0:T(8,128)(2,1)S(1)}, u32[]{:S(2)}, u32[]{:S(2)}) %collective-permute-start.3) | collective-permute-done | bytes 147488 | tf_op jit(solution)/shard_map/ppermute | solution.py:21
  14.9 0.6 shard_map.85.refs_0_
  15.5 0.0 collective-permute-done.4.refs_4_
  15.5 0.0 collective-permute-done.5.refs_6_
  15.5 0.6 collective-permute-start.6
  16.1 1.5 %collective-permute-start.7 = (bf16[128,1152]{1,0:T(8,128)(2,1)S(1)}, bf16[128,1152]{1,0:T(8,128)(2,1)S(1)}, u32[]{:S(2)}, u32[]{:S(2)}) collective-permute-start(bf16[128,1152]{1,0:T(8,128)(2,1)S(1)} %shard_map.85.refs_0_), channel_id=1, source_target_pairs={{0,2},{1,3},{2,0},{3,1},{4,6},{5,7},{6,4},{7,5},{8,10},{9,11},{10,... | collective-permute-start | bytes 884744 | tf_op jit(solution)/shard_map/ppermute | solution.py:21
  17.6 5.1 %collective-permute-done.1.refs_0_.refs_2_ = bf16[64,1152]{1,0:T(8,128)(2,1)S(1)} collective-permute-done((bf16[64,1152]{1,0:T(8,128)(2,1)S(1)}, bf16[64,1152]{1,0:T(8,128)(2,1)S(1)}, u32[]{:S(2)}, u32[]{:S(2)}) %collective-permute-start.1) | collective-permute-done | bytes 147488 | tf_op jit(solution)/shard_map/ppermute | solution.py:21
  22.7 0.6 shard_map.84.refs_0_
  23.2 0.0 copy-start.3
  23.2 0.3 collective-permute-done.6.refs_1_
  23.6 0.4 collective-permute-done.7.refs_0_.refs_2_
  24.0 1.5 %collective-permute-start.10 = (bf16[64,1152]{1,0:T(8,128)(2,1)S(1)}, bf16[64,1152]{1,0:T(8,128)(2,1)S(1)}, u32[]{:S(2)}, u32[]{:S(2)}) collective-permute-start(bf16[64,1152]{1,0:T(8,128)(2,1)S(1)} %get-tuple-element.63), channel_id=1, source_target_pairs={{0,2},{1,3},{2,0},{3,1},{4,6},{5,7},{6,4},{7,5},{8,10},{9,11},{10,... | collective-permute-start | bytes 442376 | tf_op jit(solution)/shard_map/ppermute | solution.py:21
  25.5 1.4 %collective-permute-start.9 = (bf16[64,1152]{1,0:T(8,128)(2,1)S(1)}, bf16[64,1152]{1,0:T(8,128)(2,1)S(1)}, u32[]{:S(2)}, u32[]{:S(2)}) collective-permute-start(bf16[64,1152]{1,0:T(8,128)(2,1)S(1)} %get-tuple-element.62), channel_id=1, source_target_pairs={{0,1},{1,0},{2,3},{3,2},{4,5},{5,4},{6,7},{7,6},{8,9},{9,8},{10,11... | collective-permute-start | bytes 442376 | tf_op jit(solution)/shard_map/ppermute | solution.py:21
  26.9 1.3 %shard_map.90 = (bf16[256,1152]{1,0:T(8,128)(2,1)S(1)}, bf16[256,1152]{1,0:T(8,128)(2,1)S(1)}) custom-call(s32[1,4]{1,0:T(1,128)S(1)} %copy-done.3, s32[1]{0:T(128)} %bitcast.place_ref.owner_ref, s32[1]{0:T(128)} %bitcast.2.place_ref, s32[1,4,16]{2,1,0:T(4,128)S(1)} %copy-done.1, bf16[3,4,1152]{2,1,0:T(4,128)(2,1)S(1)} %bitcast.14, ...), custom_call_target="tpu_custom_call" | custom-call | flops 1000000000 | bytes 1048576 | tf_op jit(solution)/shard_map/pallas_call | solution.py:337
  28.2 0.7 collective-permute-start.8
  28.8 0.6 collective-permute-start.11
  29.4 2.3 %collective-permute-start.12 = (bf16[128,1152]{1,0:T(8,128)(2,1)S(1)}, bf16[128,1152]{1,0:T(8,128)(2,1)S(1)}, u32[]{:S(2)}, u32[]{:S(2)}) collective-permute-start(bf16[128,1152]{1,0:T(8,128)(2,1)S(1)} %shard_map.84.refs_0_), channel_id=1, source_target_pairs={{0,3},{1,2},{2,1},{3,0},{4,7},{5,6},{6,5},{7,4},{8,11},{9,10},{10,... | collective-permute-start | bytes 884744 | tf_op jit(solution)/shard_map/ppermute | solution.py:21
  31.7 0.0 collective-permute-done.10.refs_4_
  31.7 0.4 collective-permute-done.9.refs_3_
  32.2 1.4 %shard_map.88.stacked_ref = bf16[864,512]{1,0:T(8,128)(2,1)S(1)} custom-call(bf16[864,1152]{1,0:T(8,128)(2,1)S(1)} %bitcast.9, f32[2,72]{1,0:T(2,128)S(1)} %copy-done.2, bf16[128,1152]{1,0:T(8,128)(2,1)S(1)} %shard_map.85.refs_0_, bf16[128,1152]{1,0:T(8,128)(2,1)S(1)} %collective-permute-done.6.refs_1_, ...), custom_call_target="tpu_custom_call" | custom-call | flops 3000000000 | bytes 1048576 | tf_op jit(solution)/shard_map/pallas_call | solution.py:337
  33.5 1.8 %shard_map.89.refs_0_ = bf16[4,864,256]{2,1,0:T(8,128)(2,1)S(1)} custom-call(s32[1]{0:T(128)} %bitcast.place_ref.owner_ref, s32[1]{0:T(128)} %bitcast.2.place_ref, s32[1,4,16]{2,1,0:T(4,128)S(1)} %copy-done.1, bf16[864,512]{1,0:T(8,128)(2,1)S(1)} %shard_map.88.stacked_ref), custom_call_target="tpu_custom_call" | custom-call | flops 3000000000 | bytes 1048576 | tf_op jit(solution)/shard_map/pallas_call | solution.py:337
  35.3 0.1 collective-permute-start.13
  35.4 0.5 collective-permute-start.14
  35.9 2.6 %collective-permute-done.8.refs_1_ = bf16[128,1152]{1,0:T(8,128)(2,1)S(1)} collective-permute-done((bf16[128,1152]{1,0:T(8,128)(2,1)S(1)}, bf16[128,1152]{1,0:T(8,128)(2,1)S(1)}, u32[]{:S(2)}, u32[]{:S(2)}) %collective-permute-start.8) | collective-permute-done | bytes 294944 | tf_op jit(solution)/shard_map/ppermute | solution.py:21
  38.5 0.8 %shard_map.91.stacked_ref = bf16[864,256]{1,0:T(8,128)(2,1)S(1)} custom-call(bf16[864,1152]{1,0:T(8,128)(2,1)S(1)} %bitcast.10, f32[2,72]{1,0:T(2,128)S(1)} %copy-done.2, bf16[128,1152]{1,0:T(8,128)(2,1)S(1)} %shard_map.84.refs_0_, bf16[128,1152]{1,0:T(8,128)(2,1)S(1)} %collective-permute-done.8.refs_1_), custom_call_target="tpu_custom_call" | custom-call | flops 3000000000 | bytes 1048576 | tf_op jit(solution)/shard_map/pallas_call | solution.py:337
  39.3 1.3 %shard_map.92.refs_0_ = bf16[4,864,256]{2,1,0:T(8,128)(2,1)S(1)} custom-call(s32[1]{0:T(128)} %bitcast.place_ref.owner_ref, s32[1]{0:T(128)} %bitcast.2.place_ref, s32[1,4,16]{2,1,0:T(4,128)S(1)} %copy-done.1, bf16[864,256]{1,0:T(8,128)(2,1)S(1)} %shard_map.91.stacked_ref, bf16[4,864,256]{2,1,0:T(8,128)(2,1)S(1)} %shard_map.89.refs_0_), custom_call_target="tpu_custom_call" | custom-call | flops 3000000000 | bytes 1048576 | tf_op jit(solution)/shard_map/pallas_call | solution.py:337
  40.6 1.6 %collective-permute-start.18 = (bf16[144,1152]{1,0:T(8,128)(2,1)S(1)}, bf16[144,1152]{1,0:T(8,128)(2,1)S(1)}, u32[]{:S(2)}, u32[]{:S(2)}) collective-permute-start(bf16[144,1152]{1,0:T(8,128)(2,1)S(1)} %collective-permute-done.5.refs_6_), channel_id=1, source_target_pairs={{0,1},{1,0},{2,3},{3,2},{4,5},{5,4},{6,7},{7,6},{8,9},{9,8},{10,11... | collective-permute-start | bytes 995336 | tf_op jit(solution)/shard_map/ppermute | solution.py:21
  42.2 0.0 collective-permute-done.11.refs_0_
  42.2 1.9 %collective-permute-done.12.refs_1_ = bf16[128,1152]{1,0:T(8,128)(2,1)S(1)} collective-permute-done((bf16[128,1152]{1,0:T(8,128)(2,1)S(1)}, bf16[128,1152]{1,0:T(8,128)(2,1)S(1)}, u32[]{:S(2)}, u32[]{:S(2)}) %collective-permute-start.12) | collective-permute-done | bytes 294944 | tf_op jit(solution)/shard_map/ppermute | solution.py:21
  44.1 0.8 %shard_map.93.refs_1_ = bf16[864,256]{1,0:T(8,128)(2,1)S(1)} custom-call(bf16[864,1152]{1,0:T(8,128)(2,1)S(1)} %bitcast.11, f32[2,72]{1,0:T(2,128)S(1)} %copy-done.2, bf16[128,1152]{1,0:T(8,128)(2,1)S(1)} %collective-permute-done.11.refs_0_, bf16[128,1152]{1,0:T(8,128)(2,1)S(1)} %collective-permute-done.12.refs_1_), custom_call_target="tpu_custom_call" | custom-call | flops 100000000 | bytes 1048576 | tf_op jit(solution)/shard_map/pallas_call | solution.py:337
  44.9 0.0 collective-permute-done.13.refs_5_
  44.9 4.2 %shard_map.94 = (bf16[288,256]{1,0:T(8,128)(2,1)S(1)}, bf16[288,256]{1,0:T(8,128)(2,1)S(1)}, bf16[288,256]{1,0:T(8,128)(2,1)S(1)}, bf16[288,256]{1,0:T(8,128)(2,1)S(1)}) custom-call(s32[1,4]{1,0:T(1,128)S(1)} %copy-done.3, s32[1]{0:T(128)} %bitcast.place_ref.owner_ref, s32[1]{0:T(128)} %bitcast.2.place_ref, s32[1,4,16]{2,1,0:T(4,128)S(1)} %copy-done.1, ...), custom_call_target="tpu_custom_call" | custom-call | flops 100000000 | bytes 1048576 | tf_op jit(solution)/shard_map/pallas_call | solution.py:337
  49.1 0.1 collective-permute-start.15
  49.2 1.9 %collective-permute-start.16 = (bf16[288,256]{1,0:T(8,128)(2,1)S(1)}, bf16[288,256]{1,0:T(8,128)(2,1)S(1)}, u32[]{:S(2)}, u32[]{:S(2)}) collective-permute-start(bf16[288,256]{1,0:T(8,128)(2,1)S(1)} %get-tuple-element.83), channel_id=1, source_target_pairs={{0,2},{1,3},{2,0},{3,1},{4,6},{5,7},{6,4},{7,5},{8,10},{9,11},{10,... | collective-permute-start | bytes 442376 | tf_op jit(solution)/shard_map/ppermute | solution.py:21
  51.1 1.5 %collective-permute-start.17 = (bf16[288,256]{1,0:T(8,128)(2,1)S(1)}, bf16[288,256]{1,0:T(8,128)(2,1)S(1)}, u32[]{:S(2)}, u32[]{:S(2)}) collective-permute-start(bf16[288,256]{1,0:T(8,128)(2,1)S(1)} %get-tuple-element.88), channel_id=1, source_target_pairs={{0,3},{1,2},{2,1},{3,0},{4,7},{5,6},{6,5},{7,4},{8,11},{9,10},{10,... | collective-permute-start | bytes 442376 | tf_op jit(solution)/shard_map/ppermute | solution.py:21
  52.6 0.0 collective-permute-done.18.refs_1_
  52.6 0.0 collective-permute-start.19
  52.6 1.9 %collective-permute-done.15.refs_1_ = bf16[288,256]{1,0:T(8,128)(2,1)S(1)} collective-permute-done((bf16[288,256]{1,0:T(8,128)(2,1)S(1)}, bf16[288,256]{1,0:T(8,128)(2,1)S(1)}, u32[]{:S(2)}, u32[]{:S(2)}) %collective-permute-start.15) | collective-permute-done | bytes 147488 | tf_op jit(solution)/shard_map/ppermute | solution.py:21
  54.5 0.0 collective-permute-done.16.refs_2_
  54.5 1.2 %shard_map.95.partial_ref = f32[256,1152]{1,0:T(8,128)S(1)} custom-call(s32[1]{0:T(128)} %bitcast.1.core_ref, bf16[288,256]{1,0:T(8,128)(2,1)S(1)} %get-tuple-element.81.refs_0_, bf16[288,256]{1,0:T(8,128)(2,1)S(1)} %collective-permute-done.15.refs_1_, bf16[288,256]{1,0:T(8,128)(2,1)S(1)} %collective-permute-done.16.refs_2_, ...), custom_call_target="tpu_custom_call" | custom-call | flops 10000000000 | bytes 1048576 | tf_op jit(solution)/shard_map/pallas_call | solution.py:337
  55.7 1.4 %collective-permute-done.17.refs_0_ = bf16[288,256]{1,0:T(8,128)(2,1)S(1)} collective-permute-done((bf16[288,256]{1,0:T(8,128)(2,1)S(1)}, bf16[288,256]{1,0:T(8,128)(2,1)S(1)}, u32[]{:S(2)}, u32[]{:S(2)}) %collective-permute-start.17) | collective-permute-done | bytes 147488 | tf_op jit(solution)/shard_map/ppermute | solution.py:21
  57.2 0.0 collective-permute-done.19.refs_2_
  57.2 0.6 shard_map.96
  57.8 3.3 %collective-permute-start.24 = (bf16[64,1152]{1,0:T(8,128)(2,1)S(1)}, bf16[64,1152]{1,0:T(8,128)(2,1)S(1)}, u32[]{:S(2)}, u32[]{:S(2)}) collective-permute-start(bf16[64,1152]{1,0:T(8,128)(2,1)S(1)} %get-tuple-element.95), channel_id=1, source_target_pairs={{0,8},{4,12},{8,0},{12,4},{16,24},{20,28},{24,16},{28,20},{1,9},{5... | collective-permute-start | bytes 442376 | tf_op jit(solution)/shard_map/ppermute | solution.py:21
  61.1 1.4 %collective-permute-start.20 = (bf16[32,1152]{1,0:T(8,128)(2,1)S(1)}, bf16[32,1152]{1,0:T(8,128)(2,1)S(1)}, u32[]{:S(2)}, u32[]{:S(2)}) collective-permute-start(bf16[32,1152]{1,0:T(8,128)(2,1)S(1)} %get-tuple-element.90), channel_id=1, source_target_pairs={{0,16},{4,20},{8,24},{12,28},{16,0},{20,4},{24,8},{28,12},{1,17},{... | collective-permute-start | bytes 221192 | tf_op jit(solution)/shard_map/ppermute | solution.py:21
  62.5 0.0 collective-permute-start.21
  62.5 1.4 %collective-permute-start.22 = (bf16[32,1152]{1,0:T(8,128)(2,1)S(1)}, bf16[32,1152]{1,0:T(8,128)(2,1)S(1)}, u32[]{:S(2)}, u32[]{:S(2)}) collective-permute-start(bf16[32,1152]{1,0:T(8,128)(2,1)S(1)} %get-tuple-element.92), channel_id=1, source_target_pairs={{0,24},{4,28},{8,16},{12,20},{16,8},{20,12},{24,0},{28,4},{1,25},{... | collective-permute-start | bytes 221192 | tf_op jit(solution)/shard_map/ppermute | solution.py:21
  63.9 3.4 %collective-permute-start.23 = (bf16[32,1152]{1,0:T(8,128)(2,1)S(1)}, bf16[32,1152]{1,0:T(8,128)(2,1)S(1)}, u32[]{:S(2)}, u32[]{:S(2)}) collective-permute-start(bf16[32,1152]{1,0:T(8,128)(2,1)S(1)} %get-tuple-element.93), channel_id=1, source_target_pairs={{0,28},{4,24},{8,20},{12,16},{16,12},{20,8},{24,4},{28,0},{1,29},{... | collective-permute-start | bytes 221192 | tf_op jit(solution)/shard_map/ppermute | solution.py:21
  67.3 0.0 collective-permute-done.24.refs_0_.refs_3_
  67.3 0.1 collective-permute-start.25
  67.4 6.1 %collective-permute-done.21.refs_1_ = bf16[32,1152]{1,0:T(8,128)(2,1)S(1)} collective-permute-done((bf16[32,1152]{1,0:T(8,128)(2,1)S(1)}, bf16[32,1152]{1,0:T(8,128)(2,1)S(1)}, u32[]{:S(2)}, u32[]{:S(2)}) %collective-permute-start.21) | collective-permute-done | bytes 73760 | tf_op jit(solution)/shard_map/ppermute | solution.py:21
  73.5 0.0 collective-permute-done.22.refs_2_
  73.5 0.0 collective-permute-done.23.refs_3_
  73.5 1.5 %shard_map.99 = bf16[1,64,4,1152]{3,2,1,0:T(4,128)(2,1)} custom-call(s32[64]{0:T(128)S(1)} %copy-done.7, bf16[128,1152]{1,0:T(8,128)(2,1)S(1)} %shard_map.97.refs_0_, bf16[64,1152]{1,0:T(8,128)(2,1)S(1)} %collective-permute-done.25.refs_1_, bf16[32,1152]{1,0:T(8,128)(2,1)S(1)} %get-tuple-element.96.refs_2_, ...), custom_call_target="tpu_custom_call" | custom-call | flops 1000000000 | bytes 1048576 | tf_op jit(solution)/shard_map/pallas_call | solution.py:337
  (22 shorter events, 0.1 us)
Async XLA Ops:
  0.0 2.7 %copy-start.4 = (bf16[288,1152]{1,0:T(8,128)(2,1)S(1)}, bf16[288,1152]{1,0:T(8,128)(2,1)}, u32[]{:S(2)}) copy-start(bf16[288,1152]{1,0:T(8,128)(2,1)} %refs_3_.1) | copy-start | bytes 1990660
  2.1 4.8 %collective-permute-start = (bf16[128,1152]{1,0:T(8,128)(2,1)}, bf16[128,1152]{1,0:T(8,128)(2,1)S(1)}, u32[]{:S(2)}, u32[]{:S(2)}) collective-permute-start(bf16[128,1152]{1,0:T(8,128)(2,1)} %get-tuple-element.53), channel_id=1, source_target_pairs={{0,4},{4,0},{8,12},{12,8},{16,20},{20,16},{24,28},{28,24},{1,5},{5... | collective-permute-start | bytes 884744 | tf_op jit(solution)/shard_map/ppermute | solution.py:21
  2.7 4.2 %copy-start.6 = (bf16[128,1152]{1,0:T(8,128)(2,1)S(1)}, bf16[128,1152]{1,0:T(8,128)(2,1)}, u32[]{:S(2)}) copy-start(bf16[128,1152]{1,0:T(8,128)(2,1)} %get-tuple-element.52.own_hbm) | copy-start | bytes 884740
  2.8 12.7 %collective-permute-start.4 = (bf16[144,1152]{1,0:T(8,128)(2,1)S(1)}, bf16[144,1152]{1,0:T(8,128)(2,1)S(1)}, u32[]{:S(2)}, u32[]{:S(2)}) collective-permute-start(bf16[144,1152]{1,0:T(8,128)(2,1)S(1)} %shard_map.86), channel_id=1, source_target_pairs={{0,1},{1,0},{2,3},{3,2},{4,5},{5,4},{6,7},{7,6},{8,9},{9,8},{10,11... | collective-permute-start | bytes 995336 | tf_op jit(solution)/shard_map/ppermute | solution.py:21
  5.4 10.1 %collective-permute-start.5 = (bf16[144,1152]{1,0:T(8,128)(2,1)S(1)}, bf16[144,1152]{1,0:T(8,128)(2,1)S(1)}, u32[]{:S(2)}, u32[]{:S(2)}) collective-permute-start(bf16[144,1152]{1,0:T(8,128)(2,1)S(1)} %shard_map.86), channel_id=1, source_target_pairs={{0,2},{1,3},{2,0},{3,1},{4,6},{5,7},{6,4},{7,5},{8,10},{9,11},{10,... | collective-permute-start | bytes 995336 | tf_op jit(solution)/shard_map/ppermute | solution.py:21
  6.9 8.0 %copy-start.1 = (s32[1,4,16]{2,1,0:T(4,128)S(1)}, s32[1,4,16]{2,1,0:T(4,128)}, u32[]{:S(2)}) copy-start(s32[1,4,16]{2,1,0:T(4,128)} %table_ref.11) | copy-start | bytes 772
  6.9 8.0 %copy-start.5 = (bf16[1,4,3,1152]{3,1,2,0:T(4,128)(2,1)S(1)}, bf16[1,4,3,1152]{3,1,2,0:T(4,128)(2,1)}, u32[]{:S(2)}) copy-start(bf16[1,4,3,1152]{3,1,2,0:T(4,128)(2,1)} %param.12) | copy-start | bytes 82948
  7.0 7.9 %collective-permute-start.3 = (bf16[64,1152]{1,0:T(8,128)(2,1)S(1)}, bf16[64,1152]{1,0:T(8,128)(2,1)S(1)}, u32[]{:S(2)}, u32[]{:S(2)}) collective-permute-start(bf16[64,1152]{1,0:T(8,128)(2,1)S(1)} %get-tuple-element.57), channel_id=1, source_target_pairs={{0,8},{4,12},{8,0},{12,4},{16,24},{20,28},{24,16},{28,20},{1,9},{5... | collective-permute-start | bytes 442376 | tf_op jit(solution)/shard_map/ppermute | solution.py:21
  8.7 14.0 %collective-permute-start.1 = (bf16[64,1152]{1,0:T(8,128)(2,1)S(1)}, bf16[64,1152]{1,0:T(8,128)(2,1)S(1)}, u32[]{:S(2)}, u32[]{:S(2)}) collective-permute-start(bf16[64,1152]{1,0:T(8,128)(2,1)S(1)} %get-tuple-element.54), channel_id=1, source_target_pairs={{0,16},{4,20},{8,24},{12,28},{16,0},{20,4},{24,8},{28,12},{1,17},{... | collective-permute-start | bytes 442376 | tf_op jit(solution)/shard_map/ppermute | solution.py:21
  11.3 11.4 %collective-permute-start.2 = (bf16[64,1152]{1,0:T(8,128)(2,1)S(1)}, bf16[64,1152]{1,0:T(8,128)(2,1)S(1)}, u32[]{:S(2)}, u32[]{:S(2)}) collective-permute-start(bf16[64,1152]{1,0:T(8,128)(2,1)S(1)} %get-tuple-element.55), channel_id=1, source_target_pairs={{0,24},{4,28},{8,16},{12,20},{16,8},{20,12},{24,0},{28,4},{1,25},{... | collective-permute-start | bytes 442376 | tf_op jit(solution)/shard_map/ppermute | solution.py:21
  15.5 8.1 %collective-permute-start.6 = (bf16[128,1152]{1,0:T(8,128)(2,1)S(1)}, bf16[128,1152]{1,0:T(8,128)(2,1)S(1)}, u32[]{:S(2)}, u32[]{:S(2)}) collective-permute-start(bf16[128,1152]{1,0:T(8,128)(2,1)S(1)} %shard_map.85.refs_0_), channel_id=1, source_target_pairs={{0,1},{1,0},{2,3},{3,2},{4,5},{5,4},{6,7},{7,6},{8,9},{9,8},{10,11... | collective-permute-start | bytes 884744 | tf_op jit(solution)/shard_map/ppermute | solution.py:21
  16.1 7.9 %collective-permute-start.7 = (bf16[128,1152]{1,0:T(8,128)(2,1)S(1)}, bf16[128,1152]{1,0:T(8,128)(2,1)S(1)}, u32[]{:S(2)}, u32[]{:S(2)}) collective-permute-start(bf16[128,1152]{1,0:T(8,128)(2,1)S(1)} %shard_map.85.refs_0_), channel_id=1, source_target_pairs={{0,2},{1,3},{2,0},{3,1},{4,6},{5,7},{6,4},{7,5},{8,10},{9,11},{10,... | collective-permute-start | bytes 884744 | tf_op jit(solution)/shard_map/ppermute | solution.py:21
  23.2 3.7 %copy-start.3 = (s32[1,4]{1,0:T(1,128)S(1)}, s32[1,4]{1,0:T(1,128)}, u32[]{:S(2)}) copy-start(s32[1,4]{1,0:T(1,128)} %length_ref.3) | copy-start | bytes 52
  24.0 7.8 %collective-permute-start.10 = (bf16[64,1152]{1,0:T(8,128)(2,1)S(1)}, bf16[64,1152]{1,0:T(8,128)(2,1)S(1)}, u32[]{:S(2)}, u32[]{:S(2)}) collective-permute-start(bf16[64,1152]{1,0:T(8,128)(2,1)S(1)} %get-tuple-element.63), channel_id=1, source_target_pairs={{0,2},{1,3},{2,0},{3,1},{4,6},{5,7},{6,4},{7,5},{8,10},{9,11},{10,... | collective-permute-start | bytes 442376 | tf_op jit(solution)/shard_map/ppermute | solution.py:21
  25.5 6.7 %copy-start = (bf16[1152,3,288]{0,2,1:T(8,128)(2,1)S(1)}, bf16[1152,3,288]{0,2,1:T(8,128)(2,1)}, u32[]{:S(2)}) copy-start(bf16[1152,3,288]{0,2,1:T(8,128)(2,1)} %param.13) | copy-start | bytes 5971972
  25.5 6.7 %copy-start.2 = (f32[2,72]{1,0:T(2,128)S(1)}, f32[2,72]{1,0:T(2,128)}, u32[]{:S(2)}) copy-start(f32[2,72]{1,0:T(2,128)} %gain_ref.5) | copy-start | bytes 1732
  25.5 6.7 %collective-permute-start.9 = (bf16[64,1152]{1,0:T(8,128)(2,1)S(1)}, bf16[64,1152]{1,0:T(8,128)(2,1)S(1)}, u32[]{:S(2)}, u32[]{:S(2)}) collective-permute-start(bf16[64,1152]{1,0:T(8,128)(2,1)S(1)} %get-tuple-element.62), channel_id=1, source_target_pairs={{0,1},{1,0},{2,3},{3,2},{4,5},{5,4},{6,7},{7,6},{8,9},{9,8},{10,11... | collective-permute-start | bytes 442376 | tf_op jit(solution)/shard_map/ppermute | solution.py:21
  28.2 10.3 %collective-permute-start.8 = (bf16[128,1152]{1,0:T(8,128)(2,1)S(1)}, bf16[128,1152]{1,0:T(8,128)(2,1)S(1)}, u32[]{:S(2)}, u32[]{:S(2)}) collective-permute-start(bf16[128,1152]{1,0:T(8,128)(2,1)S(1)} %shard_map.84.refs_0_), channel_id=1, source_target_pairs={{0,1},{1,0},{2,3},{3,2},{4,5},{5,4},{6,7},{7,6},{8,9},{9,8},{10,11... | collective-permute-start | bytes 884744 | tf_op jit(solution)/shard_map/ppermute | solution.py:21
  28.8 13.4 %collective-permute-start.11 = (bf16[128,1152]{1,0:T(8,128)(2,1)S(1)}, bf16[128,1152]{1,0:T(8,128)(2,1)S(1)}, u32[]{:S(2)}, u32[]{:S(2)}) collective-permute-start(bf16[128,1152]{1,0:T(8,128)(2,1)S(1)} %shard_map.84.refs_0_), channel_id=1, source_target_pairs={{0,2},{1,3},{2,0},{3,1},{4,6},{5,7},{6,4},{7,5},{8,10},{9,11},{10,... | collective-permute-start | bytes 884744 | tf_op jit(solution)/shard_map/ppermute | solution.py:21
  29.4 14.7 %collective-permute-start.12 = (bf16[128,1152]{1,0:T(8,128)(2,1)S(1)}, bf16[128,1152]{1,0:T(8,128)(2,1)S(1)}, u32[]{:S(2)}, u32[]{:S(2)}) collective-permute-start(bf16[128,1152]{1,0:T(8,128)(2,1)S(1)} %shard_map.84.refs_0_), channel_id=1, source_target_pairs={{0,3},{1,2},{2,1},{3,0},{4,7},{5,6},{6,5},{7,4},{8,11},{9,10},{10,... | collective-permute-start | bytes 884744 | tf_op jit(solution)/shard_map/ppermute | solution.py:21
  35.3 9.6 %collective-permute-start.13 = (bf16[144,1152]{1,0:T(8,128)(2,1)S(1)}, bf16[144,1152]{1,0:T(8,128)(2,1)S(1)}, u32[]{:S(2)}, u32[]{:S(2)}) collective-permute-start(bf16[144,1152]{1,0:T(8,128)(2,1)S(1)} %collective-permute-done.4.refs_4_), channel_id=1, source_target_pairs={{0,4},{4,0},{8,12},{12,8},{16,20},{20,16},{24,28},{28,24},{1,5},{5... | collective-permute-start | bytes 995336 | tf_op jit(solution)/shard_map/ppermute | solution.py:21
  35.4 9.5 %collective-permute-start.14 = (bf16[144,1152]{1,0:T(8,128)(2,1)S(1)}, bf16[144,1152]{1,0:T(8,128)(2,1)S(1)}, u32[]{:S(2)}, u32[]{:S(2)}) collective-permute-start(bf16[144,1152]{1,0:T(8,128)(2,1)S(1)} %collective-permute-done.5.refs_6_), channel_id=1, source_target_pairs={{0,4},{4,0},{8,12},{12,8},{16,20},{20,16},{24,28},{28,24},{1,5},{5... | collective-permute-start | bytes 995336 | tf_op jit(solution)/shard_map/ppermute | solution.py:21
  40.6 12.1 %collective-permute-start.18 = (bf16[144,1152]{1,0:T(8,128)(2,1)S(1)}, bf16[144,1152]{1,0:T(8,128)(2,1)S(1)}, u32[]{:S(2)}, u32[]{:S(2)}) collective-permute-start(bf16[144,1152]{1,0:T(8,128)(2,1)S(1)} %collective-permute-done.5.refs_6_), channel_id=1, source_target_pairs={{0,1},{1,0},{2,3},{3,2},{4,5},{5,4},{6,7},{7,6},{8,9},{9,8},{10,11... | collective-permute-start | bytes 995336 | tf_op jit(solution)/shard_map/ppermute | solution.py:21
  49.1 5.4 %collective-permute-start.15 = (bf16[288,256]{1,0:T(8,128)(2,1)S(1)}, bf16[288,256]{1,0:T(8,128)(2,1)S(1)}, u32[]{:S(2)}, u32[]{:S(2)}) collective-permute-start(bf16[288,256]{1,0:T(8,128)(2,1)S(1)} %get-tuple-element.82), channel_id=1, source_target_pairs={{0,1},{1,0},{2,3},{3,2},{4,5},{5,4},{6,7},{7,6},{8,9},{9,8},{10,11... | collective-permute-start | bytes 442376 | tf_op jit(solution)/shard_map/ppermute | solution.py:21
  49.2 5.4 %collective-permute-start.16 = (bf16[288,256]{1,0:T(8,128)(2,1)S(1)}, bf16[288,256]{1,0:T(8,128)(2,1)S(1)}, u32[]{:S(2)}, u32[]{:S(2)}) collective-permute-start(bf16[288,256]{1,0:T(8,128)(2,1)S(1)} %get-tuple-element.83), channel_id=1, source_target_pairs={{0,2},{1,3},{2,0},{3,1},{4,6},{5,7},{6,4},{7,5},{8,10},{9,11},{10,... | collective-permute-start | bytes 442376 | tf_op jit(solution)/shard_map/ppermute | solution.py:21
  51.1 6.1 %collective-permute-start.17 = (bf16[288,256]{1,0:T(8,128)(2,1)S(1)}, bf16[288,256]{1,0:T(8,128)(2,1)S(1)}, u32[]{:S(2)}, u32[]{:S(2)}) collective-permute-start(bf16[288,256]{1,0:T(8,128)(2,1)S(1)} %get-tuple-element.88), channel_id=1, source_target_pairs={{0,3},{1,2},{2,1},{3,0},{4,7},{5,6},{6,5},{7,4},{8,11},{9,10},{10,... | collective-permute-start | bytes 442376 | tf_op jit(solution)/shard_map/ppermute | solution.py:21
  52.6 4.5 %collective-permute-start.19 = (bf16[144,1152]{1,0:T(8,128)(2,1)S(1)}, bf16[144,1152]{1,0:T(8,128)(2,1)S(1)}, u32[]{:S(2)}, u32[]{:S(2)}) collective-permute-start(bf16[144,1152]{1,0:T(8,128)(2,1)S(1)} %collective-permute-done.18.refs_1_), channel_id=1, source_target_pairs={{0,4},{4,0},{8,12},{12,8},{16,20},{20,16},{24,28},{28,24},{1,5},{5... | collective-permute-start | bytes 995336 | tf_op jit(solution)/shard_map/ppermute | solution.py:21
  57.8 9.5 %collective-permute-start.24 = (bf16[64,1152]{1,0:T(8,128)(2,1)S(1)}, bf16[64,1152]{1,0:T(8,128)(2,1)S(1)}, u32[]{:S(2)}, u32[]{:S(2)}) collective-permute-start(bf16[64,1152]{1,0:T(8,128)(2,1)S(1)} %get-tuple-element.95), channel_id=1, source_target_pairs={{0,8},{4,12},{8,0},{12,4},{16,24},{20,28},{24,16},{28,20},{1,9},{5... | collective-permute-start | bytes 442376 | tf_op jit(solution)/shard_map/ppermute | solution.py:21
  61.1 6.3 %collective-permute-start.20 = (bf16[32,1152]{1,0:T(8,128)(2,1)S(1)}, bf16[32,1152]{1,0:T(8,128)(2,1)S(1)}, u32[]{:S(2)}, u32[]{:S(2)}) collective-permute-start(bf16[32,1152]{1,0:T(8,128)(2,1)S(1)} %get-tuple-element.90), channel_id=1, source_target_pairs={{0,16},{4,20},{8,24},{12,28},{16,0},{20,4},{24,8},{28,12},{1,17},{... | collective-permute-start | bytes 221192 | tf_op jit(solution)/shard_map/ppermute | solution.py:21
  62.5 11.0 %collective-permute-start.21 = (bf16[32,1152]{1,0:T(8,128)(2,1)S(1)}, bf16[32,1152]{1,0:T(8,128)(2,1)S(1)}, u32[]{:S(2)}, u32[]{:S(2)}) collective-permute-start(bf16[32,1152]{1,0:T(8,128)(2,1)S(1)} %get-tuple-element.91), channel_id=1, source_target_pairs={{0,20},{4,16},{8,28},{12,24},{16,4},{20,0},{24,12},{28,8},{1,21},{... | collective-permute-start | bytes 221192 | tf_op jit(solution)/shard_map/ppermute | solution.py:21
  62.5 11.0 %collective-permute-start.22 = (bf16[32,1152]{1,0:T(8,128)(2,1)S(1)}, bf16[32,1152]{1,0:T(8,128)(2,1)S(1)}, u32[]{:S(2)}, u32[]{:S(2)}) collective-permute-start(bf16[32,1152]{1,0:T(8,128)(2,1)S(1)} %get-tuple-element.92), channel_id=1, source_target_pairs={{0,24},{4,28},{8,16},{12,20},{16,8},{20,12},{24,0},{28,4},{1,25},{... | collective-permute-start | bytes 221192 | tf_op jit(solution)/shard_map/ppermute | solution.py:21
  63.9 9.6 %collective-permute-start.23 = (bf16[32,1152]{1,0:T(8,128)(2,1)S(1)}, bf16[32,1152]{1,0:T(8,128)(2,1)S(1)}, u32[]{:S(2)}, u32[]{:S(2)}) collective-permute-start(bf16[32,1152]{1,0:T(8,128)(2,1)S(1)} %get-tuple-element.93), channel_id=1, source_target_pairs={{0,28},{4,24},{8,20},{12,16},{16,12},{20,8},{24,4},{28,0},{1,29},{... | collective-permute-start | bytes 221192 | tf_op jit(solution)/shard_map/ppermute | solution.py:21
  67.3 6.2 %copy-start.7 = (s32[64]{0:T(128)S(1)}, s32[64]{0:T(128)}, u32[]{:S(2)}) copy-start(s32[64]{0:T(128)} %get-tuple-element.51.slot_ref) | copy-start | bytes 772
  67.3 6.2 %collective-permute-start.25 = (bf16[64,1152]{1,0:T(8,128)(2,1)S(1)}, bf16[64,1152]{1,0:T(8,128)(2,1)S(1)}, u32[]{:S(2)}, u32[]{:S(2)}) collective-permute-start(bf16[64,1152]{1,0:T(8,128)(2,1)S(1)} %shard_map.98), channel_id=1, source_target_pairs={{0,4},{4,0},{8,12},{12,8},{16,20},{20,16},{24,28},{28,24},{1,5},{5... | collective-permute-start | bytes 442376 | tf_op jit(solution)/shard_map/ppermute | solution.py:21

commit v2 on v1

--- a/solution.py
+++ b/solution.py
@@ -455,12 +455,12 @@
         return gathered
 
     gathered = gather(0, stacked_near)
-    gathered, proj_parts = lax.optimization_barrier((gathered, proj_parts))
+    gathered, proj_parts, settled = lax.optimization_barrier((gathered, proj_parts, arrived))
     early_blocks, late_blocks = far_blocks[: seq_count // 2], far_blocks[seq_count // 2 :]
     residual = call(
         functools.partial(residual_kernel, clip_tokens, codes_of(0)),
         [clip_length, owner_place, place],
-        [clip_pieces, factors] + arrived,
+        [clip_pieces, factors] + settled,
         [((rows_here, model_width), BF16)] * 2,
     )
     early_blocks, gathered, residual = lax.optimization_barrier(

time: 76.2 us -> 74.5 us (0.978)
  starting transfers between devices: 33 us -> 32.2 us
where the time goes in v2:
time: 74.5 us; the launch traced here: 73.7 us
  starting transfers between devices  32.2 us (43%)
  waiting for transfers between devices  22.9 us (31%)
  Pallas kernels  18.3 us (25%)
    ppermute x26, starting transfers between devices, send(): return lax.ppermute(array, axis, [(i, i ^ mask) for i in range(count)])  32.2 us
    ppermute x26, waiting for transfers between devices, send(): return lax.ppermute(array, axis, [(i, i ^ mask) for i in range(count)])  22.9 us
    pallas_call x18, Pallas kernels, call(): pl.pallas_call(kernel, in_specs=[smem] * len(scalars) + (where if isinsta...  18.3 us
  transfers between devices with their start and end apart: 26, of which 10 were waited for; matrix products, arithmetic and copies ran while one was open for 0% of the time, Pallas kernels for 19%

profile of v2, /device:TPU:0, one launch (start us, length us, event | category | flops | bytes accessed | tf_op | source)
XLA Modules:
  0.0 73.7 jit_solution(3495712739799708321)
XLA Ops:
  0.0 2.1 %shard_map.82 = (s32[64]{0:T(128)}, bf16[128,1152]{1,0:T(8,128)(2,1)}, bf16[128,1152]{1,0:T(8,128)(2,1)}) custom-call(s32[1]{0:T(128)} %bitcast.place_ref.owner_ref, s32[1,64]{1,0:T(1,128)} %owner_hbm.1, bf16[1,64,4,1152]{3,2,1,0:T(4,128)(2,1)} %token_hbm.1), custom_call_target="tpu_custom_call" | custom-call | flops 30000001024 | bytes 1048576 | tf_op jit(solution)/shard_map/pallas_call | solution.py:337
  2.1 0.5 collective-permute-start
  2.7 0.1 shard_map.86
  2.8 2.6 %collective-permute-start.4 = (bf16[144,1152]{1,0:T(8,128)(2,1)S(1)}, bf16[144,1152]{1,0:T(8,128)(2,1)S(1)}, u32[]{:S(2)}, u32[]{:S(2)}) collective-permute-start(bf16[144,1152]{1,0:T(8,128)(2,1)S(1)} %shard_map.86), channel_id=1, source_target_pairs={{0,1},{1,0},{2,3},{3,2},{4,5},{5,4},{6,7},{7,6},{8,9},{9,8},{10,11... | collective-permute-start | bytes 995336 | tf_op jit(solution)/shard_map/ppermute | solution.py:21
  5.4 1.5 %collective-permute-start.5 = (bf16[144,1152]{1,0:T(8,128)(2,1)S(1)}, bf16[144,1152]{1,0:T(8,128)(2,1)S(1)}, u32[]{:S(2)}, u32[]{:S(2)}) collective-permute-start(bf16[144,1152]{1,0:T(8,128)(2,1)S(1)} %shard_map.86), channel_id=1, source_target_pairs={{0,2},{1,3},{2,0},{3,1},{4,6},{5,7},{6,4},{7,5},{8,10},{9,11},{10,... | collective-permute-start | bytes 995336 | tf_op jit(solution)/shard_map/ppermute | solution.py:21
  6.9 0.0 collective-permute-done.other_ref
  6.9 0.1 shard_map.83
  7.0 1.6 %collective-permute-start.3 = (bf16[64,1152]{1,0:T(8,128)(2,1)S(1)}, bf16[64,1152]{1,0:T(8,128)(2,1)S(1)}, u32[]{:S(2)}, u32[]{:S(2)}) collective-permute-start(bf16[64,1152]{1,0:T(8,128)(2,1)S(1)} %get-tuple-element.61), channel_id=1, source_target_pairs={{0,8},{4,12},{8,0},{12,4},{16,24},{20,28},{24,16},{28,20},{1,9},{5... | collective-permute-start | bytes 442376 | tf_op jit(solution)/shard_map/ppermute | solution.py:21
  8.7 2.6 %collective-permute-start.1 = (bf16[64,1152]{1,0:T(8,128)(2,1)S(1)}, bf16[64,1152]{1,0:T(8,128)(2,1)S(1)}, u32[]{:S(2)}, u32[]{:S(2)}) collective-permute-start(bf16[64,1152]{1,0:T(8,128)(2,1)S(1)} %get-tuple-element.58), channel_id=1, source_target_pairs={{0,16},{4,20},{8,24},{12,28},{16,0},{20,4},{24,8},{28,12},{1,17},{... | collective-permute-start | bytes 442376 | tf_op jit(solution)/shard_map/ppermute | solution.py:21
  11.3 0.2 collective-permute-start.2
  11.5 3.4 %collective-permute-done.3.refs_1_ = bf16[64,1152]{1,0:T(8,128)(2,1)S(1)} collective-permute-done((bf16[64,1152]{1,0:T(8,128)(2,1)S(1)}, bf16[64,1152]{1,0:T(8,128)(2,1)S(1)}, u32[]{:S(2)}, u32[]{:S(2)}) %collective-permute-start.3) | collective-permute-done | bytes 147488 | tf_op jit(solution)/shard_map/ppermute | solution.py:21
  14.9 0.6 shard_map.85.refs_0_
  15.5 0.0 collective-permute-done.4.refs_4_
  15.5 0.0 collective-permute-done.5.refs_6_
  15.5 0.6 collective-permute-start.6
  16.1 1.5 %collective-permute-start.7 = (bf16[128,1152]{1,0:T(8,128)(2,1)S(1)}, bf16[128,1152]{1,0:T(8,128)(2,1)S(1)}, u32[]{:S(2)}, u32[]{:S(2)}) collective-permute-start(bf16[128,1152]{1,0:T(8,128)(2,1)S(1)} %shard_map.85.refs_0_), channel_id=1, source_target_pairs={{0,2},{1,3},{2,0},{3,1},{4,6},{5,7},{6,4},{7,5},{8,10},{9,11},{10,... | collective-permute-start | bytes 884744 | tf_op jit(solution)/shard_map/ppermute | solution.py:21
  17.6 5.1 %collective-permute-done.1.refs_0_.refs_2_ = bf16[64,1152]{1,0:T(8,128)(2,1)S(1)} collective-permute-done((bf16[64,1152]{1,0:T(8,128)(2,1)S(1)}, bf16[64,1152]{1,0:T(8,128)(2,1)S(1)}, u32[]{:S(2)}, u32[]{:S(2)}) %collective-permute-start.1) | collective-permute-done | bytes 147488 | tf_op jit(solution)/shard_map/ppermute | solution.py:21
  22.7 0.6 shard_map.84.refs_0_
  23.2 0.0 copy-start
  23.2 0.0 copy-start.2
  23.3 0.3 collective-permute-done.6.refs_1_
  23.6 0.4 collective-permute-done.7.refs_0_.refs_2_
  24.0 1.5 %collective-permute-start.10 = (bf16[64,1152]{1,0:T(8,128)(2,1)S(1)}, bf16[64,1152]{1,0:T(8,128)(2,1)S(1)}, u32[]{:S(2)}, u32[]{:S(2)}) collective-permute-start(bf16[64,1152]{1,0:T(8,128)(2,1)S(1)} %get-tuple-element.67), channel_id=1, source_target_pairs={{0,2},{1,3},{2,0},{3,1},{4,6},{5,7},{6,4},{7,5},{8,10},{9,11},{10,... | collective-permute-start | bytes 442376 | tf_op jit(solution)/shard_map/ppermute | solution.py:21
  25.5 1.4 %collective-permute-start.9 = (bf16[64,1152]{1,0:T(8,128)(2,1)S(1)}, bf16[64,1152]{1,0:T(8,128)(2,1)S(1)}, u32[]{:S(2)}, u32[]{:S(2)}) collective-permute-start(bf16[64,1152]{1,0:T(8,128)(2,1)S(1)} %get-tuple-element.66), channel_id=1, source_target_pairs={{0,1},{1,0},{2,3},{3,2},{4,5},{5,4},{6,7},{7,6},{8,9},{9,8},{10,11... | collective-permute-start | bytes 442376 | tf_op jit(solution)/shard_map/ppermute | solution.py:21
  26.9 0.6 collective-permute-start.8
  27.5 0.6 collective-permute-start.11
  28.1 2.3 %collective-permute-start.12 = (bf16[128,1152]{1,0:T(8,128)(2,1)S(1)}, bf16[128,1152]{1,0:T(8,128)(2,1)S(1)}, u32[]{:S(2)}, u32[]{:S(2)}) collective-permute-start(bf16[128,1152]{1,0:T(8,128)(2,1)S(1)} %shard_map.84.refs_0_), channel_id=1, source_target_pairs={{0,3},{1,2},{2,1},{3,0},{4,7},{5,6},{6,5},{7,4},{8,11},{9,10},{10,... | collective-permute-start | bytes 884744 | tf_op jit(solution)/shard_map/ppermute | solution.py:21
  30.4 0.4 collective-permute-done.10.refs_4_
  30.8 1.5 %collective-permute-done.9.refs_3_ = bf16[64,1152]{1,0:T(8,128)(2,1)S(1)} collective-permute-done((bf16[64,1152]{1,0:T(8,128)(2,1)S(1)}, bf16[64,1152]{1,0:T(8,128)(2,1)S(1)}, u32[]{:S(2)}, u32[]{:S(2)}) %collective-permute-start.9) | collective-permute-done | bytes 147488 | tf_op jit(solution)/shard_map/ppermute | solution.py:21
  32.3 1.4 %shard_map.88.stacked_ref = bf16[864,512]{1,0:T(8,128)(2,1)S(1)} custom-call(bf16[864,1152]{1,0:T(8,128)(2,1)S(1)} %bitcast.9, f32[2,72]{1,0:T(2,128)S(1)} %copy-done.2, bf16[128,1152]{1,0:T(8,128)(2,1)S(1)} %shard_map.85.refs_0_, bf16[128,1152]{1,0:T(8,128)(2,1)S(1)} %collective-permute-done.6.refs_1_, ...), custom_call_target="tpu_custom_call" | custom-call | flops 3000000000 | bytes 1048576 | tf_op jit(solution)/shard_map/pallas_call | solution.py:337
  33.7 0.0 copy-start.3
  33.7 1.8 %shard_map.89.refs_0_ = bf16[4,864,256]{2,1,0:T(8,128)(2,1)S(1)} custom-call(s32[1]{0:T(128)} %bitcast.place_ref.owner_ref, s32[1]{0:T(128)} %bitcast.2.place_ref, s32[1,4,16]{2,1,0:T(4,128)S(1)} %copy-done.1, bf16[864,512]{1,0:T(8,128)(2,1)S(1)} %shard_map.88.stacked_ref), custom_call_target="tpu_custom_call" | custom-call | flops 3000000000 | bytes 1048576 | tf_op jit(solution)/shard_map/pallas_call | solution.py:337
  35.4 0.1 collective-permute-start.13
  35.5 0.5 collective-permute-start.14
  36.0 1.3 %shard_map.90 = (bf16[256,1152]{1,0:T(8,128)(2,1)S(1)}, bf16[256,1152]{1,0:T(8,128)(2,1)S(1)}) custom-call(s32[1,4]{1,0:T(1,128)S(1)} %copy-done.3, s32[1]{0:T(128)} %bitcast.place_ref.owner_ref, s32[1]{0:T(128)} %bitcast.2.place_ref, s32[1,4,16]{2,1,0:T(4,128)S(1)} %copy-done.1, bf16[3,4,1152]{2,1,0:T(4,128)(2,1)S(1)} %bitcast.14, ...), custom_call_target="tpu_custom_call" | custom-call | flops 1000000000 | bytes 1048576 | tf_op jit(solution)/shard_map/pallas_call | solution.py:337
  37.3 1.3 %collective-permute-done.8.refs_1_ = bf16[128,1152]{1,0:T(8,128)(2,1)S(1)} collective-permute-done((bf16[128,1152]{1,0:T(8,128)(2,1)S(1)}, bf16[128,1152]{1,0:T(8,128)(2,1)S(1)}, u32[]{:S(2)}, u32[]{:S(2)}) %collective-permute-start.8) | collective-permute-done | bytes 294944 | tf_op jit(solution)/shard_map/ppermute | solution.py:21
  38.6 0.8 %shard_map.91.stacked_ref = bf16[864,256]{1,0:T(8,128)(2,1)S(1)} custom-call(bf16[864,1152]{1,0:T(8,128)(2,1)S(1)} %bitcast.10, f32[2,72]{1,0:T(2,128)S(1)} %copy-done.2, bf16[128,1152]{1,0:T(8,128)(2,1)S(1)} %shard_map.84.refs_0_, bf16[128,1152]{1,0:T(8,128)(2,1)S(1)} %collective-permute-done.8.refs_1_), custom_call_target="tpu_custom_call" | custom-call | flops 3000000000 | bytes 1048576 | tf_op jit(solution)/shard_map/pallas_call | solution.py:337
  39.3 1.3 %shard_map.92.refs_0_ = bf16[4,864,256]{2,1,0:T(8,128)(2,1)S(1)} custom-call(s32[1]{0:T(128)} %bitcast.place_ref.owner_ref, s32[1]{0:T(128)} %bitcast.2.place_ref, s32[1,4,16]{2,1,0:T(4,128)S(1)} %copy-done.1, bf16[864,256]{1,0:T(8,128)(2,1)S(1)} %shard_map.91.stacked_ref, bf16[4,864,256]{2,1,0:T(8,128)(2,1)S(1)} %shard_map.89.refs_0_), custom_call_target="tpu_custom_call" | custom-call | flops 3000000000 | bytes 1048576 | tf_op jit(solution)/shard_map/pallas_call | solution.py:337
  40.7 1.5 %collective-permute-start.18 = (bf16[144,1152]{1,0:T(8,128)(2,1)S(1)}, bf16[144,1152]{1,0:T(8,128)(2,1)S(1)}, u32[]{:S(2)}, u32[]{:S(2)}) collective-permute-start(bf16[144,1152]{1,0:T(8,128)(2,1)S(1)} %collective-permute-done.5.refs_6_), channel_id=1, source_target_pairs={{0,1},{1,0},{2,3},{3,2},{4,5},{5,4},{6,7},{7,6},{8,9},{9,8},{10,11... | collective-permute-start | bytes 995336 | tf_op jit(solution)/shard_map/ppermute | solution.py:21
  42.2 0.0 collective-permute-done.11.refs_0_
  42.2 0.0 collective-permute-done.12.refs_1_
  42.2 0.8 %shard_map.93.refs_1_ = bf16[864,256]{1,0:T(8,128)(2,1)S(1)} custom-call(bf16[864,1152]{1,0:T(8,128)(2,1)S(1)} %bitcast.11, f32[2,72]{1,0:T(2,128)S(1)} %copy-done.2, bf16[128,1152]{1,0:T(8,128)(2,1)S(1)} %collective-permute-done.11.refs_0_, bf16[128,1152]{1,0:T(8,128)(2,1)S(1)} %collective-permute-done.12.refs_1_), custom_call_target="tpu_custom_call" | custom-call | flops 100000000 | bytes 1048576 | tf_op jit(solution)/shard_map/pallas_call | solution.py:337
  43.0 0.0 collective-permute-done.13.refs_5_
  43.0 4.2 %shard_map.94 = (bf16[288,256]{1,0:T(8,128)(2,1)S(1)}, bf16[288,256]{1,0:T(8,128)(2,1)S(1)}, bf16[288,256]{1,0:T(8,128)(2,1)S(1)}, bf16[288,256]{1,0:T(8,128)(2,1)S(1)}) custom-call(s32[1,4]{1,0:T(1,128)S(1)} %copy-done.3, s32[1]{0:T(128)} %bitcast.place_ref.owner_ref, s32[1]{0:T(128)} %bitcast.2.place_ref, s32[1,4,16]{2,1,0:T(4,128)S(1)} %copy-done.1, ...), custom_call_target="tpu_custom_call" | custom-call | flops 100000000 | bytes 1048576 | tf_op jit(solution)/shard_map/pallas_call | solution.py:337
  47.2 0.9 %collective-permute-start.15 = (bf16[288,256]{1,0:T(8,128)(2,1)S(1)}, bf16[288,256]{1,0:T(8,128)(2,1)S(1)}, u32[]{:S(2)}, u32[]{:S(2)}) collective-permute-start(bf16[288,256]{1,0:T(8,128)(2,1)S(1)} %get-tuple-element.90), channel_id=1, source_target_pairs={{0,1},{1,0},{2,3},{3,2},{4,5},{5,4},{6,7},{7,6},{8,9},{9,8},{10,11... | collective-permute-start | bytes 442376 | tf_op jit(solution)/shard_map/ppermute | solution.py:21
  48.1 1.6 %collective-permute-start.16 = (bf16[288,256]{1,0:T(8,128)(2,1)S(1)}, bf16[288,256]{1,0:T(8,128)(2,1)S(1)}, u32[]{:S(2)}, u32[]{:S(2)}) collective-permute-start(bf16[288,256]{1,0:T(8,128)(2,1)S(1)} %get-tuple-element.91), channel_id=1, source_target_pairs={{0,2},{1,3},{2,0},{3,1},{4,6},{5,7},{6,4},{7,5},{8,10},{9,11},{10,... | collective-permute-start | bytes 442376 | tf_op jit(solution)/shard_map/ppermute | solution.py:21
  49.7 1.0 %collective-permute-start.17 = (bf16[288,256]{1,0:T(8,128)(2,1)S(1)}, bf16[288,256]{1,0:T(8,128)(2,1)S(1)}, u32[]{:S(2)}, u32[]{:S(2)}) collective-permute-start(bf16[288,256]{1,0:T(8,128)(2,1)S(1)} %get-tuple-element.96), channel_id=1, source_target_pairs={{0,3},{1,2},{2,1},{3,0},{4,7},{5,6},{6,5},{7,4},{8,11},{9,10},{10,... | collective-permute-start | bytes 442376 | tf_op jit(solution)/shard_map/ppermute | solution.py:21
  50.7 0.0 collective-permute-done.18.refs_1_
  50.7 0.0 collective-permute-start.19
  50.8 3.2 %collective-permute-done.15.refs_1_ = bf16[288,256]{1,0:T(8,128)(2,1)S(1)} collective-permute-done((bf16[288,256]{1,0:T(8,128)(2,1)S(1)}, bf16[288,256]{1,0:T(8,128)(2,1)S(1)}, u32[]{:S(2)}, u32[]{:S(2)}) %collective-permute-start.15) | collective-permute-done | bytes 147488 | tf_op jit(solution)/shard_map/ppermute | solution.py:21
  54.0 1.1 %collective-permute-done.16.refs_2_ = bf16[288,256]{1,0:T(8,128)(2,1)S(1)} collective-permute-done((bf16[288,256]{1,0:T(8,128)(2,1)S(1)}, bf16[288,256]{1,0:T(8,128)(2,1)S(1)}, u32[]{:S(2)}, u32[]{:S(2)}) %collective-permute-start.16) | collective-permute-done | bytes 147488 | tf_op jit(solution)/shard_map/ppermute | solution.py:21
  55.0 1.2 %shard_map.95.partial_ref = f32[256,1152]{1,0:T(8,128)S(1)} custom-call(s32[1]{0:T(128)} %bitcast.1.core_ref, bf16[288,256]{1,0:T(8,128)(2,1)S(1)} %get-tuple-element.89.refs_0_, bf16[288,256]{1,0:T(8,128)(2,1)S(1)} %collective-permute-done.15.refs_1_, bf16[288,256]{1,0:T(8,128)(2,1)S(1)} %collective-permute-done.16.refs_2_, ...), custom_call_target="tpu_custom_call" | custom-call | flops 10000000000 | bytes 1048576 | tf_op jit(solution)/shard_map/pallas_call | solution.py:337
  56.3 0.0 collective-permute-done.19.refs_2_
  56.3 0.6 shard_map.96
  56.9 2.7 %collective-permute-start.24 = (bf16[64,1152]{1,0:T(8,128)(2,1)S(1)}, bf16[64,1152]{1,0:T(8,128)(2,1)S(1)}, u32[]{:S(2)}, u32[]{:S(2)}) collective-permute-start(bf16[64,1152]{1,0:T(8,128)(2,1)S(1)} %get-tuple-element.103), channel_id=1, source_target_pairs={{0,8},{4,12},{8,0},{12,4},{16,24},{20,28},{24,16},{28,20},{1,9},{5... | collective-permute-start | bytes 442376 | tf_op jit(solution)/shard_map/ppermute | solution.py:21
  59.6 1.5 %collective-permute-start.20 = (bf16[32,1152]{1,0:T(8,128)(2,1)S(1)}, bf16[32,1152]{1,0:T(8,128)(2,1)S(1)}, u32[]{:S(2)}, u32[]{:S(2)}) collective-permute-start(bf16[32,1152]{1,0:T(8,128)(2,1)S(1)} %get-tuple-element.98), channel_id=1, source_target_pairs={{0,16},{4,20},{8,24},{12,28},{16,0},{20,4},{24,8},{28,12},{1,17},{... | collective-permute-start | bytes 221192 | tf_op jit(solution)/shard_map/ppermute | solution.py:21
  61.2 0.0 collective-permute-start.21
  61.2 1.1 %collective-permute-start.22 = (bf16[32,1152]{1,0:T(8,128)(2,1)S(1)}, bf16[32,1152]{1,0:T(8,128)(2,1)S(1)}, u32[]{:S(2)}, u32[]{:S(2)}) collective-permute-start(bf16[32,1152]{1,0:T(8,128)(2,1)S(1)} %get-tuple-element.100), channel_id=1, source_target_pairs={{0,24},{4,28},{8,16},{12,20},{16,8},{20,12},{24,0},{28,4},{1,25},{... | collective-permute-start | bytes 221192 | tf_op jit(solution)/shard_map/ppermute | solution.py:21
  62.3 3.5 %collective-permute-start.23 = (bf16[32,1152]{1,0:T(8,128)(2,1)S(1)}, bf16[32,1152]{1,0:T(8,128)(2,1)S(1)}, u32[]{:S(2)}, u32[]{:S(2)}) collective-permute-start(bf16[32,1152]{1,0:T(8,128)(2,1)S(1)} %get-tuple-element.101), channel_id=1, source_target_pairs={{0,28},{4,24},{8,20},{12,16},{16,12},{20,8},{24,4},{28,0},{1,29},{... | collective-permute-start | bytes 221192 | tf_op jit(solution)/shard_map/ppermute | solution.py:21
  65.8 0.0 collective-permute-done.24.refs_0_.refs_3_
  65.8 0.1 collective-permute-start.25
  65.9 6.2 %collective-permute-done.21.refs_1_ = bf16[32,1152]{1,0:T(8,128)(2,1)S(1)} collective-permute-done((bf16[32,1152]{1,0:T(8,128)(2,1)S(1)}, bf16[32,1152]{1,0:T(8,128)(2,1)S(1)}, u32[]{:S(2)}, u32[]{:S(2)}) %collective-permute-start.21) | collective-permute-done | bytes 73760 | tf_op jit(solution)/shard_map/ppermute | solution.py:21
  72.2 0.0 collective-permute-done.25.refs_1_
  72.2 1.5 %shard_map.99 = bf16[1,64,4,1152]{3,2,1,0:T(4,128)(2,1)} custom-call(s32[64]{0:T(128)S(1)} %copy-done.7, bf16[128,1152]{1,0:T(8,128)(2,1)S(1)} %shard_map.97.refs_0_, bf16[64,1152]{1,0:T(8,128)(2,1)S(1)} %collective-permute-done.25.refs_1_, bf16[32,1152]{1,0:T(8,128)(2,1)S(1)} %get-tuple-element.104.refs_2_, ...), custom_call_target="tpu_custom_call" | custom-call | flops 1000000000 | bytes 1048576 | tf_op jit(solution)/shard_map/pallas_call | solution.py:337
  (22 shorter events, 0.1 us)
Async XLA Ops:
  0.0 2.7 %copy-start.4 = (bf16[288,1152]{1,0:T(8,128)(2,1)S(1)}, bf16[288,1152]{1,0:T(8,128)(2,1)}, u32[]{:S(2)}) copy-start(bf16[288,1152]{1,0:T(8,128)(2,1)} %refs_3_.1) | copy-start | bytes 1990660
  2.1 4.8 %collective-permute-start = (bf16[128,1152]{1,0:T(8,128)(2,1)}, bf16[128,1152]{1,0:T(8,128)(2,1)S(1)}, u32[]{:S(2)}, u32[]{:S(2)}) collective-permute-start(bf16[128,1152]{1,0:T(8,128)(2,1)} %get-tuple-element.57), channel_id=1, source_target_pairs={{0,4},{4,0},{8,12},{12,8},{16,20},{20,16},{24,28},{28,24},{1,5},{5... | collective-permute-start | bytes 884744 | tf_op jit(solution)/shard_map/ppermute | solution.py:21
  2.7 4.2 %copy-start.6 = (bf16[128,1152]{1,0:T(8,128)(2,1)S(1)}, bf16[128,1152]{1,0:T(8,128)(2,1)}, u32[]{:S(2)}) copy-start(bf16[128,1152]{1,0:T(8,128)(2,1)} %get-tuple-element.56.own_hbm) | copy-start | bytes 884740
  2.8 12.7 %collective-permute-start.4 = (bf16[144,1152]{1,0:T(8,128)(2,1)S(1)}, bf16[144,1152]{1,0:T(8,128)(2,1)S(1)}, u32[]{:S(2)}, u32[]{:S(2)}) collective-permute-start(bf16[144,1152]{1,0:T(8,128)(2,1)S(1)} %shard_map.86), channel_id=1, source_target_pairs={{0,1},{1,0},{2,3},{3,2},{4,5},{5,4},{6,7},{7,6},{8,9},{9,8},{10,11... | collective-permute-start | bytes 995336 | tf_op jit(solution)/shard_map/ppermute | solution.py:21
  5.4 10.1 %collective-permute-start.5 = (bf16[144,1152]{1,0:T(8,128)(2,1)S(1)}, bf16[144,1152]{1,0:T(8,128)(2,1)S(1)}, u32[]{:S(2)}, u32[]{:S(2)}) collective-permute-start(bf16[144,1152]{1,0:T(8,128)(2,1)S(1)} %shard_map.86), channel_id=1, source_target_pairs={{0,2},{1,3},{2,0},{3,1},{4,6},{5,7},{6,4},{7,5},{8,10},{9,11},{10,... | collective-permute-start | bytes 995336 | tf_op jit(solution)/shard_map/ppermute | solution.py:21
  6.9 8.0 %copy-start.1 = (s32[1,4,16]{2,1,0:T(4,128)S(1)}, s32[1,4,16]{2,1,0:T(4,128)}, u32[]{:S(2)}) copy-start(s32[1,4,16]{2,1,0:T(4,128)} %table_ref.11) | copy-start | bytes 772
  6.9 8.0 %copy-start.5 = (bf16[1,4,3,1152]{3,1,2,0:T(4,128)(2,1)S(1)}, bf16[1,4,3,1152]{3,1,2,0:T(4,128)(2,1)}, u32[]{:S(2)}) copy-start(bf16[1,4,3,1152]{3,1,2,0:T(4,128)(2,1)} %param.12) | copy-start | bytes 82948
  7.0 7.9 %collective-permute-start.3 = (bf16[64,1152]{1,0:T(8,128)(2,1)S(1)}, bf16[64,1152]{1,0:T(8,128)(2,1)S(1)}, u32[]{:S(2)}, u32[]{:S(2)}) collective-permute-start(bf16[64,1152]{1,0:T(8,128)(2,1)S(1)} %get-tuple-element.61), channel_id=1, source_target_pairs={{0,8},{4,12},{8,0},{12,4},{16,24},{20,28},{24,16},{28,20},{1,9},{5... | collective-permute-start | bytes 442376 | tf_op jit(solution)/shard_map/ppermute | solution.py:21
  8.7 14.0 %collective-permute-start.1 = (bf16[64,1152]{1,0:T(8,128)(2,1)S(1)}, bf16[64,1152]{1,0:T(8,128)(2,1)S(1)}, u32[]{:S(2)}, u32[]{:S(2)}) collective-permute-start(bf16[64,1152]{1,0:T(8,128)(2,1)S(1)} %get-tuple-element.58), channel_id=1, source_target_pairs={{0,16},{4,20},{8,24},{12,28},{16,0},{20,4},{24,8},{28,12},{1,17},{... | collective-permute-start | bytes 442376 | tf_op jit(solution)/shard_map/ppermute | solution.py:21
  11.3 11.4 %collective-permute-start.2 = (bf16[64,1152]{1,0:T(8,128)(2,1)S(1)}, bf16[64,1152]{1,0:T(8,128)(2,1)S(1)}, u32[]{:S(2)}, u32[]{:S(2)}) collective-permute-start(bf16[64,1152]{1,0:T(8,128)(2,1)S(1)} %get-tuple-element.59), channel_id=1, source_target_pairs={{0,24},{4,28},{8,16},{12,20},{16,8},{20,12},{24,0},{28,4},{1,25},{... | collective-permute-start | bytes 442376 | tf_op jit(solution)/shard_map/ppermute | solution.py:21
  15.5 8.1 %collective-permute-start.6 = (bf16[128,1152]{1,0:T(8,128)(2,1)S(1)}, bf16[128,1152]{1,0:T(8,128)(2,1)S(1)}, u32[]{:S(2)}, u32[]{:S(2)}) collective-permute-start(bf16[128,1152]{1,0:T(8,128)(2,1)S(1)} %shard_map.85.refs_0_), channel_id=1, source_target_pairs={{0,1},{1,0},{2,3},{3,2},{4,5},{5,4},{6,7},{7,6},{8,9},{9,8},{10,11... | collective-permute-start | bytes 884744 | tf_op jit(solution)/shard_map/ppermute | solution.py:21
  16.1 7.9 %collective-permute-start.7 = (bf16[128,1152]{1,0:T(8,128)(2,1)S(1)}, bf16[128,1152]{1,0:T(8,128)(2,1)S(1)}, u32[]{:S(2)}, u32[]{:S(2)}) collective-permute-start(bf16[128,1152]{1,0:T(8,128)(2,1)S(1)} %shard_map.85.refs_0_), channel_id=1, source_target_pairs={{0,2},{1,3},{2,0},{3,1},{4,6},{5,7},{6,4},{7,5},{8,10},{9,11},{10,... | collective-permute-start | bytes 884744 | tf_op jit(solution)/shard_map/ppermute | solution.py:21
  23.2 9.0 %copy-start = (bf16[1152,3,288]{0,2,1:T(8,128)(2,1)S(1)}, bf16[1152,3,288]{0,2,1:T(8,128)(2,1)}, u32[]{:S(2)}) copy-start(bf16[1152,3,288]{0,2,1:T(8,128)(2,1)} %param.13) | copy-start | bytes 5971972
  23.2 9.0 %copy-start.2 = (f32[2,72]{1,0:T(2,128)S(1)}, f32[2,72]{1,0:T(2,128)}, u32[]{:S(2)}) copy-start(f32[2,72]{1,0:T(2,128)} %gain_ref.5) | copy-start | bytes 1732
  24.0 6.8 %collective-permute-start.10 = (bf16[64,1152]{1,0:T(8,128)(2,1)S(1)}, bf16[64,1152]{1,0:T(8,128)(2,1)S(1)}, u32[]{:S(2)}, u32[]{:S(2)}) collective-permute-start(bf16[64,1152]{1,0:T(8,128)(2,1)S(1)} %get-tuple-element.67), channel_id=1, source_target_pairs={{0,2},{1,3},{2,0},{3,1},{4,6},{5,7},{6,4},{7,5},{8,10},{9,11},{10,... | collective-permute-start | bytes 442376 | tf_op jit(solution)/shard_map/ppermute | solution.py:21
  25.5 6.8 %collective-permute-start.9 = (bf16[64,1152]{1,0:T(8,128)(2,1)S(1)}, bf16[64,1152]{1,0:T(8,128)(2,1)S(1)}, u32[]{:S(2)}, u32[]{:S(2)}) collective-permute-start(bf16[64,1152]{1,0:T(8,128)(2,1)S(1)} %get-tuple-element.66), channel_id=1, source_target_pairs={{0,1},{1,0},{2,3},{3,2},{4,5},{5,4},{6,7},{7,6},{8,9},{9,8},{10,11... | collective-permute-start | bytes 442376 | tf_op jit(solution)/shard_map/ppermute | solution.py:21
  26.9 11.7 %collective-permute-start.8 = (bf16[128,1152]{1,0:T(8,128)(2,1)S(1)}, bf16[128,1152]{1,0:T(8,128)(2,1)S(1)}, u32[]{:S(2)}, u32[]{:S(2)}) collective-permute-start(bf16[128,1152]{1,0:T(8,128)(2,1)S(1)} %shard_map.84.refs_0_), channel_id=1, source_target_pairs={{0,1},{1,0},{2,3},{3,2},{4,5},{5,4},{6,7},{7,6},{8,9},{9,8},{10,11... | collective-permute-start | bytes 884744 | tf_op jit(solution)/shard_map/ppermute | solution.py:21
  27.5 14.7 %collective-permute-start.11 = (bf16[128,1152]{1,0:T(8,128)(2,1)S(1)}, bf16[128,1152]{1,0:T(8,128)(2,1)S(1)}, u32[]{:S(2)}, u32[]{:S(2)}) collective-permute-start(bf16[128,1152]{1,0:T(8,128)(2,1)S(1)} %shard_map.84.refs_0_), channel_id=1, source_target_pairs={{0,2},{1,3},{2,0},{3,1},{4,6},{5,7},{6,4},{7,5},{8,10},{9,11},{10,... | collective-permute-start | bytes 884744 | tf_op jit(solution)/shard_map/ppermute | solution.py:21
  28.1 14.1 %collective-permute-start.12 = (bf16[128,1152]{1,0:T(8,128)(2,1)S(1)}, bf16[128,1152]{1,0:T(8,128)(2,1)S(1)}, u32[]{:S(2)}, u32[]{:S(2)}) collective-permute-start(bf16[128,1152]{1,0:T(8,128)(2,1)S(1)} %shard_map.84.refs_0_), channel_id=1, source_target_pairs={{0,3},{1,2},{2,1},{3,0},{4,7},{5,6},{6,5},{7,4},{8,11},{9,10},{10,... | collective-permute-start | bytes 884744 | tf_op jit(solution)/shard_map/ppermute | solution.py:21
  33.7 2.4 %copy-start.3 = (s32[1,4]{1,0:T(1,128)S(1)}, s32[1,4]{1,0:T(1,128)}, u32[]{:S(2)}) copy-start(s32[1,4]{1,0:T(1,128)} %length_ref.3) | copy-start | bytes 52
  35.4 7.5 %collective-permute-start.13 = (bf16[144,1152]{1,0:T(8,128)(2,1)S(1)}, bf16[144,1152]{1,0:T(8,128)(2,1)S(1)}, u32[]{:S(2)}, u32[]{:S(2)}) collective-permute-start(bf16[144,1152]{1,0:T(8,128)(2,1)S(1)} %collective-permute-done.4.refs_4_), channel_id=1, source_target_pairs={{0,4},{4,0},{8,12},{12,8},{16,20},{20,16},{24,28},{28,24},{1,5},{5... | collective-permute-start | bytes 995336 | tf_op jit(solution)/shard_map/ppermute | solution.py:21
  35.5 7.5 %collective-permute-start.14 = (bf16[144,1152]{1,0:T(8,128)(2,1)S(1)}, bf16[144,1152]{1,0:T(8,128)(2,1)S(1)}, u32[]{:S(2)}, u32[]{:S(2)}) collective-permute-start(bf16[144,1152]{1,0:T(8,128)(2,1)S(1)} %collective-permute-done.5.refs_6_), channel_id=1, source_target_pairs={{0,4},{4,0},{8,12},{12,8},{16,20},{20,16},{24,28},{28,24},{1,5},{5... | collective-permute-start | bytes 995336 | tf_op jit(solution)/shard_map/ppermute | solution.py:21
  40.7 10.1 %collective-permute-start.18 = (bf16[144,1152]{1,0:T(8,128)(2,1)S(1)}, bf16[144,1152]{1,0:T(8,128)(2,1)S(1)}, u32[]{:S(2)}, u32[]{:S(2)}) collective-permute-start(bf16[144,1152]{1,0:T(8,128)(2,1)S(1)} %collective-permute-done.5.refs_6_), channel_id=1, source_target_pairs={{0,1},{1,0},{2,3},{3,2},{4,5},{5,4},{6,7},{7,6},{8,9},{9,8},{10,11... | collective-permute-start | bytes 995336 | tf_op jit(solution)/shard_map/ppermute | solution.py:21
  47.2 6.8 %collective-permute-start.15 = (bf16[288,256]{1,0:T(8,128)(2,1)S(1)}, bf16[288,256]{1,0:T(8,128)(2,1)S(1)}, u32[]{:S(2)}, u32[]{:S(2)}) collective-permute-start(bf16[288,256]{1,0:T(8,128)(2,1)S(1)} %get-tuple-element.90), channel_id=1, source_target_pairs={{0,1},{1,0},{2,3},{3,2},{4,5},{5,4},{6,7},{7,6},{8,9},{9,8},{10,11... | collective-permute-start | bytes 442376 | tf_op jit(solution)/shard_map/ppermute | solution.py:21
  48.1 6.9 %collective-permute-start.16 = (bf16[288,256]{1,0:T(8,128)(2,1)S(1)}, bf16[288,256]{1,0:T(8,128)(2,1)S(1)}, u32[]{:S(2)}, u32[]{:S(2)}) collective-permute-start(bf16[288,256]{1,0:T(8,128)(2,1)S(1)} %get-tuple-element.91), channel_id=1, source_target_pairs={{0,2},{1,3},{2,0},{3,1},{4,6},{5,7},{6,4},{7,5},{8,10},{9,11},{10,... | collective-permute-start | bytes 442376 | tf_op jit(solution)/shard_map/ppermute | solution.py:21
  49.7 6.6 %collective-permute-start.17 = (bf16[288,256]{1,0:T(8,128)(2,1)S(1)}, bf16[288,256]{1,0:T(8,128)(2,1)S(1)}, u32[]{:S(2)}, u32[]{:S(2)}) collective-permute-start(bf16[288,256]{1,0:T(8,128)(2,1)S(1)} %get-tuple-element.96), channel_id=1, source_target_pairs={{0,3},{1,2},{2,1},{3,0},{4,7},{5,6},{6,5},{7,4},{8,11},{9,10},{10,... | collective-permute-start | bytes 442376 | tf_op jit(solution)/shard_map/ppermute | solution.py:21
  50.7 5.5 %collective-permute-start.19 = (bf16[144,1152]{1,0:T(8,128)(2,1)S(1)}, bf16[144,1152]{1,0:T(8,128)(2,1)S(1)}, u32[]{:S(2)}, u32[]{:S(2)}) collective-permute-start(bf16[144,1152]{1,0:T(8,128)(2,1)S(1)} %collective-permute-done.18.refs_1_), channel_id=1, source_target_pairs={{0,4},{4,0},{8,12},{12,8},{16,20},{20,16},{24,28},{28,24},{1,5},{5... | collective-permute-start | bytes 995336 | tf_op jit(solution)/shard_map/ppermute | solution.py:21
  56.9 8.9 %collective-permute-start.24 = (bf16[64,1152]{1,0:T(8,128)(2,1)S(1)}, bf16[64,1152]{1,0:T(8,128)(2,1)S(1)}, u32[]{:S(2)}, u32[]{:S(2)}) collective-permute-start(bf16[64,1152]{1,0:T(8,128)(2,1)S(1)} %get-tuple-element.103), channel_id=1, source_target_pairs={{0,8},{4,12},{8,0},{12,4},{16,24},{20,28},{24,16},{28,20},{1,9},{5... | collective-permute-start | bytes 442376 | tf_op jit(solution)/shard_map/ppermute | solution.py:21
  59.6 6.3 %collective-permute-start.20 = (bf16[32,1152]{1,0:T(8,128)(2,1)S(1)}, bf16[32,1152]{1,0:T(8,128)(2,1)S(1)}, u32[]{:S(2)}, u32[]{:S(2)}) collective-permute-start(bf16[32,1152]{1,0:T(8,128)(2,1)S(1)} %get-tuple-element.98), channel_id=1, source_target_pairs={{0,16},{4,20},{8,24},{12,28},{16,0},{20,4},{24,8},{28,12},{1,17},{... | collective-permute-start | bytes 221192 | tf_op jit(solution)/shard_map/ppermute | solution.py:21
  61.2 11.0 %collective-permute-start.21 = (bf16[32,1152]{1,0:T(8,128)(2,1)S(1)}, bf16[32,1152]{1,0:T(8,128)(2,1)S(1)}, u32[]{:S(2)}, u32[]{:S(2)}) collective-permute-start(bf16[32,1152]{1,0:T(8,128)(2,1)S(1)} %get-tuple-element.99), channel_id=1, source_target_pairs={{0,20},{4,16},{8,28},{12,24},{16,4},{20,0},{24,12},{28,8},{1,21},{... | collective-permute-start | bytes 221192 | tf_op jit(solution)/shard_map/ppermute | solution.py:21
  61.2 11.0 %collective-permute-start.22 = (bf16[32,1152]{1,0:T(8,128)(2,1)S(1)}, bf16[32,1152]{1,0:T(8,128)(2,1)S(1)}, u32[]{:S(2)}, u32[]{:S(2)}) collective-permute-start(bf16[32,1152]{1,0:T(8,128)(2,1)S(1)} %get-tuple-element.100), channel_id=1, source_target_pairs={{0,24},{4,28},{8,16},{12,20},{16,8},{20,12},{24,0},{28,4},{1,25},{... | collective-permute-start | bytes 221192 | tf_op jit(solution)/shard_map/ppermute | solution.py:21
  62.3 9.9 %collective-permute-start.23 = (bf16[32,1152]{1,0:T(8,128)(2,1)S(1)}, bf16[32,1152]{1,0:T(8,128)(2,1)S(1)}, u32[]{:S(2)}, u32[]{:S(2)}) collective-permute-start(bf16[32,1152]{1,0:T(8,128)(2,1)S(1)} %get-tuple-element.101), channel_id=1, source_target_pairs={{0,28},{4,24},{8,20},{12,16},{16,12},{20,8},{24,4},{28,0},{1,29},{... | collective-permute-start | bytes 221192 | tf_op jit(solution)/shard_map/ppermute | solution.py:21
  65.8 6.4 %copy-start.7 = (s32[64]{0:T(128)S(1)}, s32[64]{0:T(128)}, u32[]{:S(2)}) copy-start(s32[64]{0:T(128)} %get-tuple-element.55.slot_ref) | copy-start | bytes 772
  65.8 6.3 %collective-permute-start.25 = (bf16[64,1152]{1,0:T(8,128)(2,1)S(1)}, bf16[64,1152]{1,0:T(8,128)(2,1)S(1)}, u32[]{:S(2)}, u32[]{:S(2)}) collective-permute-start(bf16[64,1152]{1,0:T(8,128)(2,1)S(1)} %shard_map.98), channel_id=1, source_target_pairs={{0,4},{4,0},{8,12},{12,8},{16,20},{20,16},{24,28},{28,24},{1,5},{5... | collective-permute-start | bytes 442376 | tf_op jit(solution)/shard_map/ppermute | solution.py:21

commit v3 on v2

--- a/solution.py
+++ b/solution.py
@@ -430,16 +430,16 @@
     halved = call(
         sides_kernel,
         [],
-        [sides[mask] for mask in along_y + along_x],
+        [sides[mask] for mask in along_x + along_y],
         [((group_rows // 2, model_width), BF16)] * len(sides),
     )
-    halved = dict(zip(along_y + along_x, halved))
+    halved = dict(zip(along_x + along_y, halved))
     near_blocks = []
     for mask in range(seq_count):
         mx = mask % x_count
         my = mask - mx
         if mx > 0 and my > 0:
-            near_blocks += [send(halved[my], "seq", mx), send(halved[mx], "seq", my)]
+            near_blocks += [send(halved[mx], "seq", my), send(halved[my], "seq", mx)]
         else:
             near_blocks.append(sides[mask] if mask > 0 else near)
     stacked_near = project(near_blocks)

time: 74.5 us -> 74.3 us (level)
  transfers between devices with their start and end apart: 26 -> 26, of which waited for: 10 -> 11; matrix products, arithmetic and copies ran while one was open for 0% -> 0% of each run, Pallas kernels for 19% -> 19%
where the time goes in v3:
time: 74.3 us; the launch traced here: 73.2 us
  starting transfers between devices  31.5 us (42%)
  waiting for transfers between devices  23.2 us (31%)
  Pallas kernels  18.3 us (25%)
    ppermute x26, starting transfers between devices, send(): return lax.ppermute(array, axis, [(i, i ^ mask) for i in range(count)])  31.5 us
    ppermute x26, waiting for transfers between devices, send(): return lax.ppermute(array, axis, [(i, i ^ mask) for i in range(count)])  23.2 us
    pallas_call x18, Pallas kernels, call(): pl.pallas_call(kernel, in_specs=[smem] * len(scalars) + (where if isinsta...  18.3 us
  transfers between devices with their start and end apart: 26, of which 11 were waited for; matrix products, arithmetic and copies ran while one was open for 0% of the time, Pallas kernels for 19%

profile of v3, /device:TPU:0, one launch (start us, length us, event | category | flops | bytes accessed | tf_op | source)
XLA Modules:
  0.0 73.2 jit_solution(16836622935182225576)
XLA Ops:
  0.0 2.1 %shard_map.82 = (s32[64]{0:T(128)}, bf16[128,1152]{1,0:T(8,128)(2,1)}, bf16[128,1152]{1,0:T(8,128)(2,1)}) custom-call(s32[1]{0:T(128)} %bitcast.place_ref.owner_ref, s32[1,64]{1,0:T(1,128)} %owner_hbm.1, bf16[1,64,4,1152]{3,2,1,0:T(4,128)(2,1)} %token_hbm.1), custom_call_target="tpu_custom_call" | custom-call | flops 30000001024 | bytes 1048576 | tf_op jit(solution)/shard_map/pallas_call | solution.py:337
  2.1 0.5 collective-permute-start
  2.7 0.1 shard_map.86
  2.8 2.6 %collective-permute-start.4 = (bf16[144,1152]{1,0:T(8,128)(2,1)S(1)}, bf16[144,1152]{1,0:T(8,128)(2,1)S(1)}, u32[]{:S(2)}, u32[]{:S(2)}) collective-permute-start(bf16[144,1152]{1,0:T(8,128)(2,1)S(1)} %shard_map.86), channel_id=1, source_target_pairs={{0,1},{1,0},{2,3},{3,2},{4,5},{5,4},{6,7},{7,6},{8,9},{9,8},{10,11... | collective-permute-start | bytes 995336 | tf_op jit(solution)/shard_map/ppermute | solution.py:21
  5.4 1.5 %collective-permute-start.5 = (bf16[144,1152]{1,0:T(8,128)(2,1)S(1)}, bf16[144,1152]{1,0:T(8,128)(2,1)S(1)}, u32[]{:S(2)}, u32[]{:S(2)}) collective-permute-start(bf16[144,1152]{1,0:T(8,128)(2,1)S(1)} %shard_map.86), channel_id=1, source_target_pairs={{0,2},{1,3},{2,0},{3,1},{4,6},{5,7},{6,4},{7,5},{8,10},{9,11},{10,... | collective-permute-start | bytes 995336 | tf_op jit(solution)/shard_map/ppermute | solution.py:21
  6.9 0.0 collective-permute-done.other_ref
  6.9 0.1 shard_map.83
  7.0 1.6 %collective-permute-start.3 = (bf16[64,1152]{1,0:T(8,128)(2,1)S(1)}, bf16[64,1152]{1,0:T(8,128)(2,1)S(1)}, u32[]{:S(2)}, u32[]{:S(2)}) collective-permute-start(bf16[64,1152]{1,0:T(8,128)(2,1)S(1)} %get-tuple-element.61), channel_id=1, source_target_pairs={{0,8},{4,12},{8,0},{12,4},{16,24},{20,28},{24,16},{28,20},{1,9},{5... | collective-permute-start | bytes 442376 | tf_op jit(solution)/shard_map/ppermute | solution.py:21
  8.7 2.6 %collective-permute-start.1 = (bf16[64,1152]{1,0:T(8,128)(2,1)S(1)}, bf16[64,1152]{1,0:T(8,128)(2,1)S(1)}, u32[]{:S(2)}, u32[]{:S(2)}) collective-permute-start(bf16[64,1152]{1,0:T(8,128)(2,1)S(1)} %get-tuple-element.58), channel_id=1, source_target_pairs={{0,16},{4,20},{8,24},{12,28},{16,0},{20,4},{24,8},{28,12},{1,17},{... | collective-permute-start | bytes 442376 | tf_op jit(solution)/shard_map/ppermute | solution.py:21
  11.3 0.2 collective-permute-start.2
  11.5 3.4 %collective-permute-done.3.refs_1_ = bf16[64,1152]{1,0:T(8,128)(2,1)S(1)} collective-permute-done((bf16[64,1152]{1,0:T(8,128)(2,1)S(1)}, bf16[64,1152]{1,0:T(8,128)(2,1)S(1)}, u32[]{:S(2)}, u32[]{:S(2)}) %collective-permute-start.3) | collective-permute-done | bytes 147488 | tf_op jit(solution)/shard_map/ppermute | solution.py:21
  14.9 0.6 shard_map.85.refs_0_
  15.5 0.0 collective-permute-done.4.refs_4_
  15.5 0.0 collective-permute-done.5.refs_6_
  15.5 0.6 collective-permute-start.6
  16.1 1.5 %collective-permute-start.7 = (bf16[128,1152]{1,0:T(8,128)(2,1)S(1)}, bf16[128,1152]{1,0:T(8,128)(2,1)S(1)}, u32[]{:S(2)}, u32[]{:S(2)}) collective-permute-start(bf16[128,1152]{1,0:T(8,128)(2,1)S(1)} %shard_map.85.refs_0_), channel_id=1, source_target_pairs={{0,2},{1,3},{2,0},{3,1},{4,6},{5,7},{6,4},{7,5},{8,10},{9,11},{10,... | collective-permute-start | bytes 884744 | tf_op jit(solution)/shard_map/ppermute | solution.py:21
  17.6 5.1 %collective-permute-done.1.refs_0_.refs_2_ = bf16[64,1152]{1,0:T(8,128)(2,1)S(1)} collective-permute-done((bf16[64,1152]{1,0:T(8,128)(2,1)S(1)}, bf16[64,1152]{1,0:T(8,128)(2,1)S(1)}, u32[]{:S(2)}, u32[]{:S(2)}) %collective-permute-start.1) | collective-permute-done | bytes 147488 | tf_op jit(solution)/shard_map/ppermute | solution.py:21
  22.7 0.0 collective-permute-done.2.refs_1_.refs_3_
  22.7 0.6 shard_map.84.refs_0_
  23.2 0.0 copy-start
  23.2 0.0 copy-start.2
  23.3 0.3 collective-permute-done.6.refs_0_.refs_1_
  23.6 0.4 collective-permute-done.7.refs_1_.refs_2_
  24.0 1.4 %collective-permute-start.10 = (bf16[64,1152]{1,0:T(8,128)(2,1)S(1)}, bf16[64,1152]{1,0:T(8,128)(2,1)S(1)}, u32[]{:S(2)}, u32[]{:S(2)}) collective-permute-start(bf16[64,1152]{1,0:T(8,128)(2,1)S(1)} %get-tuple-element.67), channel_id=1, source_target_pairs={{0,1},{1,0},{2,3},{3,2},{4,5},{5,4},{6,7},{7,6},{8,9},{9,8},{10,11... | collective-permute-start | bytes 442376 | tf_op jit(solution)/shard_map/ppermute | solution.py:21
  25.4 1.5 %collective-permute-start.9 = (bf16[64,1152]{1,0:T(8,128)(2,1)S(1)}, bf16[64,1152]{1,0:T(8,128)(2,1)S(1)}, u32[]{:S(2)}, u32[]{:S(2)}) collective-permute-start(bf16[64,1152]{1,0:T(8,128)(2,1)S(1)} %get-tuple-element.66), channel_id=1, source_target_pairs={{0,2},{1,3},{2,0},{3,1},{4,6},{5,7},{6,4},{7,5},{8,10},{9,11},{10,... | collective-permute-start | bytes 442376 | tf_op jit(solution)/shard_map/ppermute | solution.py:21
  26.9 0.6 collective-permute-start.8
  27.5 0.6 collective-permute-start.11
  28.1 2.3 %collective-permute-start.12 = (bf16[128,1152]{1,0:T(8,128)(2,1)S(1)}, bf16[128,1152]{1,0:T(8,128)(2,1)S(1)}, u32[]{:S(2)}, u32[]{:S(2)}) collective-permute-start(bf16[128,1152]{1,0:T(8,128)(2,1)S(1)} %shard_map.84.refs_0_), channel_id=1, source_target_pairs={{0,3},{1,2},{2,1},{3,0},{4,7},{5,6},{6,5},{7,4},{8,11},{9,10},{10,... | collective-permute-start | bytes 884744 | tf_op jit(solution)/shard_map/ppermute | solution.py:21
  30.4 0.3 collective-permute-done.10.refs_4_
  30.7 1.4 %collective-permute-done.9.refs_3_ = bf16[64,1152]{1,0:T(8,128)(2,1)S(1)} collective-permute-done((bf16[64,1152]{1,0:T(8,128)(2,1)S(1)}, bf16[64,1152]{1,0:T(8,128)(2,1)S(1)}, u32[]{:S(2)}, u32[]{:S(2)}) %collective-permute-start.9) | collective-permute-done | bytes 147488 | tf_op jit(solution)/shard_map/ppermute | solution.py:21
  32.1 1.4 %shard_map.88.stacked_ref = bf16[864,512]{1,0:T(8,128)(2,1)S(1)} custom-call(bf16[864,1152]{1,0:T(8,128)(2,1)S(1)} %bitcast.9, f32[2,72]{1,0:T(2,128)S(1)} %copy-done.2, bf16[128,1152]{1,0:T(8,128)(2,1)S(1)} %shard_map.85.refs_0_, bf16[128,1152]{1,0:T(8,128)(2,1)S(1)} %collective-permute-done.6.refs_0_.refs_1_, ...), custom_call_target="tpu_custom_call" | custom-call | flops 3000000000 | bytes 1048576 | tf_op jit(solution)/shard_map/pallas_call | solution.py:337
  33.5 0.0 copy-start.3
  33.5 1.8 %shard_map.89.refs_0_ = bf16[4,864,256]{2,1,0:T(8,128)(2,1)S(1)} custom-call(s32[1]{0:T(128)} %bitcast.place_ref.owner_ref, s32[1]{0:T(128)} %bitcast.2.place_ref, s32[1,4,16]{2,1,0:T(4,128)S(1)} %copy-done.1, bf16[864,512]{1,0:T(8,128)(2,1)S(1)} %shard_map.88.stacked_ref), custom_call_target="tpu_custom_call" | custom-call | flops 3000000000 | bytes 1048576 | tf_op jit(solution)/shard_map/pallas_call | solution.py:337
  35.3 0.1 collective-permute-start.13
  35.4 0.5 collective-permute-start.14
  35.9 1.3 %shard_map.90 = (bf16[256,1152]{1,0:T(8,128)(2,1)S(1)}, bf16[256,1152]{1,0:T(8,128)(2,1)S(1)}) custom-call(s32[1,4]{1,0:T(1,128)S(1)} %copy-done.3, s32[1]{0:T(128)} %bitcast.place_ref.owner_ref, s32[1]{0:T(128)} %bitcast.2.place_ref, s32[1,4,16]{2,1,0:T(4,128)S(1)} %copy-done.1, bf16[3,4,1152]{2,1,0:T(4,128)(2,1)S(1)} %bitcast.14, ...), custom_call_target="tpu_custom_call" | custom-call | flops 1000000000 | bytes 1048576 | tf_op jit(solution)/shard_map/pallas_call | solution.py:337
  37.1 0.0 collective-permute-done.8.refs_1_
  37.2 0.8 %shard_map.91.stacked_ref = bf16[864,256]{1,0:T(8,128)(2,1)S(1)} custom-call(bf16[864,1152]{1,0:T(8,128)(2,1)S(1)} %bitcast.10, f32[2,72]{1,0:T(2,128)S(1)} %copy-done.2, bf16[128,1152]{1,0:T(8,128)(2,1)S(1)} %shard_map.84.refs_0_, bf16[128,1152]{1,0:T(8,128)(2,1)S(1)} %collective-permute-done.8.refs_1_), custom_call_target="tpu_custom_call" | custom-call | flops 3000000000 | bytes 1048576 | tf_op jit(solution)/shard_map/pallas_call | solution.py:337
  37.9 1.3 %shard_map.92.refs_0_ = bf16[4,864,256]{2,1,0:T(8,128)(2,1)S(1)} custom-call(s32[1]{0:T(128)} %bitcast.place_ref.owner_ref, s32[1]{0:T(128)} %bitcast.2.place_ref, s32[1,4,16]{2,1,0:T(4,128)S(1)} %copy-done.1, bf16[864,256]{1,0:T(8,128)(2,1)S(1)} %shard_map.91.stacked_ref, bf16[4,864,256]{2,1,0:T(8,128)(2,1)S(1)} %shard_map.89.refs_0_), custom_call_target="tpu_custom_call" | custom-call | flops 3000000000 | bytes 1048576 | tf_op jit(solution)/shard_map/pallas_call | solution.py:337
  39.3 1.4 %collective-permute-start.18 = (bf16[144,1152]{1,0:T(8,128)(2,1)S(1)}, bf16[144,1152]{1,0:T(8,128)(2,1)S(1)}, u32[]{:S(2)}, u32[]{:S(2)}) collective-permute-start(bf16[144,1152]{1,0:T(8,128)(2,1)S(1)} %collective-permute-done.5.refs_6_), channel_id=1, source_target_pairs={{0,1},{1,0},{2,3},{3,2},{4,5},{5,4},{6,7},{7,6},{8,9},{9,8},{10,11... | collective-permute-start | bytes 995336 | tf_op jit(solution)/shard_map/ppermute | solution.py:21
  40.6 1.0 %collective-permute-done.11.refs_0_ = bf16[128,1152]{1,0:T(8,128)(2,1)S(1)} collective-permute-done((bf16[128,1152]{1,0:T(8,128)(2,1)S(1)}, bf16[128,1152]{1,0:T(8,128)(2,1)S(1)}, u32[]{:S(2)}, u32[]{:S(2)}) %collective-permute-start.11) | collective-permute-done | bytes 294944 | tf_op jit(solution)/shard_map/ppermute | solution.py:21
  41.6 0.0 collective-permute-done.12.refs_1_
  41.6 0.8 %shard_map.93.refs_1_ = bf16[864,256]{1,0:T(8,128)(2,1)S(1)} custom-call(bf16[864,1152]{1,0:T(8,128)(2,1)S(1)} %bitcast.11, f32[2,72]{1,0:T(2,128)S(1)} %copy-done.2, bf16[128,1152]{1,0:T(8,128)(2,1)S(1)} %collective-permute-done.11.refs_0_, bf16[128,1152]{1,0:T(8,128)(2,1)S(1)} %collective-permute-done.12.refs_1_), custom_call_target="tpu_custom_call" | custom-call | flops 100000000 | bytes 1048576 | tf_op jit(solution)/shard_map/pallas_call | solution.py:337
  42.4 0.0 collective-permute-done.13.refs_5_
  42.4 0.0 collective-permute-done.14.refs_7_
  42.4 4.2 %shard_map.94 = (bf16[288,256]{1,0:T(8,128)(2,1)S(1)}, bf16[288,256]{1,0:T(8,128)(2,1)S(1)}, bf16[288,256]{1,0:T(8,128)(2,1)S(1)}, bf16[288,256]{1,0:T(8,128)(2,1)S(1)}) custom-call(s32[1,4]{1,0:T(1,128)S(1)} %copy-done.3, s32[1]{0:T(128)} %bitcast.place_ref.owner_ref, s32[1]{0:T(128)} %bitcast.2.place_ref, s32[1,4,16]{2,1,0:T(4,128)S(1)} %copy-done.1, ...), custom_call_target="tpu_custom_call" | custom-call | flops 100000000 | bytes 1048576 | tf_op jit(solution)/shard_map/pallas_call | solution.py:337
  46.6 1.5 %collective-permute-start.15 = (bf16[288,256]{1,0:T(8,128)(2,1)S(1)}, bf16[288,256]{1,0:T(8,128)(2,1)S(1)}, u32[]{:S(2)}, u32[]{:S(2)}) collective-permute-start(bf16[288,256]{1,0:T(8,128)(2,1)S(1)} %get-tuple-element.90), channel_id=1, source_target_pairs={{0,1},{1,0},{2,3},{3,2},{4,5},{5,4},{6,7},{7,6},{8,9},{9,8},{10,11... | collective-permute-start | bytes 442376 | tf_op jit(solution)/shard_map/ppermute | solution.py:21
  48.1 0.7 collective-permute-start.16
  48.8 1.4 %collective-permute-start.17 = (bf16[288,256]{1,0:T(8,128)(2,1)S(1)}, bf16[288,256]{1,0:T(8,128)(2,1)S(1)}, u32[]{:S(2)}, u32[]{:S(2)}) collective-permute-start(bf16[288,256]{1,0:T(8,128)(2,1)S(1)} %get-tuple-element.96), channel_id=1, source_target_pairs={{0,3},{1,2},{2,1},{3,0},{4,7},{5,6},{6,5},{7,4},{8,11},{9,10},{10,... | collective-permute-start | bytes 442376 | tf_op jit(solution)/shard_map/ppermute | solution.py:21
  50.2 3.3 %collective-permute-done.15.refs_1_ = bf16[288,256]{1,0:T(8,128)(2,1)S(1)} collective-permute-done((bf16[288,256]{1,0:T(8,128)(2,1)S(1)}, bf16[288,256]{1,0:T(8,128)(2,1)S(1)}, u32[]{:S(2)}, u32[]{:S(2)}) %collective-permute-start.15) | collective-permute-done | bytes 147488 | tf_op jit(solution)/shard_map/ppermute | solution.py:21
  53.5 1.0 %collective-permute-done.16.refs_2_ = bf16[288,256]{1,0:T(8,128)(2,1)S(1)} collective-permute-done((bf16[288,256]{1,0:T(8,128)(2,1)S(1)}, bf16[288,256]{1,0:T(8,128)(2,1)S(1)}, u32[]{:S(2)}, u32[]{:S(2)}) %collective-permute-start.16) | collective-permute-done | bytes 147488 | tf_op jit(solution)/shard_map/ppermute | solution.py:21
  54.5 1.2 %shard_map.95.partial_ref = f32[256,1152]{1,0:T(8,128)S(1)} custom-call(s32[1]{0:T(128)} %bitcast.1.core_ref, bf16[288,256]{1,0:T(8,128)(2,1)S(1)} %get-tuple-element.89.refs_0_, bf16[288,256]{1,0:T(8,128)(2,1)S(1)} %collective-permute-done.15.refs_1_, bf16[288,256]{1,0:T(8,128)(2,1)S(1)} %collective-permute-done.16.refs_2_, ...), custom_call_target="tpu_custom_call" | custom-call | flops 10000000000 | bytes 1048576 | tf_op jit(solution)/shard_map/pallas_call | solution.py:337
  55.7 0.7 collective-permute-done.17.refs_0_
  56.4 0.0 collective-permute-done.19.refs_2_
  56.4 0.6 shard_map.96
  57.1 1.7 %collective-permute-start.24 = (bf16[64,1152]{1,0:T(8,128)(2,1)S(1)}, bf16[64,1152]{1,0:T(8,128)(2,1)S(1)}, u32[]{:S(2)}, u32[]{:S(2)}) collective-permute-start(bf16[64,1152]{1,0:T(8,128)(2,1)S(1)} %get-tuple-element.103), channel_id=1, source_target_pairs={{0,8},{4,12},{8,0},{12,4},{16,24},{20,28},{24,16},{28,20},{1,9},{5... | collective-permute-start | bytes 442376 | tf_op jit(solution)/shard_map/ppermute | solution.py:21
  58.7 2.6 %collective-permute-start.20 = (bf16[32,1152]{1,0:T(8,128)(2,1)S(1)}, bf16[32,1152]{1,0:T(8,128)(2,1)S(1)}, u32[]{:S(2)}, u32[]{:S(2)}) collective-permute-start(bf16[32,1152]{1,0:T(8,128)(2,1)S(1)} %get-tuple-element.98), channel_id=1, source_target_pairs={{0,16},{4,20},{8,24},{12,28},{16,0},{20,4},{24,8},{28,12},{1,17},{... | collective-permute-start | bytes 221192 | tf_op jit(solution)/shard_map/ppermute | solution.py:21
  61.3 0.0 collective-permute-start.21
  61.3 1.3 %collective-permute-start.22 = (bf16[32,1152]{1,0:T(8,128)(2,1)S(1)}, bf16[32,1152]{1,0:T(8,128)(2,1)S(1)}, u32[]{:S(2)}, u32[]{:S(2)}) collective-permute-start(bf16[32,1152]{1,0:T(8,128)(2,1)S(1)} %get-tuple-element.100), channel_id=1, source_target_pairs={{0,24},{4,28},{8,16},{12,20},{16,8},{20,12},{24,0},{28,4},{1,25},{... | collective-permute-start | bytes 221192 | tf_op jit(solution)/shard_map/ppermute | solution.py:21
  62.6 2.7 %collective-permute-start.23 = (bf16[32,1152]{1,0:T(8,128)(2,1)S(1)}, bf16[32,1152]{1,0:T(8,128)(2,1)S(1)}, u32[]{:S(2)}, u32[]{:S(2)}) collective-permute-start(bf16[32,1152]{1,0:T(8,128)(2,1)S(1)} %get-tuple-element.101), channel_id=1, source_target_pairs={{0,28},{4,24},{8,20},{12,16},{16,12},{20,8},{24,4},{28,0},{1,29},{... | collective-permute-start | bytes 221192 | tf_op jit(solution)/shard_map/ppermute | solution.py:21
  65.3 0.2 collective-permute-start.25
  65.5 6.2 %collective-permute-done.21.refs_1_ = bf16[32,1152]{1,0:T(8,128)(2,1)S(1)} collective-permute-done((bf16[32,1152]{1,0:T(8,128)(2,1)S(1)}, bf16[32,1152]{1,0:T(8,128)(2,1)S(1)}, u32[]{:S(2)}, u32[]{:S(2)}) %collective-permute-start.21) | collective-permute-done | bytes 73760 | tf_op jit(solution)/shard_map/ppermute | solution.py:21
  71.7 0.0 collective-permute-done.25.refs_1_
  71.7 1.5 %shard_map.99 = bf16[1,64,4,1152]{3,2,1,0:T(4,128)(2,1)} custom-call(s32[64]{0:T(128)S(1)} %copy-done.7, bf16[128,1152]{1,0:T(8,128)(2,1)S(1)} %shard_map.97.refs_0_, bf16[64,1152]{1,0:T(8,128)(2,1)S(1)} %collective-permute-done.25.refs_1_, bf16[32,1152]{1,0:T(8,128)(2,1)S(1)} %get-tuple-element.104.refs_2_, ...), custom_call_target="tpu_custom_call" | custom-call | flops 1000000000 | bytes 1048576 | tf_op jit(solution)/shard_map/pallas_call | solution.py:337
  (22 shorter events, 0.1 us)
Async XLA Ops:
  0.0 2.7 %copy-start.4 = (bf16[288,1152]{1,0:T(8,128)(2,1)S(1)}, bf16[288,1152]{1,0:T(8,128)(2,1)}, u32[]{:S(2)}) copy-start(bf16[288,1152]{1,0:T(8,128)(2,1)} %refs_3_.1) | copy-start | bytes 1990660
  2.1 4.8 %collective-permute-start = (bf16[128,1152]{1,0:T(8,128)(2,1)}, bf16[128,1152]{1,0:T(8,128)(2,1)S(1)}, u32[]{:S(2)}, u32[]{:S(2)}) collective-permute-start(bf16[128,1152]{1,0:T(8,128)(2,1)} %get-tuple-element.57), channel_id=1, source_target_pairs={{0,4},{4,0},{8,12},{12,8},{16,20},{20,16},{24,28},{28,24},{1,5},{5... | collective-permute-start | bytes 884744 | tf_op jit(solution)/shard_map/ppermute | solution.py:21
  2.7 4.2 %copy-start.6 = (bf16[128,1152]{1,0:T(8,128)(2,1)S(1)}, bf16[128,1152]{1,0:T(8,128)(2,1)}, u32[]{:S(2)}) copy-start(bf16[128,1152]{1,0:T(8,128)(2,1)} %get-tuple-element.56.own_hbm) | copy-start | bytes 884740
  2.8 12.7 %collective-permute-start.4 = (bf16[144,1152]{1,0:T(8,128)(2,1)S(1)}, bf16[144,1152]{1,0:T(8,128)(2,1)S(1)}, u32[]{:S(2)}, u32[]{:S(2)}) collective-permute-start(bf16[144,1152]{1,0:T(8,128)(2,1)S(1)} %shard_map.86), channel_id=1, source_target_pairs={{0,1},{1,0},{2,3},{3,2},{4,5},{5,4},{6,7},{7,6},{8,9},{9,8},{10,11... | collective-permute-start | bytes 995336 | tf_op jit(solution)/shard_map/ppermute | solution.py:21
  5.4 10.1 %collective-permute-start.5 = (bf16[144,1152]{1,0:T(8,128)(2,1)S(1)}, bf16[144,1152]{1,0:T(8,128)(2,1)S(1)}, u32[]{:S(2)}, u32[]{:S(2)}) collective-permute-start(bf16[144,1152]{1,0:T(8,128)(2,1)S(1)} %shard_map.86), channel_id=1, source_target_pairs={{0,2},{1,3},{2,0},{3,1},{4,6},{5,7},{6,4},{7,5},{8,10},{9,11},{10,... | collective-permute-start | bytes 995336 | tf_op jit(solution)/shard_map/ppermute | solution.py:21
  6.9 8.0 %copy-start.1 = (s32[1,4,16]{2,1,0:T(4,128)S(1)}, s32[1,4,16]{2,1,0:T(4,128)}, u32[]{:S(2)}) copy-start(s32[1,4,16]{2,1,0:T(4,128)} %table_ref.11) | copy-start | bytes 772
  6.9 8.0 %copy-start.5 = (bf16[1,4,3,1152]{3,1,2,0:T(4,128)(2,1)S(1)}, bf16[1,4,3,1152]{3,1,2,0:T(4,128)(2,1)}, u32[]{:S(2)}) copy-start(bf16[1,4,3,1152]{3,1,2,0:T(4,128)(2,1)} %param.12) | copy-start | bytes 82948
  7.0 7.9 %collective-permute-start.3 = (bf16[64,1152]{1,0:T(8,128)(2,1)S(1)}, bf16[64,1152]{1,0:T(8,128)(2,1)S(1)}, u32[]{:S(2)}, u32[]{:S(2)}) collective-permute-start(bf16[64,1152]{1,0:T(8,128)(2,1)S(1)} %get-tuple-element.61), channel_id=1, source_target_pairs={{0,8},{4,12},{8,0},{12,4},{16,24},{20,28},{24,16},{28,20},{1,9},{5... | collective-permute-start | bytes 442376 | tf_op jit(solution)/shard_map/ppermute | solution.py:21
  8.7 14.0 %collective-permute-start.1 = (bf16[64,1152]{1,0:T(8,128)(2,1)S(1)}, bf16[64,1152]{1,0:T(8,128)(2,1)S(1)}, u32[]{:S(2)}, u32[]{:S(2)}) collective-permute-start(bf16[64,1152]{1,0:T(8,128)(2,1)S(1)} %get-tuple-element.58), channel_id=1, source_target_pairs={{0,16},{4,20},{8,24},{12,28},{16,0},{20,4},{24,8},{28,12},{1,17},{... | collective-permute-start | bytes 442376 | tf_op jit(solution)/shard_map/ppermute | solution.py:21
  11.3 11.4 %collective-permute-start.2 = (bf16[64,1152]{1,0:T(8,128)(2,1)S(1)}, bf16[64,1152]{1,0:T(8,128)(2,1)S(1)}, u32[]{:S(2)}, u32[]{:S(2)}) collective-permute-start(bf16[64,1152]{1,0:T(8,128)(2,1)S(1)} %get-tuple-element.59), channel_id=1, source_target_pairs={{0,24},{4,28},{8,16},{12,20},{16,8},{20,12},{24,0},{28,4},{1,25},{... | collective-permute-start | bytes 442376 | tf_op jit(solution)/shard_map/ppermute | solution.py:21
  15.5 8.1 %collective-permute-start.6 = (bf16[128,1152]{1,0:T(8,128)(2,1)S(1)}, bf16[128,1152]{1,0:T(8,128)(2,1)S(1)}, u32[]{:S(2)}, u32[]{:S(2)}) collective-permute-start(bf16[128,1152]{1,0:T(8,128)(2,1)S(1)} %shard_map.85.refs_0_), channel_id=1, source_target_pairs={{0,1},{1,0},{2,3},{3,2},{4,5},{5,4},{6,7},{7,6},{8,9},{9,8},{10,11... | collective-permute-start | bytes 884744 | tf_op jit(solution)/shard_map/ppermute | solution.py:21
  16.1 7.9 %collective-permute-start.7 = (bf16[128,1152]{1,0:T(8,128)(2,1)S(1)}, bf16[128,1152]{1,0:T(8,128)(2,1)S(1)}, u32[]{:S(2)}, u32[]{:S(2)}) collective-permute-start(bf16[128,1152]{1,0:T(8,128)(2,1)S(1)} %shard_map.85.refs_0_), channel_id=1, source_target_pairs={{0,2},{1,3},{2,0},{3,1},{4,6},{5,7},{6,4},{7,5},{8,10},{9,11},{10,... | collective-permute-start | bytes 884744 | tf_op jit(solution)/shard_map/ppermute | solution.py:21
  23.2 8.9 %copy-start = (bf16[1152,3,288]{0,2,1:T(8,128)(2,1)S(1)}, bf16[1152,3,288]{0,2,1:T(8,128)(2,1)}, u32[]{:S(2)}) copy-start(bf16[1152,3,288]{0,2,1:T(8,128)(2,1)} %param.13) | copy-start | bytes 5971972
  23.2 8.9 %copy-start.2 = (f32[2,72]{1,0:T(2,128)S(1)}, f32[2,72]{1,0:T(2,128)}, u32[]{:S(2)}) copy-start(f32[2,72]{1,0:T(2,128)} %gain_ref.5) | copy-start | bytes 1732
  24.0 6.7 %collective-permute-start.10 = (bf16[64,1152]{1,0:T(8,128)(2,1)S(1)}, bf16[64,1152]{1,0:T(8,128)(2,1)S(1)}, u32[]{:S(2)}, u32[]{:S(2)}) collective-permute-start(bf16[64,1152]{1,0:T(8,128)(2,1)S(1)} %get-tuple-element.67), channel_id=1, source_target_pairs={{0,1},{1,0},{2,3},{3,2},{4,5},{5,4},{6,7},{7,6},{8,9},{9,8},{10,11... | collective-permute-start | bytes 442376 | tf_op jit(solution)/shard_map/ppermute | solution.py:21
  25.4 6.7 %collective-permute-start.9 = (bf16[64,1152]{1,0:T(8,128)(2,1)S(1)}, bf16[64,1152]{1,0:T(8,128)(2,1)S(1)}, u32[]{:S(2)}, u32[]{:S(2)}) collective-permute-start(bf16[64,1152]{1,0:T(8,128)(2,1)S(1)} %get-tuple-element.66), channel_id=1, source_target_pairs={{0,2},{1,3},{2,0},{3,1},{4,6},{5,7},{6,4},{7,5},{8,10},{9,11},{10,... | collective-permute-start | bytes 442376 | tf_op jit(solution)/shard_map/ppermute | solution.py:21
  26.9 10.2 %collective-permute-start.8 = (bf16[128,1152]{1,0:T(8,128)(2,1)S(1)}, bf16[128,1152]{1,0:T(8,128)(2,1)S(1)}, u32[]{:S(2)}, u32[]{:S(2)}) collective-permute-start(bf16[128,1152]{1,0:T(8,128)(2,1)S(1)} %shard_map.84.refs_0_), channel_id=1, source_target_pairs={{0,1},{1,0},{2,3},{3,2},{4,5},{5,4},{6,7},{7,6},{8,9},{9,8},{10,11... | collective-permute-start | bytes 884744 | tf_op jit(solution)/shard_map/ppermute | solution.py:21
  27.5 14.1 %collective-permute-start.11 = (bf16[128,1152]{1,0:T(8,128)(2,1)S(1)}, bf16[128,1152]{1,0:T(8,128)(2,1)S(1)}, u32[]{:S(2)}, u32[]{:S(2)}) collective-permute-start(bf16[128,1152]{1,0:T(8,128)(2,1)S(1)} %shard_map.84.refs_0_), channel_id=1, source_target_pairs={{0,2},{1,3},{2,0},{3,1},{4,6},{5,7},{6,4},{7,5},{8,10},{9,11},{10,... | collective-permute-start | bytes 884744 | tf_op jit(solution)/shard_map/ppermute | solution.py:21
  28.1 13.5 %collective-permute-start.12 = (bf16[128,1152]{1,0:T(8,128)(2,1)S(1)}, bf16[128,1152]{1,0:T(8,128)(2,1)S(1)}, u32[]{:S(2)}, u32[]{:S(2)}) collective-permute-start(bf16[128,1152]{1,0:T(8,128)(2,1)S(1)} %shard_map.84.refs_0_), channel_id=1, source_target_pairs={{0,3},{1,2},{2,1},{3,0},{4,7},{5,6},{6,5},{7,4},{8,11},{9,10},{10,... | collective-permute-start | bytes 884744 | tf_op jit(solution)/shard_map/ppermute | solution.py:21
  33.5 2.4 %copy-start.3 = (s32[1,4]{1,0:T(1,128)S(1)}, s32[1,4]{1,0:T(1,128)}, u32[]{:S(2)}) copy-start(s32[1,4]{1,0:T(1,128)} %length_ref.3) | copy-start | bytes 52
  35.3 7.1 %collective-permute-start.13 = (bf16[144,1152]{1,0:T(8,128)(2,1)S(1)}, bf16[144,1152]{1,0:T(8,128)(2,1)S(1)}, u32[]{:S(2)}, u32[]{:S(2)}) collective-permute-start(bf16[144,1152]{1,0:T(8,128)(2,1)S(1)} %collective-permute-done.4.refs_4_), channel_id=1, source_target_pairs={{0,4},{4,0},{8,12},{12,8},{16,20},{20,16},{24,28},{28,24},{1,5},{5... | collective-permute-start | bytes 995336 | tf_op jit(solution)/shard_map/ppermute | solution.py:21
  35.4 7.0 %collective-permute-start.14 = (bf16[144,1152]{1,0:T(8,128)(2,1)S(1)}, bf16[144,1152]{1,0:T(8,128)(2,1)S(1)}, u32[]{:S(2)}, u32[]{:S(2)}) collective-permute-start(bf16[144,1152]{1,0:T(8,128)(2,1)S(1)} %collective-permute-done.5.refs_6_), channel_id=1, source_target_pairs={{0,4},{4,0},{8,12},{12,8},{16,20},{20,16},{24,28},{28,24},{1,5},{5... | collective-permute-start | bytes 995336 | tf_op jit(solution)/shard_map/ppermute | solution.py:21
  39.3 10.9 %collective-permute-start.18 = (bf16[144,1152]{1,0:T(8,128)(2,1)S(1)}, bf16[144,1152]{1,0:T(8,128)(2,1)S(1)}, u32[]{:S(2)}, u32[]{:S(2)}) collective-permute-start(bf16[144,1152]{1,0:T(8,128)(2,1)S(1)} %collective-permute-done.5.refs_6_), channel_id=1, source_target_pairs={{0,1},{1,0},{2,3},{3,2},{4,5},{5,4},{6,7},{7,6},{8,9},{9,8},{10,11... | collective-permute-start | bytes 995336 | tf_op jit(solution)/shard_map/ppermute | solution.py:21
  46.6 6.9 %collective-permute-start.15 = (bf16[288,256]{1,0:T(8,128)(2,1)S(1)}, bf16[288,256]{1,0:T(8,128)(2,1)S(1)}, u32[]{:S(2)}, u32[]{:S(2)}) collective-permute-start(bf16[288,256]{1,0:T(8,128)(2,1)S(1)} %get-tuple-element.90), channel_id=1, source_target_pairs={{0,1},{1,0},{2,3},{3,2},{4,5},{5,4},{6,7},{7,6},{8,9},{9,8},{10,11... | collective-permute-start | bytes 442376 | tf_op jit(solution)/shard_map/ppermute | solution.py:21
  48.1 6.4 %collective-permute-start.16 = (bf16[288,256]{1,0:T(8,128)(2,1)S(1)}, bf16[288,256]{1,0:T(8,128)(2,1)S(1)}, u32[]{:S(2)}, u32[]{:S(2)}) collective-permute-start(bf16[288,256]{1,0:T(8,128)(2,1)S(1)} %get-tuple-element.91), channel_id=1, source_target_pairs={{0,2},{1,3},{2,0},{3,1},{4,6},{5,7},{6,4},{7,5},{8,10},{9,11},{10,... | collective-permute-start | bytes 442376 | tf_op jit(solution)/shard_map/ppermute | solution.py:21
  48.8 7.6 %collective-permute-start.17 = (bf16[288,256]{1,0:T(8,128)(2,1)S(1)}, bf16[288,256]{1,0:T(8,128)(2,1)S(1)}, u32[]{:S(2)}, u32[]{:S(2)}) collective-permute-start(bf16[288,256]{1,0:T(8,128)(2,1)S(1)} %get-tuple-element.96), channel_id=1, source_target_pairs={{0,3},{1,2},{2,1},{3,0},{4,7},{5,6},{6,5},{7,4},{8,11},{9,10},{10,... | collective-permute-start | bytes 442376 | tf_op jit(solution)/shard_map/ppermute | solution.py:21
  50.2 6.3 %collective-permute-start.19 = (bf16[144,1152]{1,0:T(8,128)(2,1)S(1)}, bf16[144,1152]{1,0:T(8,128)(2,1)S(1)}, u32[]{:S(2)}, u32[]{:S(2)}) collective-permute-start(bf16[144,1152]{1,0:T(8,128)(2,1)S(1)} %collective-permute-done.18.refs_1_), channel_id=1, source_target_pairs={{0,4},{4,0},{8,12},{12,8},{16,20},{20,16},{24,28},{28,24},{1,5},{5... | collective-permute-start | bytes 995336 | tf_op jit(solution)/shard_map/ppermute | solution.py:21
  57.1 8.2 %collective-permute-start.24 = (bf16[64,1152]{1,0:T(8,128)(2,1)S(1)}, bf16[64,1152]{1,0:T(8,128)(2,1)S(1)}, u32[]{:S(2)}, u32[]{:S(2)}) collective-permute-start(bf16[64,1152]{1,0:T(8,128)(2,1)S(1)} %get-tuple-element.103), channel_id=1, source_target_pairs={{0,8},{4,12},{8,0},{12,4},{16,24},{20,28},{24,16},{28,20},{1,9},{5... | collective-permute-start | bytes 442376 | tf_op jit(solution)/shard_map/ppermute | solution.py:21
  58.7 6.7 %collective-permute-start.20 = (bf16[32,1152]{1,0:T(8,128)(2,1)S(1)}, bf16[32,1152]{1,0:T(8,128)(2,1)S(1)}, u32[]{:S(2)}, u32[]{:S(2)}) collective-permute-start(bf16[32,1152]{1,0:T(8,128)(2,1)S(1)} %get-tuple-element.98), channel_id=1, source_target_pairs={{0,16},{4,20},{8,24},{12,28},{16,0},{20,4},{24,8},{28,12},{1,17},{... | collective-permute-start | bytes 221192 | tf_op jit(solution)/shard_map/ppermute | solution.py:21
  61.3 10.4 %collective-permute-start.21 = (bf16[32,1152]{1,0:T(8,128)(2,1)S(1)}, bf16[32,1152]{1,0:T(8,128)(2,1)S(1)}, u32[]{:S(2)}, u32[]{:S(2)}) collective-permute-start(bf16[32,1152]{1,0:T(8,128)(2,1)S(1)} %get-tuple-element.99), channel_id=1, source_target_pairs={{0,20},{4,16},{8,28},{12,24},{16,4},{20,0},{24,12},{28,8},{1,21},{... | collective-permute-start | bytes 221192 | tf_op jit(solution)/shard_map/ppermute | solution.py:21
  61.3 10.4 %collective-permute-start.22 = (bf16[32,1152]{1,0:T(8,128)(2,1)S(1)}, bf16[32,1152]{1,0:T(8,128)(2,1)S(1)}, u32[]{:S(2)}, u32[]{:S(2)}) collective-permute-start(bf16[32,1152]{1,0:T(8,128)(2,1)S(1)} %get-tuple-element.100), channel_id=1, source_target_pairs={{0,24},{4,28},{8,16},{12,20},{16,8},{20,12},{24,0},{28,4},{1,25},{... | collective-permute-start | bytes 221192 | tf_op jit(solution)/shard_map/ppermute | solution.py:21
  62.6 9.1 %collective-permute-start.23 = (bf16[32,1152]{1,0:T(8,128)(2,1)S(1)}, bf16[32,1152]{1,0:T(8,128)(2,1)S(1)}, u32[]{:S(2)}, u32[]{:S(2)}) collective-permute-start(bf16[32,1152]{1,0:T(8,128)(2,1)S(1)} %get-tuple-element.101), channel_id=1, source_target_pairs={{0,28},{4,24},{8,20},{12,16},{16,12},{20,8},{24,4},{28,0},{1,29},{... | collective-permute-start | bytes 221192 | tf_op jit(solution)/shard_map/ppermute | solution.py:21
  65.3 6.4 %copy-start.7 = (s32[64]{0:T(128)S(1)}, s32[64]{0:T(128)}, u32[]{:S(2)}) copy-start(s32[64]{0:T(128)} %get-tuple-element.55.slot_ref) | copy-start | bytes 772
  65.3 6.4 %collective-permute-start.25 = (bf16[64,1152]{1,0:T(8,128)(2,1)S(1)}, bf16[64,1152]{1,0:T(8,128)(2,1)S(1)}, u32[]{:S(2)}, u32[]{:S(2)}) collective-permute-start(bf16[64,1152]{1,0:T(8,128)(2,1)S(1)} %shard_map.98), channel_id=1, source_target_pairs={{0,4},{4,0},{8,12},{12,8},{16,20},{20,16},{24,28},{28,24},{1,5},{5... | collective-permute-start | bytes 442376 | tf_op jit(solution)/shard_map/ppermute | solution.py:21

commit v4 on v3

--- a/solution.py
+++ b/solution.py
@@ -455,17 +455,9 @@
         return gathered
 
     gathered = gather(0, stacked_near)
-    gathered, proj_parts, settled = lax.optimization_barrier((gathered, proj_parts, arrived))
+    gathered, proj_parts = lax.optimization_barrier((gathered, proj_parts))
     early_blocks, late_blocks = far_blocks[: seq_count // 2], far_blocks[seq_count // 2 :]
-    residual = call(
-        functools.partial(residual_kernel, clip_tokens, codes_of(0)),
-        [clip_length, owner_place, place],
-        [clip_pieces, factors] + settled,
-        [((rows_here, model_width), BF16)] * 2,
-    )
-    early_blocks, gathered, residual = lax.optimization_barrier(
-        (early_blocks, gathered, list(residual))
-    )
+    early_blocks, gathered = lax.optimization_barrier((early_blocks, gathered))
     gathered = gather(seq_count * group_rows, project(early_blocks), gathered)
     swapped = {mask: send(proj_parts[mask], "dp", 1) for mask in proj_parts} if halves == 2 else {}
     gathered, proj_parts = lax.optimization_barrier((gathered, proj_parts))
@@ -509,10 +501,18 @@
 
     beside = [0] + along_x + along_y
     across = [mask for mask in range(seq_count) if mask not in beside]
+    _, settled = lax.optimization_barrier((attended[0], arrived))
+    residual = call(
+        functools.partial(residual_kernel, clip_tokens, codes_of(0)),
+        [clip_length, owner_place, place],
+        [clip_pieces, factors] + settled,
+        [((rows_here, model_width), BF16)] * 2,
+    )
+    proj_own, residual = lax.optimization_barrier((proj_weight, list(residual)))
     (partial,) = call(
         functools.partial(sides_output_kernel, beside, halves),
         [core],
-        [returned[mask] for mask in beside] + weights_of(beside),
+        [returned[mask] for mask in beside] + [proj_own] + weights_of(beside)[1:],
         [((rows_here, model_width), F32)],
         flops=10**10,
     )

time: 74.3 us -> 74.9 us (level); the launches traced: 73.2 us -> 74.6 us
  waiting for transfers between devices: 23.2 us -> 24.5 us
    ppermute x26, waiting for transfers between devices: 23.2 us -> 24.5 us  [send(): return lax.ppermute(array, axis, [(i, i ^ mask) for i in range(count)])]
  transfers between devices with their start and end apart: 26 -> 26, of which waited for: 11 -> 12; matrix products, arithmetic and copies ran while one was open for 0% -> 0% of each run, Pallas kernels for 19% -> 19%
where the time goes in v4:
time: 74.9 us; the launch traced here: 74.6 us
  starting transfers between devices  31.5 us (42%)
  waiting for transfers between devices  24.5 us (33%)
  Pallas kernels  18.3 us (24%)
    ppermute x26, starting transfers between devices, send(): return lax.ppermute(array, axis, [(i, i ^ mask) for i in range(count)])  31.5 us
    ppermute x26, waiting for transfers between devices, send(): return lax.ppermute(array, axis, [(i, i ^ mask) for i in range(count)])  24.5 us
    pallas_call x18, Pallas kernels, call(): pl.pallas_call(kernel, in_specs=[smem] * len(scalars) + (where if isinsta...  18.3 us
  transfers between devices with their start and end apart: 26, of which 12 were waited for; matrix products, arithmetic and copies ran while one was open for 0% of the time, Pallas kernels for 19%

profile of v4, /device:TPU:0, one launch (start us, length us, event | category | flops | bytes accessed | tf_op | source)
XLA Modules:
  0.0 74.6 jit_solution(9420538409967684371)
XLA Ops:
  0.0 2.1 %shard_map.82 = (s32[64]{0:T(128)}, bf16[128,1152]{1,0:T(8,128)(2,1)}, bf16[128,1152]{1,0:T(8,128)(2,1)}) custom-call(s32[1]{0:T(128)} %bitcast.place_ref.owner_ref, s32[1,64]{1,0:T(1,128)} %owner_hbm.1, bf16[1,64,4,1152]{3,2,1,0:T(4,128)(2,1)} %token_hbm.1), custom_call_target="tpu_custom_call" | custom-call | flops 30000001024 | bytes 1048576 | tf_op jit(solution)/shard_map/pallas_call | solution.py:337
  2.1 0.5 collective-permute-start
  2.7 0.1 shard_map.86
  2.8 2.6 %collective-permute-start.4 = (bf16[144,1152]{1,0:T(8,128)(2,1)S(1)}, bf16[144,1152]{1,0:T(8,128)(2,1)S(1)}, u32[]{:S(2)}, u32[]{:S(2)}) collective-permute-start(bf16[144,1152]{1,0:T(8,128)(2,1)S(1)} %shard_map.86), channel_id=1, source_target_pairs={{0,1},{1,0},{2,3},{3,2},{4,5},{5,4},{6,7},{7,6},{8,9},{9,8},{10,11... | collective-permute-start | bytes 995336 | tf_op jit(solution)/shard_map/ppermute | solution.py:21
  5.4 1.5 %collective-permute-start.5 = (bf16[144,1152]{1,0:T(8,128)(2,1)S(1)}, bf16[144,1152]{1,0:T(8,128)(2,1)S(1)}, u32[]{:S(2)}, u32[]{:S(2)}) collective-permute-start(bf16[144,1152]{1,0:T(8,128)(2,1)S(1)} %shard_map.86), channel_id=1, source_target_pairs={{0,2},{1,3},{2,0},{3,1},{4,6},{5,7},{6,4},{7,5},{8,10},{9,11},{10,... | collective-permute-start | bytes 995336 | tf_op jit(solution)/shard_map/ppermute | solution.py:21
  6.9 0.0 collective-permute-done.other_ref
  6.9 0.1 shard_map.83
  7.0 1.6 %collective-permute-start.3 = (bf16[64,1152]{1,0:T(8,128)(2,1)S(1)}, bf16[64,1152]{1,0:T(8,128)(2,1)S(1)}, u32[]{:S(2)}, u32[]{:S(2)}) collective-permute-start(bf16[64,1152]{1,0:T(8,128)(2,1)S(1)} %get-tuple-element.62), channel_id=1, source_target_pairs={{0,8},{4,12},{8,0},{12,4},{16,24},{20,28},{24,16},{28,20},{1,9},{5... | collective-permute-start | bytes 442376 | tf_op jit(solution)/shard_map/ppermute | solution.py:21
  8.7 2.6 %collective-permute-start.1 = (bf16[64,1152]{1,0:T(8,128)(2,1)S(1)}, bf16[64,1152]{1,0:T(8,128)(2,1)S(1)}, u32[]{:S(2)}, u32[]{:S(2)}) collective-permute-start(bf16[64,1152]{1,0:T(8,128)(2,1)S(1)} %get-tuple-element.59), channel_id=1, source_target_pairs={{0,16},{4,20},{8,24},{12,28},{16,0},{20,4},{24,8},{28,12},{1,17},{... | collective-permute-start | bytes 442376 | tf_op jit(solution)/shard_map/ppermute | solution.py:21
  11.3 0.2 collective-permute-start.2
  11.5 3.4 %collective-permute-done.3.refs_1_ = bf16[64,1152]{1,0:T(8,128)(2,1)S(1)} collective-permute-done((bf16[64,1152]{1,0:T(8,128)(2,1)S(1)}, bf16[64,1152]{1,0:T(8,128)(2,1)S(1)}, u32[]{:S(2)}, u32[]{:S(2)}) %collective-permute-start.3) | collective-permute-done | bytes 147488 | tf_op jit(solution)/shard_map/ppermute | solution.py:21
  14.9 0.6 shard_map.85.refs_0_
  15.5 0.0 collective-permute-done.4.refs_4_
  15.5 0.6 collective-permute-start.6
  16.1 1.5 %collective-permute-start.7 = (bf16[128,1152]{1,0:T(8,128)(2,1)S(1)}, bf16[128,1152]{1,0:T(8,128)(2,1)S(1)}, u32[]{:S(2)}, u32[]{:S(2)}) collective-permute-start(bf16[128,1152]{1,0:T(8,128)(2,1)S(1)} %shard_map.85.refs_0_), channel_id=1, source_target_pairs={{0,2},{1,3},{2,0},{3,1},{4,6},{5,7},{6,4},{7,5},{8,10},{9,11},{10,... | collective-permute-start | bytes 884744 | tf_op jit(solution)/shard_map/ppermute | solution.py:21
  17.6 5.1 %collective-permute-done.1.refs_0_.refs_2_ = bf16[64,1152]{1,0:T(8,128)(2,1)S(1)} collective-permute-done((bf16[64,1152]{1,0:T(8,128)(2,1)S(1)}, bf16[64,1152]{1,0:T(8,128)(2,1)S(1)}, u32[]{:S(2)}, u32[]{:S(2)}) %collective-permute-start.1) | collective-permute-done | bytes 147488 | tf_op jit(solution)/shard_map/ppermute | solution.py:21
  22.7 0.0 collective-permute-done.2.refs_1_.refs_3_
  22.7 0.6 shard_map.84.refs_0_
  23.2 0.0 copy-start
  23.2 0.0 copy-start.2
  23.3 0.3 collective-permute-done.6.refs_0_.refs_1_
  23.6 0.4 collective-permute-done.7.refs_1_.refs_2_
  24.0 1.5 %collective-permute-start.11 = (bf16[64,1152]{1,0:T(8,128)(2,1)S(1)}, bf16[64,1152]{1,0:T(8,128)(2,1)S(1)}, u32[]{:S(2)}, u32[]{:S(2)}) collective-permute-start(bf16[64,1152]{1,0:T(8,128)(2,1)S(1)} %get-tuple-element.67), channel_id=1, source_target_pairs={{0,2},{1,3},{2,0},{3,1},{4,6},{5,7},{6,4},{7,5},{8,10},{9,11},{10,... | collective-permute-start | bytes 442376 | tf_op jit(solution)/shard_map/ppermute | solution.py:21
  25.5 1.4 %collective-permute-start.12 = (bf16[64,1152]{1,0:T(8,128)(2,1)S(1)}, bf16[64,1152]{1,0:T(8,128)(2,1)S(1)}, u32[]{:S(2)}, u32[]{:S(2)}) collective-permute-start(bf16[64,1152]{1,0:T(8,128)(2,1)S(1)} %get-tuple-element.68), channel_id=1, source_target_pairs={{0,1},{1,0},{2,3},{3,2},{4,5},{5,4},{6,7},{7,6},{8,9},{9,8},{10,11... | collective-permute-start | bytes 442376 | tf_op jit(solution)/shard_map/ppermute | solution.py:21
  26.9 0.6 collective-permute-start.10
  27.5 0.6 collective-permute-start.8
  28.1 2.3 %collective-permute-start.9 = (bf16[128,1152]{1,0:T(8,128)(2,1)S(1)}, bf16[128,1152]{1,0:T(8,128)(2,1)S(1)}, u32[]{:S(2)}, u32[]{:S(2)}) collective-permute-start(bf16[128,1152]{1,0:T(8,128)(2,1)S(1)} %shard_map.84.refs_0_), channel_id=1, source_target_pairs={{0,3},{1,2},{2,1},{3,0},{4,7},{5,6},{6,5},{7,4},{8,11},{9,10},{10,... | collective-permute-start | bytes 884744 | tf_op jit(solution)/shard_map/ppermute | solution.py:21
  30.4 0.4 collective-permute-done.11.refs_3_
  30.8 1.5 %collective-permute-done.12.refs_4_ = bf16[64,1152]{1,0:T(8,128)(2,1)S(1)} collective-permute-done((bf16[64,1152]{1,0:T(8,128)(2,1)S(1)}, bf16[64,1152]{1,0:T(8,128)(2,1)S(1)}, u32[]{:S(2)}, u32[]{:S(2)}) %collective-permute-start.12) | collective-permute-done | bytes 147488 | tf_op jit(solution)/shard_map/ppermute | solution.py:21
  32.3 1.4 %shard_map.88.stacked_ref = bf16[864,512]{1,0:T(8,128)(2,1)S(1)} custom-call(bf16[864,1152]{1,0:T(8,128)(2,1)S(1)} %bitcast.9, f32[2,72]{1,0:T(2,128)S(1)} %copy-done.2, bf16[128,1152]{1,0:T(8,128)(2,1)S(1)} %shard_map.85.refs_0_, bf16[128,1152]{1,0:T(8,128)(2,1)S(1)} %collective-permute-done.6.refs_0_.refs_1_, ...), custom_call_target="tpu_custom_call" | custom-call | flops 3000000000 | bytes 1048576 | tf_op jit(solution)/shard_map/pallas_call | solution.py:337
  33.6 1.8 %shard_map.89.refs_0_ = bf16[4,864,256]{2,1,0:T(8,128)(2,1)S(1)} custom-call(s32[1]{0:T(128)} %bitcast.place_ref.owner_ref, s32[1]{0:T(128)} %bitcast.2.place_ref, s32[1,4,16]{2,1,0:T(4,128)S(1)} %copy-done.1, bf16[864,512]{1,0:T(8,128)(2,1)S(1)} %shard_map.88.stacked_ref), custom_call_target="tpu_custom_call" | custom-call | flops 3000000000 | bytes 1048576 | tf_op jit(solution)/shard_map/pallas_call | solution.py:337
  35.4 0.1 collective-permute-start.13
  35.5 0.5 collective-permute-start.14
  36.0 2.6 %collective-permute-done.10.refs_1_ = bf16[128,1152]{1,0:T(8,128)(2,1)S(1)} collective-permute-done((bf16[128,1152]{1,0:T(8,128)(2,1)S(1)}, bf16[128,1152]{1,0:T(8,128)(2,1)S(1)}, u32[]{:S(2)}, u32[]{:S(2)}) %collective-permute-start.10) | collective-permute-done | bytes 294944 | tf_op jit(solution)/shard_map/ppermute | solution.py:21
  38.6 0.8 %shard_map.90.stacked_ref = bf16[864,256]{1,0:T(8,128)(2,1)S(1)} custom-call(bf16[864,1152]{1,0:T(8,128)(2,1)S(1)} %bitcast.10, f32[2,72]{1,0:T(2,128)S(1)} %copy-done.2, bf16[128,1152]{1,0:T(8,128)(2,1)S(1)} %shard_map.84.refs_0_, bf16[128,1152]{1,0:T(8,128)(2,1)S(1)} %collective-permute-done.10.refs_1_), custom_call_target="tpu_custom_call" | custom-call | flops 3000000000 | bytes 1048576 | tf_op jit(solution)/shard_map/pallas_call | solution.py:337
  39.3 1.3 %shard_map.91.refs_0_ = bf16[4,864,256]{2,1,0:T(8,128)(2,1)S(1)} custom-call(s32[1]{0:T(128)} %bitcast.place_ref.owner_ref, s32[1]{0:T(128)} %bitcast.2.place_ref, s32[1,4,16]{2,1,0:T(4,128)S(1)} %copy-done.1, bf16[864,256]{1,0:T(8,128)(2,1)S(1)} %shard_map.90.stacked_ref, bf16[4,864,256]{2,1,0:T(8,128)(2,1)S(1)} %shard_map.89.refs_0_), custom_call_target="tpu_custom_call" | custom-call | flops 3000000000 | bytes 1048576 | tf_op jit(solution)/shard_map/pallas_call | solution.py:337
  40.7 0.0 copy-start.3
  40.7 1.5 %collective-permute-start.18 = (bf16[144,1152]{1,0:T(8,128)(2,1)S(1)}, bf16[144,1152]{1,0:T(8,128)(2,1)S(1)}, u32[]{:S(2)}, u32[]{:S(2)}) collective-permute-start(bf16[144,1152]{1,0:T(8,128)(2,1)S(1)} %collective-permute-done.5.refs_6_), channel_id=1, source_target_pairs={{0,1},{1,0},{2,3},{3,2},{4,5},{5,4},{6,7},{7,6},{8,9},{9,8},{10,11... | collective-permute-start | bytes 995336 | tf_op jit(solution)/shard_map/ppermute | solution.py:21
  42.2 0.1 collective-permute-done.9.refs_1_
  42.3 0.8 %shard_map.92.refs_1_ = bf16[864,256]{1,0:T(8,128)(2,1)S(1)} custom-call(bf16[864,1152]{1,0:T(8,128)(2,1)S(1)} %bitcast.11, f32[2,72]{1,0:T(2,128)S(1)} %copy-done.2, bf16[128,1152]{1,0:T(8,128)(2,1)S(1)} %collective-permute-done.8.refs_0_, bf16[128,1152]{1,0:T(8,128)(2,1)S(1)} %collective-permute-done.9.refs_1_), custom_call_target="tpu_custom_call" | custom-call | flops 100000000 | bytes 1048576 | tf_op jit(solution)/shard_map/pallas_call | solution.py:337
  43.1 0.0 collective-permute-done.13.refs_5_
  43.1 0.0 collective-permute-done.14.refs_7_
  43.1 4.2 %shard_map.93 = (bf16[288,256]{1,0:T(8,128)(2,1)S(1)}, bf16[288,256]{1,0:T(8,128)(2,1)S(1)}, bf16[288,256]{1,0:T(8,128)(2,1)S(1)}, bf16[288,256]{1,0:T(8,128)(2,1)S(1)}) custom-call(s32[1,4]{1,0:T(1,128)S(1)} %copy-done.3, s32[1]{0:T(128)} %bitcast.place_ref.owner_ref, s32[1]{0:T(128)} %bitcast.2.place_ref, s32[1,4,16]{2,1,0:T(4,128)S(1)} %copy-done.1, ...), custom_call_target="tpu_custom_call" | custom-call | flops 100000000 | bytes 1048576 | tf_op jit(solution)/shard_map/pallas_call | solution.py:337
  47.3 1.5 %collective-permute-start.15 = (bf16[288,256]{1,0:T(8,128)(2,1)S(1)}, bf16[288,256]{1,0:T(8,128)(2,1)S(1)}, u32[]{:S(2)}, u32[]{:S(2)}) collective-permute-start(bf16[288,256]{1,0:T(8,128)(2,1)S(1)} %get-tuple-element.91), channel_id=1, source_target_pairs={{0,1},{1,0},{2,3},{3,2},{4,5},{5,4},{6,7},{7,6},{8,9},{9,8},{10,11... | collective-permute-start | bytes 442376 | tf_op jit(solution)/shard_map/ppermute | solution.py:21
  48.8 1.7 %collective-permute-start.16 = (bf16[288,256]{1,0:T(8,128)(2,1)S(1)}, bf16[288,256]{1,0:T(8,128)(2,1)S(1)}, u32[]{:S(2)}, u32[]{:S(2)}) collective-permute-start(bf16[288,256]{1,0:T(8,128)(2,1)S(1)} %get-tuple-element.92), channel_id=1, source_target_pairs={{0,2},{1,3},{2,0},{3,1},{4,6},{5,7},{6,4},{7,5},{8,10},{9,11},{10,... | collective-permute-start | bytes 442376 | tf_op jit(solution)/shard_map/ppermute | solution.py:21
  50.5 1.3 %shard_map.94 = (bf16[256,1152]{1,0:T(8,128)(2,1)S(1)}, bf16[256,1152]{1,0:T(8,128)(2,1)S(1)}) custom-call(s32[1,4]{1,0:T(1,128)S(1)} %copy-done.3, s32[1]{0:T(128)} %bitcast.place_ref.owner_ref, s32[1]{0:T(128)} %bitcast.2.place_ref, s32[1,4,16]{2,1,0:T(4,128)S(1)} %copy-done.1, bf16[3,4,1152]{2,1,0:T(4,128)(2,1)S(1)} %bitcast.14, ...), custom_call_target="tpu_custom_call" | custom-call | flops 1000000000 | bytes 1048576 | tf_op jit(solution)/shard_map/pallas_call | solution.py:337
  51.8 0.4 collective-permute-start.17
  52.2 0.0 collective-permute-done.18.refs_1_
  52.2 0.0 collective-permute-start.19
  52.2 1.4 %collective-permute-done.15.refs_1_ = bf16[288,256]{1,0:T(8,128)(2,1)S(1)} collective-permute-done((bf16[288,256]{1,0:T(8,128)(2,1)S(1)}, bf16[288,256]{1,0:T(8,128)(2,1)S(1)}, u32[]{:S(2)}, u32[]{:S(2)}) %collective-permute-start.15) | collective-permute-done | bytes 147488 | tf_op jit(solution)/shard_map/ppermute | solution.py:21
  53.6 0.7 collective-permute-done.16.refs_2_
  54.2 1.2 %shard_map.95.partial_ref = f32[256,1152]{1,0:T(8,128)S(1)} custom-call(s32[1]{0:T(128)} %bitcast.1.core_ref, bf16[288,256]{1,0:T(8,128)(2,1)S(1)} %get-tuple-element.82.refs_0_, bf16[288,256]{1,0:T(8,128)(2,1)S(1)} %collective-permute-done.15.refs_1_, bf16[288,256]{1,0:T(8,128)(2,1)S(1)} %collective-permute-done.16.refs_2_, ...), custom_call_target="tpu_custom_call" | custom-call | flops 10000000000 | bytes 1048576 | tf_op jit(solution)/shard_map/pallas_call | solution.py:337
  55.5 2.4 %collective-permute-done.17.refs_0_ = bf16[288,256]{1,0:T(8,128)(2,1)S(1)} collective-permute-done((bf16[288,256]{1,0:T(8,128)(2,1)S(1)}, bf16[288,256]{1,0:T(8,128)(2,1)S(1)}, u32[]{:S(2)}, u32[]{:S(2)}) %collective-permute-start.17) | collective-permute-done | bytes 147488 | tf_op jit(solution)/shard_map/ppermute | solution.py:21
  57.9 0.6 shard_map.96
  58.5 1.6 %collective-permute-start.24 = (bf16[64,1152]{1,0:T(8,128)(2,1)S(1)}, bf16[64,1152]{1,0:T(8,128)(2,1)S(1)}, u32[]{:S(2)}, u32[]{:S(2)}) collective-permute-start(bf16[64,1152]{1,0:T(8,128)(2,1)S(1)} %get-tuple-element.105), channel_id=1, source_target_pairs={{0,8},{4,12},{8,0},{12,4},{16,24},{20,28},{24,16},{28,20},{1,9},{5... | collective-permute-start | bytes 442376 | tf_op jit(solution)/shard_map/ppermute | solution.py:21
  60.2 2.6 %collective-permute-start.20 = (bf16[32,1152]{1,0:T(8,128)(2,1)S(1)}, bf16[32,1152]{1,0:T(8,128)(2,1)S(1)}, u32[]{:S(2)}, u32[]{:S(2)}) collective-permute-start(bf16[32,1152]{1,0:T(8,128)(2,1)S(1)} %get-tuple-element.100), channel_id=1, source_target_pairs={{0,16},{4,20},{8,24},{12,28},{16,0},{20,4},{24,8},{28,12},{1,17},{... | collective-permute-start | bytes 221192 | tf_op jit(solution)/shard_map/ppermute | solution.py:21
  62.8 0.0 collective-permute-start.21
  62.8 0.2 collective-permute-start.22
  63.0 3.4 %collective-permute-start.23 = (bf16[32,1152]{1,0:T(8,128)(2,1)S(1)}, bf16[32,1152]{1,0:T(8,128)(2,1)S(1)}, u32[]{:S(2)}, u32[]{:S(2)}) collective-permute-start(bf16[32,1152]{1,0:T(8,128)(2,1)S(1)} %get-tuple-element.103), channel_id=1, source_target_pairs={{0,28},{4,24},{8,20},{12,16},{16,12},{20,8},{24,4},{28,0},{1,29},{... | collective-permute-start | bytes 221192 | tf_op jit(solution)/shard_map/ppermute | solution.py:21
  66.4 0.0 collective-permute-done.24.refs_0_.refs_3_
  66.4 0.4 collective-permute-start.25
  66.8 6.2 %collective-permute-done.21.refs_1_ = bf16[32,1152]{1,0:T(8,128)(2,1)S(1)} collective-permute-done((bf16[32,1152]{1,0:T(8,128)(2,1)S(1)}, bf16[32,1152]{1,0:T(8,128)(2,1)S(1)}, u32[]{:S(2)}, u32[]{:S(2)}) %collective-permute-start.21) | collective-permute-done | bytes 73760 | tf_op jit(solution)/shard_map/ppermute | solution.py:21
  73.1 0.0 collective-permute-done.25.refs_1_
  73.1 1.5 %shard_map.99 = bf16[1,64,4,1152]{3,2,1,0:T(4,128)(2,1)} custom-call(s32[64]{0:T(128)S(1)} %copy-done.7, bf16[128,1152]{1,0:T(8,128)(2,1)S(1)} %shard_map.97.refs_0_, bf16[64,1152]{1,0:T(8,128)(2,1)S(1)} %collective-permute-done.25.refs_1_, bf16[32,1152]{1,0:T(8,128)(2,1)S(1)} %get-tuple-element.106.refs_2_, ...), custom_call_target="tpu_custom_call" | custom-call | flops 1000000000 | bytes 1048576 | tf_op jit(solution)/shard_map/pallas_call | solution.py:337
  (22 shorter events, 0.1 us)
Async XLA Ops:
  0.0 2.7 %copy-start.4 = (bf16[288,1152]{1,0:T(8,128)(2,1)S(1)}, bf16[288,1152]{1,0:T(8,128)(2,1)}, u32[]{:S(2)}) copy-start(bf16[288,1152]{1,0:T(8,128)(2,1)} %refs_3_) | copy-start | bytes 1990660
  2.1 4.8 %collective-permute-start = (bf16[128,1152]{1,0:T(8,128)(2,1)}, bf16[128,1152]{1,0:T(8,128)(2,1)S(1)}, u32[]{:S(2)}, u32[]{:S(2)}) collective-permute-start(bf16[128,1152]{1,0:T(8,128)(2,1)} %get-tuple-element.58), channel_id=1, source_target_pairs={{0,4},{4,0},{8,12},{12,8},{16,20},{20,16},{24,28},{28,24},{1,5},{5... | collective-permute-start | bytes 884744 | tf_op jit(solution)/shard_map/ppermute | solution.py:21
  2.7 4.2 %copy-start.6 = (bf16[128,1152]{1,0:T(8,128)(2,1)S(1)}, bf16[128,1152]{1,0:T(8,128)(2,1)}, u32[]{:S(2)}) copy-start(bf16[128,1152]{1,0:T(8,128)(2,1)} %get-tuple-element.57.own_hbm) | copy-start | bytes 884740
  2.8 12.7 %collective-permute-start.4 = (bf16[144,1152]{1,0:T(8,128)(2,1)S(1)}, bf16[144,1152]{1,0:T(8,128)(2,1)S(1)}, u32[]{:S(2)}, u32[]{:S(2)}) collective-permute-start(bf16[144,1152]{1,0:T(8,128)(2,1)S(1)} %shard_map.86), channel_id=1, source_target_pairs={{0,1},{1,0},{2,3},{3,2},{4,5},{5,4},{6,7},{7,6},{8,9},{9,8},{10,11... | collective-permute-start | bytes 995336 | tf_op jit(solution)/shard_map/ppermute | solution.py:21
  5.4 10.1 %collective-permute-start.5 = (bf16[144,1152]{1,0:T(8,128)(2,1)S(1)}, bf16[144,1152]{1,0:T(8,128)(2,1)S(1)}, u32[]{:S(2)}, u32[]{:S(2)}) collective-permute-start(bf16[144,1152]{1,0:T(8,128)(2,1)S(1)} %shard_map.86), channel_id=1, source_target_pairs={{0,2},{1,3},{2,0},{3,1},{4,6},{5,7},{6,4},{7,5},{8,10},{9,11},{10,... | collective-permute-start | bytes 995336 | tf_op jit(solution)/shard_map/ppermute | solution.py:21
  6.9 8.0 %copy-start.1 = (s32[1,4,16]{2,1,0:T(4,128)S(1)}, s32[1,4,16]{2,1,0:T(4,128)}, u32[]{:S(2)}) copy-start(s32[1,4,16]{2,1,0:T(4,128)} %table_ref.11) | copy-start | bytes 772
  6.9 8.0 %copy-start.5 = (bf16[1,4,3,1152]{3,1,2,0:T(4,128)(2,1)S(1)}, bf16[1,4,3,1152]{3,1,2,0:T(4,128)(2,1)}, u32[]{:S(2)}) copy-start(bf16[1,4,3,1152]{3,1,2,0:T(4,128)(2,1)} %param.12) | copy-start | bytes 82948
  7.0 7.9 %collective-permute-start.3 = (bf16[64,1152]{1,0:T(8,128)(2,1)S(1)}, bf16[64,1152]{1,0:T(8,128)(2,1)S(1)}, u32[]{:S(2)}, u32[]{:S(2)}) collective-permute-start(bf16[64,1152]{1,0:T(8,128)(2,1)S(1)} %get-tuple-element.62), channel_id=1, source_target_pairs={{0,8},{4,12},{8,0},{12,4},{16,24},{20,28},{24,16},{28,20},{1,9},{5... | collective-permute-start | bytes 442376 | tf_op jit(solution)/shard_map/ppermute | solution.py:21
  8.7 14.0 %collective-permute-start.1 = (bf16[64,1152]{1,0:T(8,128)(2,1)S(1)}, bf16[64,1152]{1,0:T(8,128)(2,1)S(1)}, u32[]{:S(2)}, u32[]{:S(2)}) collective-permute-start(bf16[64,1152]{1,0:T(8,128)(2,1)S(1)} %get-tuple-element.59), channel_id=1, source_target_pairs={{0,16},{4,20},{8,24},{12,28},{16,0},{20,4},{24,8},{28,12},{1,17},{... | collective-permute-start | bytes 442376 | tf_op jit(solution)/shard_map/ppermute | solution.py:21
  11.3 11.4 %collective-permute-start.2 = (bf16[64,1152]{1,0:T(8,128)(2,1)S(1)}, bf16[64,1152]{1,0:T(8,128)(2,1)S(1)}, u32[]{:S(2)}, u32[]{:S(2)}) collective-permute-start(bf16[64,1152]{1,0:T(8,128)(2,1)S(1)} %get-tuple-element.60), channel_id=1, source_target_pairs={{0,24},{4,28},{8,16},{12,20},{16,8},{20,12},{24,0},{28,4},{1,25},{... | collective-permute-start | bytes 442376 | tf_op jit(solution)/shard_map/ppermute | solution.py:21
  15.5 8.1 %collective-permute-start.6 = (bf16[128,1152]{1,0:T(8,128)(2,1)S(1)}, bf16[128,1152]{1,0:T(8,128)(2,1)S(1)}, u32[]{:S(2)}, u32[]{:S(2)}) collective-permute-start(bf16[128,1152]{1,0:T(8,128)(2,1)S(1)} %shard_map.85.refs_0_), channel_id=1, source_target_pairs={{0,1},{1,0},{2,3},{3,2},{4,5},{5,4},{6,7},{7,6},{8,9},{9,8},{10,11... | collective-permute-start | bytes 884744 | tf_op jit(solution)/shard_map/ppermute | solution.py:21
  16.1 7.9 %collective-permute-start.7 = (bf16[128,1152]{1,0:T(8,128)(2,1)S(1)}, bf16[128,1152]{1,0:T(8,128)(2,1)S(1)}, u32[]{:S(2)}, u32[]{:S(2)}) collective-permute-start(bf16[128,1152]{1,0:T(8,128)(2,1)S(1)} %shard_map.85.refs_0_), channel_id=1, source_target_pairs={{0,2},{1,3},{2,0},{3,1},{4,6},{5,7},{6,4},{7,5},{8,10},{9,11},{10,... | collective-permute-start | bytes 884744 | tf_op jit(solution)/shard_map/ppermute | solution.py:21
  23.2 9.0 %copy-start = (bf16[1152,3,288]{0,2,1:T(8,128)(2,1)S(1)}, bf16[1152,3,288]{0,2,1:T(8,128)(2,1)}, u32[]{:S(2)}) copy-start(bf16[1152,3,288]{0,2,1:T(8,128)(2,1)} %param.13) | copy-start | bytes 5971972
  23.2 9.0 %copy-start.2 = (f32[2,72]{1,0:T(2,128)S(1)}, f32[2,72]{1,0:T(2,128)}, u32[]{:S(2)}) copy-start(f32[2,72]{1,0:T(2,128)} %gain_ref.5) | copy-start | bytes 1732
  24.0 6.8 %collective-permute-start.11 = (bf16[64,1152]{1,0:T(8,128)(2,1)S(1)}, bf16[64,1152]{1,0:T(8,128)(2,1)S(1)}, u32[]{:S(2)}, u32[]{:S(2)}) collective-permute-start(bf16[64,1152]{1,0:T(8,128)(2,1)S(1)} %get-tuple-element.67), channel_id=1, source_target_pairs={{0,2},{1,3},{2,0},{3,1},{4,6},{5,7},{6,4},{7,5},{8,10},{9,11},{10,... | collective-permute-start | bytes 442376 | tf_op jit(solution)/shard_map/ppermute | solution.py:21
  25.5 6.8 %collective-permute-start.12 = (bf16[64,1152]{1,0:T(8,128)(2,1)S(1)}, bf16[64,1152]{1,0:T(8,128)(2,1)S(1)}, u32[]{:S(2)}, u32[]{:S(2)}) collective-permute-start(bf16[64,1152]{1,0:T(8,128)(2,1)S(1)} %get-tuple-element.68), channel_id=1, source_target_pairs={{0,1},{1,0},{2,3},{3,2},{4,5},{5,4},{6,7},{7,6},{8,9},{9,8},{10,11... | collective-permute-start | bytes 442376 | tf_op jit(solution)/shard_map/ppermute | solution.py:21
  26.9 11.7 %collective-permute-start.10 = (bf16[128,1152]{1,0:T(8,128)(2,1)S(1)}, bf16[128,1152]{1,0:T(8,128)(2,1)S(1)}, u32[]{:S(2)}, u32[]{:S(2)}) collective-permute-start(bf16[128,1152]{1,0:T(8,128)(2,1)S(1)} %shard_map.84.refs_0_), channel_id=1, source_target_pairs={{0,1},{1,0},{2,3},{3,2},{4,5},{5,4},{6,7},{7,6},{8,9},{9,8},{10,11... | collective-permute-start | bytes 884744 | tf_op jit(solution)/shard_map/ppermute | solution.py:21
  27.5 14.7 %collective-permute-start.8 = (bf16[128,1152]{1,0:T(8,128)(2,1)S(1)}, bf16[128,1152]{1,0:T(8,128)(2,1)S(1)}, u32[]{:S(2)}, u32[]{:S(2)}) collective-permute-start(bf16[128,1152]{1,0:T(8,128)(2,1)S(1)} %shard_map.84.refs_0_), channel_id=1, source_target_pairs={{0,2},{1,3},{2,0},{3,1},{4,6},{5,7},{6,4},{7,5},{8,10},{9,11},{10,... | collective-permute-start | bytes 884744 | tf_op jit(solution)/shard_map/ppermute | solution.py:21
  28.1 14.2 %collective-permute-start.9 = (bf16[128,1152]{1,0:T(8,128)(2,1)S(1)}, bf16[128,1152]{1,0:T(8,128)(2,1)S(1)}, u32[]{:S(2)}, u32[]{:S(2)}) collective-permute-start(bf16[128,1152]{1,0:T(8,128)(2,1)S(1)} %shard_map.84.refs_0_), channel_id=1, source_target_pairs={{0,3},{1,2},{2,1},{3,0},{4,7},{5,6},{6,5},{7,4},{8,11},{9,10},{10,... | collective-permute-start | bytes 884744 | tf_op jit(solution)/shard_map/ppermute | solution.py:21
  35.4 7.7 %collective-permute-start.13 = (bf16[144,1152]{1,0:T(8,128)(2,1)S(1)}, bf16[144,1152]{1,0:T(8,128)(2,1)S(1)}, u32[]{:S(2)}, u32[]{:S(2)}) collective-permute-start(bf16[144,1152]{1,0:T(8,128)(2,1)S(1)} %collective-permute-done.4.refs_4_), channel_id=1, source_target_pairs={{0,4},{4,0},{8,12},{12,8},{16,20},{20,16},{24,28},{28,24},{1,5},{5... | collective-permute-start | bytes 995336 | tf_op jit(solution)/shard_map/ppermute | solution.py:21
  35.5 7.6 %collective-permute-start.14 = (bf16[144,1152]{1,0:T(8,128)(2,1)S(1)}, bf16[144,1152]{1,0:T(8,128)(2,1)S(1)}, u32[]{:S(2)}, u32[]{:S(2)}) collective-permute-start(bf16[144,1152]{1,0:T(8,128)(2,1)S(1)} %collective-permute-done.5.refs_6_), channel_id=1, source_target_pairs={{0,4},{4,0},{8,12},{12,8},{16,20},{20,16},{24,28},{28,24},{1,5},{5... | collective-permute-start | bytes 995336 | tf_op jit(solution)/shard_map/ppermute | solution.py:21
  40.7 2.4 %copy-start.3 = (s32[1,4]{1,0:T(1,128)S(1)}, s32[1,4]{1,0:T(1,128)}, u32[]{:S(2)}) copy-start(s32[1,4]{1,0:T(1,128)} %length_ref.3) | copy-start | bytes 52
  40.7 11.5 %collective-permute-start.18 = (bf16[144,1152]{1,0:T(8,128)(2,1)S(1)}, bf16[144,1152]{1,0:T(8,128)(2,1)S(1)}, u32[]{:S(2)}, u32[]{:S(2)}) collective-permute-start(bf16[144,1152]{1,0:T(8,128)(2,1)S(1)} %collective-permute-done.5.refs_6_), channel_id=1, source_target_pairs={{0,1},{1,0},{2,3},{3,2},{4,5},{5,4},{6,7},{7,6},{8,9},{9,8},{10,11... | collective-permute-start | bytes 995336 | tf_op jit(solution)/shard_map/ppermute | solution.py:21
  47.3 6.3 %collective-permute-start.15 = (bf16[288,256]{1,0:T(8,128)(2,1)S(1)}, bf16[288,256]{1,0:T(8,128)(2,1)S(1)}, u32[]{:S(2)}, u32[]{:S(2)}) collective-permute-start(bf16[288,256]{1,0:T(8,128)(2,1)S(1)} %get-tuple-element.91), channel_id=1, source_target_pairs={{0,1},{1,0},{2,3},{3,2},{4,5},{5,4},{6,7},{7,6},{8,9},{9,8},{10,11... | collective-permute-start | bytes 442376 | tf_op jit(solution)/shard_map/ppermute | solution.py:21
  48.8 5.5 %collective-permute-start.16 = (bf16[288,256]{1,0:T(8,128)(2,1)S(1)}, bf16[288,256]{1,0:T(8,128)(2,1)S(1)}, u32[]{:S(2)}, u32[]{:S(2)}) collective-permute-start(bf16[288,256]{1,0:T(8,128)(2,1)S(1)} %get-tuple-element.92), channel_id=1, source_target_pairs={{0,2},{1,3},{2,0},{3,1},{4,6},{5,7},{6,4},{7,5},{8,10},{9,11},{10,... | collective-permute-start | bytes 442376 | tf_op jit(solution)/shard_map/ppermute | solution.py:21
  51.8 6.1 %collective-permute-start.17 = (bf16[288,256]{1,0:T(8,128)(2,1)S(1)}, bf16[288,256]{1,0:T(8,128)(2,1)S(1)}, u32[]{:S(2)}, u32[]{:S(2)}) collective-permute-start(bf16[288,256]{1,0:T(8,128)(2,1)S(1)} %get-tuple-element.98), channel_id=1, source_target_pairs={{0,3},{1,2},{2,1},{3,0},{4,7},{5,6},{6,5},{7,4},{8,11},{9,10},{10,... | collective-permute-start | bytes 442376 | tf_op jit(solution)/shard_map/ppermute | solution.py:21
  52.2 5.7 %collective-permute-start.19 = (bf16[144,1152]{1,0:T(8,128)(2,1)S(1)}, bf16[144,1152]{1,0:T(8,128)(2,1)S(1)}, u32[]{:S(2)}, u32[]{:S(2)}) collective-permute-start(bf16[144,1152]{1,0:T(8,128)(2,1)S(1)} %collective-permute-done.18.refs_1_), channel_id=1, source_target_pairs={{0,4},{4,0},{8,12},{12,8},{16,20},{20,16},{24,28},{28,24},{1,5},{5... | collective-permute-start | bytes 995336 | tf_op jit(solution)/shard_map/ppermute | solution.py:21
  58.5 7.8 %collective-permute-start.24 = (bf16[64,1152]{1,0:T(8,128)(2,1)S(1)}, bf16[64,1152]{1,0:T(8,128)(2,1)S(1)}, u32[]{:S(2)}, u32[]{:S(2)}) collective-permute-start(bf16[64,1152]{1,0:T(8,128)(2,1)S(1)} %get-tuple-element.105), channel_id=1, source_target_pairs={{0,8},{4,12},{8,0},{12,4},{16,24},{20,28},{24,16},{28,20},{1,9},{5... | collective-permute-start | bytes 442376 | tf_op jit(solution)/shard_map/ppermute | solution.py:21
  60.2 6.6 %collective-permute-start.20 = (bf16[32,1152]{1,0:T(8,128)(2,1)S(1)}, bf16[32,1152]{1,0:T(8,128)(2,1)S(1)}, u32[]{:S(2)}, u32[]{:S(2)}) collective-permute-start(bf16[32,1152]{1,0:T(8,128)(2,1)S(1)} %get-tuple-element.100), channel_id=1, source_target_pairs={{0,16},{4,20},{8,24},{12,28},{16,0},{20,4},{24,8},{28,12},{1,17},{... | collective-permute-start | bytes 221192 | tf_op jit(solution)/shard_map/ppermute | solution.py:21
  62.8 10.3 %collective-permute-start.21 = (bf16[32,1152]{1,0:T(8,128)(2,1)S(1)}, bf16[32,1152]{1,0:T(8,128)(2,1)S(1)}, u32[]{:S(2)}, u32[]{:S(2)}) collective-permute-start(bf16[32,1152]{1,0:T(8,128)(2,1)S(1)} %get-tuple-element.101), channel_id=1, source_target_pairs={{0,20},{4,16},{8,28},{12,24},{16,4},{20,0},{24,12},{28,8},{1,21},{... | collective-permute-start | bytes 221192 | tf_op jit(solution)/shard_map/ppermute | solution.py:21
  62.8 10.3 %collective-permute-start.22 = (bf16[32,1152]{1,0:T(8,128)(2,1)S(1)}, bf16[32,1152]{1,0:T(8,128)(2,1)S(1)}, u32[]{:S(2)}, u32[]{:S(2)}) collective-permute-start(bf16[32,1152]{1,0:T(8,128)(2,1)S(1)} %get-tuple-element.102), channel_id=1, source_target_pairs={{0,24},{4,28},{8,16},{12,20},{16,8},{20,12},{24,0},{28,4},{1,25},{... | collective-permute-start | bytes 221192 | tf_op jit(solution)/shard_map/ppermute | solution.py:21
  63.0 10.1 %collective-permute-start.23 = (bf16[32,1152]{1,0:T(8,128)(2,1)S(1)}, bf16[32,1152]{1,0:T(8,128)(2,1)S(1)}, u32[]{:S(2)}, u32[]{:S(2)}) collective-permute-start(bf16[32,1152]{1,0:T(8,128)(2,1)S(1)} %get-tuple-element.103), channel_id=1, source_target_pairs={{0,28},{4,24},{8,20},{12,16},{16,12},{20,8},{24,4},{28,0},{1,29},{... | collective-permute-start | bytes 221192 | tf_op jit(solution)/shard_map/ppermute | solution.py:21
  66.4 6.7 %copy-start.7 = (s32[64]{0:T(128)S(1)}, s32[64]{0:T(128)}, u32[]{:S(2)}) copy-start(s32[64]{0:T(128)} %get-tuple-element.56.slot_ref) | copy-start | bytes 772
  66.4 6.7 %collective-permute-start.25 = (bf16[64,1152]{1,0:T(8,128)(2,1)S(1)}, bf16[64,1152]{1,0:T(8,128)(2,1)S(1)}, u32[]{:S(2)}, u32[]{:S(2)}) collective-permute-start(bf16[64,1152]{1,0:T(8,128)(2,1)S(1)} %shard_map.98), channel_id=1, source_target_pairs={{0,4},{4,0},{8,12},{12,8},{16,20},{20,16},{24,28},{28,24},{1,5},{5... | collective-permute-start | bytes 442376 | tf_op jit(solution)/shard_map/ppermute | solution.py:21

commit v5 on v3

--- a/solution.py
+++ b/solution.py
@@ -196,10 +196,23 @@
         out_ref[clip] = picked.astype(BF16)
 
 
+def chosen_kernel(group_rows, per_peer, piece_rows, owner_ref, place_ref, table_ref, out_ref):
+    rows, tokens = out_ref.shape
+    code = token_codes(
+        tokens, group_rows, per_peer, piece_rows, owner_ref, place_ref, table_ref
+    )
+    row = lax.broadcasted_iota(jnp.int32, (rows, 1), 0)
+    out_ref[...] = jnp.where(code == row, 1.0, 0.0).astype(BF16)
+
+
 def attention_kernel(
     head_size, per_peer, piece_rows, length_ref, owner_ref, place_ref, table_ref, *refs
 ):
-    early_ref, late_ref, out_refs = refs[0], refs[1], refs[2:]
+    early_ref, late_ref, refs = refs[0], refs[1], refs[2:]
+    one_hot_ref = None
+    if refs[0].shape[0] == refs[0].shape[1]:
+        one_hot_ref, refs = refs[0], refs[1:]
+    out_refs = refs
     clips, features, clip_tokens = early_ref.shape
     width, tokens = features // 3, clips * clip_tokens
     seq_count = len(out_refs)
@@ -213,7 +226,10 @@
     scale = math.log2(math.e) / math.sqrt(head_size)
     attended, chosen_by_clip = [], []
     for clip in range(clips):
-        chosen = jnp.where(code == position + clip * clip_tokens, 1.0, 0.0).astype(BF16)
+        if one_hot_ref is not None:
+            chosen = one_hot_ref[clip * clip_tokens : (clip + 1) * clip_tokens]
+        else:
+            chosen = jnp.where(code == position + clip * clip_tokens, 1.0, 0.0).astype(BF16)
         picked = early_ref[clip].astype(F32) + lax.dot_general(
             late_ref[...],
             chosen[:, tokens - late_ref.shape[1] :],
@@ -412,16 +428,27 @@
         )
         return projected
 
-    near, far = [
-        call(
+    def hidden_rows(group, placed):
+        return call(
             functools.partial(norm_kernel, clip_tokens, codes_of(group)),
-            [owner_place, place],
+            [placed, place],
             [clip_pieces, factors] + arrived[group * chips // 2 : (group + 1) * chips // 2],
             [((group_rows, model_width), BF16)],
             flops=(1 + 9 * group) * 10**9,
         )[0]
-        for group in range(2)
-    ]
+
+    near = hidden_rows(0, owner_place)
+    one_hot, placed = [], owner_place
+    if clip_tokens <= 256:
+        _, early = lax.optimization_barrier((near, owner_place))
+        one_hot = call(
+            functools.partial(chosen_kernel, group_rows, per_peer, piece_rows),
+            [early, place, clip_pieces],
+            [],
+            [((clips_here * clip_tokens, clips_here * clip_tokens), BF16)],
+        )
+        one_hot, placed = lax.optimization_barrier((list(one_hot), owner_place))
+    far = hidden_rows(1, placed)
     near, proj_parts = lax.optimization_barrier((near, proj_parts))
     near, proj_parts = lax.optimization_barrier((near, proj_parts))
     sides = {mask: send(near, "seq", mask) for mask in along_y + along_x}
@@ -478,7 +505,7 @@
     attended = call(
         functools.partial(attention_kernel, head_size, per_peer, piece_rows),
         [clip_length, owner_place, place, clip_pieces],
-        [gathered, stacked_late],
+        [gathered, stacked_late] + one_hot,
         [((head_width, rows_here), BF16)] * seq_count,
         limit=16 if clip_tokens <= 256 else 48,
         flops=10**8,

time: 74.3 us -> 74.3 us (level)
  Pallas kernels: 18.3 us -> 19.4 us
  waiting for transfers between devices: 23.2 us -> 22.2 us
    pallas_call x18 -> x19, Pallas kernels: 18.3 us -> 19.4 us  [call(): pl.pallas_call(kernel, in_specs=[smem] * len(scalars) + (where if isinsta...]
    ppermute x26, waiting for transfers between devices: 23.2 us -> 22.2 us  [send(): return lax.ppermute(array, axis, [(i, i ^ mask) for i in range(count)])]
  transfers between devices with their start and end apart: 26 -> 26, of which waited for: 11 -> 11; matrix products, arithmetic and copies ran while one was open for 0% -> 0% of each run, Pallas kernels for 19% -> 21%
where the time goes in v5:
time: 74.3 us; the launch traced here: 73.3 us
  starting transfers between devices  31.4 us (42%)
  waiting for transfers between devices  22.2 us (30%)
  Pallas kernels  19.4 us (26%)
    ppermute x26, starting transfers between devices, send(): return lax.ppermute(array, axis, [(i, i ^ mask) for i in range(count)])  31.4 us
    ppermute x26, waiting for transfers between devices, send(): return lax.ppermute(array, axis, [(i, i ^ mask) for i in range(count)])  22.2 us
    pallas_call x19, Pallas kernels, call(): pl.pallas_call(kernel, in_specs=[smem] * len(scalars) + (where if isinsta...  19.4 us
  transfers between devices with their start and end apart: 26, of which 11 were waited for; matrix products, arithmetic and copies ran while one was open for 0% of the time, Pallas kernels for 21%

profile of v5, /device:TPU:0, one launch (start us, length us, event | category | flops | bytes accessed | tf_op | source)
XLA Modules:
  0.0 73.3 jit_solution(16823483260704077261)
XLA Ops:
  0.0 2.1 %shard_map.82 = (s32[64]{0:T(128)}, bf16[128,1152]{1,0:T(8,128)(2,1)}, bf16[128,1152]{1,0:T(8,128)(2,1)}) custom-call(s32[1]{0:T(128)} %bitcast.place_ref.owner_ref, s32[1,64]{1,0:T(1,128)} %owner_hbm.1, bf16[1,64,4,1152]{3,2,1,0:T(4,128)(2,1)} %token_hbm.1), custom_call_target="tpu_custom_call" | custom-call | flops 30000001024 | bytes 1048576 | tf_op jit(solution)/shard_map/pallas_call | solution.py:353
  2.1 0.5 collective-permute-start
  2.7 0.1 shard_map.87
  2.8 2.6 %collective-permute-start.4 = (bf16[144,1152]{1,0:T(8,128)(2,1)S(1)}, bf16[144,1152]{1,0:T(8,128)(2,1)S(1)}, u32[]{:S(2)}, u32[]{:S(2)}) collective-permute-start(bf16[144,1152]{1,0:T(8,128)(2,1)S(1)} %shard_map.87), channel_id=1, source_target_pairs={{0,1},{1,0},{2,3},{3,2},{4,5},{5,4},{6,7},{7,6},{8,9},{9,8},{10,11... | collective-permute-start | bytes 995336 | tf_op jit(solution)/shard_map/ppermute | solution.py:21
  5.4 1.5 %collective-permute-start.5 = (bf16[144,1152]{1,0:T(8,128)(2,1)S(1)}, bf16[144,1152]{1,0:T(8,128)(2,1)S(1)}, u32[]{:S(2)}, u32[]{:S(2)}) collective-permute-start(bf16[144,1152]{1,0:T(8,128)(2,1)S(1)} %shard_map.87), channel_id=1, source_target_pairs={{0,2},{1,3},{2,0},{3,1},{4,6},{5,7},{6,4},{7,5},{8,10},{9,11},{10,... | collective-permute-start | bytes 995336 | tf_op jit(solution)/shard_map/ppermute | solution.py:21
  6.9 0.0 collective-permute-done.other_ref
  6.9 0.1 shard_map.83
  7.0 1.6 %collective-permute-start.1 = (bf16[64,1152]{1,0:T(8,128)(2,1)S(1)}, bf16[64,1152]{1,0:T(8,128)(2,1)S(1)}, u32[]{:S(2)}, u32[]{:S(2)}) collective-permute-start(bf16[64,1152]{1,0:T(8,128)(2,1)S(1)} %get-tuple-element.62), channel_id=1, source_target_pairs={{0,8},{4,12},{8,0},{12,4},{16,24},{20,28},{24,16},{28,20},{1,9},{5... | collective-permute-start | bytes 442376 | tf_op jit(solution)/shard_map/ppermute | solution.py:21
  8.7 2.6 %collective-permute-start.2 = (bf16[64,1152]{1,0:T(8,128)(2,1)S(1)}, bf16[64,1152]{1,0:T(8,128)(2,1)S(1)}, u32[]{:S(2)}, u32[]{:S(2)}) collective-permute-start(bf16[64,1152]{1,0:T(8,128)(2,1)S(1)} %get-tuple-element.65), channel_id=1, source_target_pairs={{0,16},{4,20},{8,24},{12,28},{16,0},{20,4},{24,8},{28,12},{1,17},{... | collective-permute-start | bytes 442376 | tf_op jit(solution)/shard_map/ppermute | solution.py:21
  11.3 0.2 collective-permute-start.3
  11.5 3.4 %collective-permute-done.1.refs_1_ = bf16[64,1152]{1,0:T(8,128)(2,1)S(1)} collective-permute-done((bf16[64,1152]{1,0:T(8,128)(2,1)S(1)}, bf16[64,1152]{1,0:T(8,128)(2,1)S(1)}, u32[]{:S(2)}, u32[]{:S(2)}) %collective-permute-start.1) | collective-permute-done | bytes 147488 | tf_op jit(solution)/shard_map/ppermute | solution.py:21
  14.9 0.6 shard_map.84.refs_0_
  15.5 0.0 collective-permute-done.4.refs_4_
  15.5 0.6 collective-permute-start.6
  16.1 1.5 %collective-permute-start.7 = (bf16[128,1152]{1,0:T(8,128)(2,1)S(1)}, bf16[128,1152]{1,0:T(8,128)(2,1)S(1)}, u32[]{:S(2)}, u32[]{:S(2)}) collective-permute-start(bf16[128,1152]{1,0:T(8,128)(2,1)S(1)} %shard_map.84.refs_0_), channel_id=1, source_target_pairs={{0,2},{1,3},{2,0},{3,1},{4,6},{5,7},{6,4},{7,5},{8,10},{9,11},{10,... | collective-permute-start | bytes 884744 | tf_op jit(solution)/shard_map/ppermute | solution.py:21
  17.6 1.1 %shard_map.85.refs_2_ = bf16[1024,1024]{1,0:T(8,128)(2,1)S(1)} custom-call(s32[1]{0:T(128)} %bitcast.place_ref.owner_ref, s32[1]{0:T(128)} %bitcast.2.place_ref, s32[1,4,16]{2,1,0:T(4,128)S(1)} %copy-done.1), custom_call_target="tpu_custom_call" | custom-call | flops 1000000000 | bytes 1048576 | tf_op jit(solution)/shard_map/pallas_call | solution.py:353
  18.7 4.0 %collective-permute-done.2.refs_0_.refs_2_ = bf16[64,1152]{1,0:T(8,128)(2,1)S(1)} collective-permute-done((bf16[64,1152]{1,0:T(8,128)(2,1)S(1)}, bf16[64,1152]{1,0:T(8,128)(2,1)S(1)}, u32[]{:S(2)}, u32[]{:S(2)}) %collective-permute-start.2) | collective-permute-done | bytes 147488 | tf_op jit(solution)/shard_map/ppermute | solution.py:21
  22.7 0.0 collective-permute-done.3.refs_1_.refs_3_
  22.7 0.6 shard_map.86.refs_0_
  23.2 0.0 copy-start
  23.2 0.0 copy-start.2
  23.3 0.3 collective-permute-done.6.refs_0_.refs_1_
  23.6 0.4 collective-permute-done.7.refs_1_.refs_2_
  24.0 1.4 %collective-permute-start.10 = (bf16[64,1152]{1,0:T(8,128)(2,1)S(1)}, bf16[64,1152]{1,0:T(8,128)(2,1)S(1)}, u32[]{:S(2)}, u32[]{:S(2)}) collective-permute-start(bf16[64,1152]{1,0:T(8,128)(2,1)S(1)} %get-tuple-element.72), channel_id=1, source_target_pairs={{0,1},{1,0},{2,3},{3,2},{4,5},{5,4},{6,7},{7,6},{8,9},{9,8},{10,11... | collective-permute-start | bytes 442376 | tf_op jit(solution)/shard_map/ppermute | solution.py:21
  25.4 1.5 %collective-permute-start.9 = (bf16[64,1152]{1,0:T(8,128)(2,1)S(1)}, bf16[64,1152]{1,0:T(8,128)(2,1)S(1)}, u32[]{:S(2)}, u32[]{:S(2)}) collective-permute-start(bf16[64,1152]{1,0:T(8,128)(2,1)S(1)} %get-tuple-element.71), channel_id=1, source_target_pairs={{0,2},{1,3},{2,0},{3,1},{4,6},{5,7},{6,4},{7,5},{8,10},{9,11},{10,... | collective-permute-start | bytes 442376 | tf_op jit(solution)/shard_map/ppermute | solution.py:21
  26.9 0.6 collective-permute-start.8
  27.5 0.6 collective-permute-start.11
  28.1 2.3 %collective-permute-start.12 = (bf16[128,1152]{1,0:T(8,128)(2,1)S(1)}, bf16[128,1152]{1,0:T(8,128)(2,1)S(1)}, u32[]{:S(2)}, u32[]{:S(2)}) collective-permute-start(bf16[128,1152]{1,0:T(8,128)(2,1)S(1)} %shard_map.86.refs_0_), channel_id=1, source_target_pairs={{0,3},{1,2},{2,1},{3,0},{4,7},{5,6},{6,5},{7,4},{8,11},{9,10},{10,... | collective-permute-start | bytes 884744 | tf_op jit(solution)/shard_map/ppermute | solution.py:21
  30.4 0.3 collective-permute-done.10.refs_4_
  30.7 1.4 %collective-permute-done.9.refs_3_ = bf16[64,1152]{1,0:T(8,128)(2,1)S(1)} collective-permute-done((bf16[64,1152]{1,0:T(8,128)(2,1)S(1)}, bf16[64,1152]{1,0:T(8,128)(2,1)S(1)}, u32[]{:S(2)}, u32[]{:S(2)}) %collective-permute-start.9) | collective-permute-done | bytes 147488 | tf_op jit(solution)/shard_map/ppermute | solution.py:21
  32.1 1.4 %shard_map.89.stacked_ref = bf16[864,512]{1,0:T(8,128)(2,1)S(1)} custom-call(bf16[864,1152]{1,0:T(8,128)(2,1)S(1)} %bitcast.9, f32[2,72]{1,0:T(2,128)S(1)} %copy-done.2, bf16[128,1152]{1,0:T(8,128)(2,1)S(1)} %shard_map.84.refs_0_, bf16[128,1152]{1,0:T(8,128)(2,1)S(1)} %collective-permute-done.6.refs_0_.refs_1_, ...), custom_call_target="tpu_custom_call" | custom-call | flops 3000000000 | bytes 1048576 | tf_op jit(solution)/shard_map/pallas_call | solution.py:353
  33.5 0.0 copy-start.3
  33.5 1.8 %shard_map.90.refs_0_ = bf16[4,864,256]{2,1,0:T(8,128)(2,1)S(1)} custom-call(s32[1]{0:T(128)} %bitcast.place_ref.owner_ref, s32[1]{0:T(128)} %bitcast.2.place_ref, s32[1,4,16]{2,1,0:T(4,128)S(1)} %copy-done.1, bf16[864,512]{1,0:T(8,128)(2,1)S(1)} %shard_map.89.stacked_ref), custom_call_target="tpu_custom_call" | custom-call | flops 3000000000 | bytes 1048576 | tf_op jit(solution)/shard_map/pallas_call | solution.py:353
  35.3 0.1 collective-permute-start.13
  35.4 0.5 collective-permute-start.14
  35.9 1.3 %shard_map.91 = (bf16[256,1152]{1,0:T(8,128)(2,1)S(1)}, bf16[256,1152]{1,0:T(8,128)(2,1)S(1)}) custom-call(s32[1,4]{1,0:T(1,128)S(1)} %copy-done.3, s32[1]{0:T(128)} %bitcast.place_ref.owner_ref, s32[1]{0:T(128)} %bitcast.2.place_ref, s32[1,4,16]{2,1,0:T(4,128)S(1)} %copy-done.1, bf16[3,4,1152]{2,1,0:T(4,128)(2,1)S(1)} %bitcast.14, ...), custom_call_target="tpu_custom_call" | custom-call | flops 1000000000 | bytes 1048576 | tf_op jit(solution)/shard_map/pallas_call | solution.py:353
  37.1 0.8 %shard_map.92.stacked_ref = bf16[864,256]{1,0:T(8,128)(2,1)S(1)} custom-call(bf16[864,1152]{1,0:T(8,128)(2,1)S(1)} %bitcast.10, f32[2,72]{1,0:T(2,128)S(1)} %copy-done.2, bf16[128,1152]{1,0:T(8,128)(2,1)S(1)} %shard_map.86.refs_0_, bf16[128,1152]{1,0:T(8,128)(2,1)S(1)} %collective-permute-done.8.refs_1_), custom_call_target="tpu_custom_call" | custom-call | flops 3000000000 | bytes 1048576 | tf_op jit(solution)/shard_map/pallas_call | solution.py:353
  37.9 1.3 %shard_map.93.refs_0_ = bf16[4,864,256]{2,1,0:T(8,128)(2,1)S(1)} custom-call(s32[1]{0:T(128)} %bitcast.place_ref.owner_ref, s32[1]{0:T(128)} %bitcast.2.place_ref, s32[1,4,16]{2,1,0:T(4,128)S(1)} %copy-done.1, bf16[864,256]{1,0:T(8,128)(2,1)S(1)} %shard_map.92.stacked_ref, bf16[4,864,256]{2,1,0:T(8,128)(2,1)S(1)} %shard_map.90.refs_0_), custom_call_target="tpu_custom_call" | custom-call | flops 3000000000 | bytes 1048576 | tf_op jit(solution)/shard_map/pallas_call | solution.py:353
  39.2 1.4 %collective-permute-start.18 = (bf16[144,1152]{1,0:T(8,128)(2,1)S(1)}, bf16[144,1152]{1,0:T(8,128)(2,1)S(1)}, u32[]{:S(2)}, u32[]{:S(2)}) collective-permute-start(bf16[144,1152]{1,0:T(8,128)(2,1)S(1)} %collective-permute-done.5.refs_6_), channel_id=1, source_target_pairs={{0,1},{1,0},{2,3},{3,2},{4,5},{5,4},{6,7},{7,6},{8,9},{9,8},{10,11... | collective-permute-start | bytes 995336 | tf_op jit(solution)/shard_map/ppermute | solution.py:21
  40.6 1.0 %collective-permute-done.11.refs_0_ = bf16[128,1152]{1,0:T(8,128)(2,1)S(1)} collective-permute-done((bf16[128,1152]{1,0:T(8,128)(2,1)S(1)}, bf16[128,1152]{1,0:T(8,128)(2,1)S(1)}, u32[]{:S(2)}, u32[]{:S(2)}) %collective-permute-start.11) | collective-permute-done | bytes 294944 | tf_op jit(solution)/shard_map/ppermute | solution.py:21
  41.6 0.0 collective-permute-done.12.refs_1_
  41.6 0.8 %shard_map.94.refs_1_ = bf16[864,256]{1,0:T(8,128)(2,1)S(1)} custom-call(bf16[864,1152]{1,0:T(8,128)(2,1)S(1)} %bitcast.11, f32[2,72]{1,0:T(2,128)S(1)} %copy-done.2, bf16[128,1152]{1,0:T(8,128)(2,1)S(1)} %collective-permute-done.11.refs_0_, bf16[128,1152]{1,0:T(8,128)(2,1)S(1)} %collective-permute-done.12.refs_1_), custom_call_target="tpu_custom_call" | custom-call | flops 100000000 | bytes 1048576 | tf_op jit(solution)/shard_map/pallas_call | solution.py:353
  42.4 0.0 collective-permute-done.13.refs_5_
  42.4 0.0 collective-permute-done.14.refs_7_
  42.4 4.1 %shard_map.95 = (bf16[288,256]{1,0:T(8,128)(2,1)S(1)}, bf16[288,256]{1,0:T(8,128)(2,1)S(1)}, bf16[288,256]{1,0:T(8,128)(2,1)S(1)}, bf16[288,256]{1,0:T(8,128)(2,1)S(1)}) custom-call(s32[1,4]{1,0:T(1,128)S(1)} %copy-done.3, s32[1]{0:T(128)} %bitcast.place_ref.owner_ref, s32[1]{0:T(128)} %bitcast.2.place_ref, s32[1,4,16]{2,1,0:T(4,128)S(1)} %copy-done.1, ...), custom_call_target="tpu_custom_call" | custom-call | flops 100000000 | bytes 1048576 | tf_op jit(solution)/shard_map/pallas_call | solution.py:353
  46.5 1.5 %collective-permute-start.15 = (bf16[288,256]{1,0:T(8,128)(2,1)S(1)}, bf16[288,256]{1,0:T(8,128)(2,1)S(1)}, u32[]{:S(2)}, u32[]{:S(2)}) collective-permute-start(bf16[288,256]{1,0:T(8,128)(2,1)S(1)} %get-tuple-element.96), channel_id=1, source_target_pairs={{0,1},{1,0},{2,3},{3,2},{4,5},{5,4},{6,7},{7,6},{8,9},{9,8},{10,11... | collective-permute-start | bytes 442376 | tf_op jit(solution)/shard_map/ppermute | solution.py:21
  48.1 0.7 collective-permute-start.16
  48.7 1.4 %collective-permute-start.17 = (bf16[288,256]{1,0:T(8,128)(2,1)S(1)}, bf16[288,256]{1,0:T(8,128)(2,1)S(1)}, u32[]{:S(2)}, u32[]{:S(2)}) collective-permute-start(bf16[288,256]{1,0:T(8,128)(2,1)S(1)} %get-tuple-element.102), channel_id=1, source_target_pairs={{0,3},{1,2},{2,1},{3,0},{4,7},{5,6},{6,5},{7,4},{8,11},{9,10},{10,... | collective-permute-start | bytes 442376 | tf_op jit(solution)/shard_map/ppermute | solution.py:21
  50.1 0.0 collective-permute-done.18.refs_1_
  50.1 0.0 collective-permute-start.19
  50.1 3.3 %collective-permute-done.15.refs_1_ = bf16[288,256]{1,0:T(8,128)(2,1)S(1)} collective-permute-done((bf16[288,256]{1,0:T(8,128)(2,1)S(1)}, bf16[288,256]{1,0:T(8,128)(2,1)S(1)}, u32[]{:S(2)}, u32[]{:S(2)}) %collective-permute-start.15) | collective-permute-done | bytes 147488 | tf_op jit(solution)/shard_map/ppermute | solution.py:21
  53.4 0.9 %collective-permute-done.16.refs_2_ = bf16[288,256]{1,0:T(8,128)(2,1)S(1)} collective-permute-done((bf16[288,256]{1,0:T(8,128)(2,1)S(1)}, bf16[288,256]{1,0:T(8,128)(2,1)S(1)}, u32[]{:S(2)}, u32[]{:S(2)}) %collective-permute-start.16) | collective-permute-done | bytes 147488 | tf_op jit(solution)/shard_map/ppermute | solution.py:21
  54.3 1.2 %shard_map.96.partial_ref = f32[256,1152]{1,0:T(8,128)S(1)} custom-call(s32[1]{0:T(128)} %bitcast.1.core_ref, bf16[288,256]{1,0:T(8,128)(2,1)S(1)} %get-tuple-element.95.refs_0_, bf16[288,256]{1,0:T(8,128)(2,1)S(1)} %collective-permute-done.15.refs_1_, bf16[288,256]{1,0:T(8,128)(2,1)S(1)} %collective-permute-done.16.refs_2_, ...), custom_call_target="tpu_custom_call" | custom-call | flops 10000000000 | bytes 1048576 | tf_op jit(solution)/shard_map/pallas_call | solution.py:353
  55.5 0.9 %collective-permute-done.17.refs_0_ = bf16[288,256]{1,0:T(8,128)(2,1)S(1)} collective-permute-done((bf16[288,256]{1,0:T(8,128)(2,1)S(1)}, bf16[288,256]{1,0:T(8,128)(2,1)S(1)}, u32[]{:S(2)}, u32[]{:S(2)}) %collective-permute-start.17) | collective-permute-done | bytes 147488 | tf_op jit(solution)/shard_map/ppermute | solution.py:21
  56.4 0.0 collective-permute-done.19.refs_2_
  56.4 0.6 shard_map.97
  57.1 1.6 %collective-permute-start.24 = (bf16[64,1152]{1,0:T(8,128)(2,1)S(1)}, bf16[64,1152]{1,0:T(8,128)(2,1)S(1)}, u32[]{:S(2)}, u32[]{:S(2)}) collective-permute-start(bf16[64,1152]{1,0:T(8,128)(2,1)S(1)} %get-tuple-element.109), channel_id=1, source_target_pairs={{0,8},{4,12},{8,0},{12,4},{16,24},{20,28},{24,16},{28,20},{1,9},{5... | collective-permute-start | bytes 442376 | tf_op jit(solution)/shard_map/ppermute | solution.py:21
  58.7 2.6 %collective-permute-start.20 = (bf16[32,1152]{1,0:T(8,128)(2,1)S(1)}, bf16[32,1152]{1,0:T(8,128)(2,1)S(1)}, u32[]{:S(2)}, u32[]{:S(2)}) collective-permute-start(bf16[32,1152]{1,0:T(8,128)(2,1)S(1)} %get-tuple-element.104), channel_id=1, source_target_pairs={{0,16},{4,20},{8,24},{12,28},{16,0},{20,4},{24,8},{28,12},{1,17},{... | collective-permute-start | bytes 221192 | tf_op jit(solution)/shard_map/ppermute | solution.py:21
  61.3 1.3 %collective-permute-start.22 = (bf16[32,1152]{1,0:T(8,128)(2,1)S(1)}, bf16[32,1152]{1,0:T(8,128)(2,1)S(1)}, u32[]{:S(2)}, u32[]{:S(2)}) collective-permute-start(bf16[32,1152]{1,0:T(8,128)(2,1)S(1)} %get-tuple-element.106), channel_id=1, source_target_pairs={{0,24},{4,28},{8,16},{12,20},{16,8},{20,12},{24,0},{28,4},{1,25},{... | collective-permute-start | bytes 221192 | tf_op jit(solution)/shard_map/ppermute | solution.py:21
  62.5 2.7 %collective-permute-start.23 = (bf16[32,1152]{1,0:T(8,128)(2,1)S(1)}, bf16[32,1152]{1,0:T(8,128)(2,1)S(1)}, u32[]{:S(2)}, u32[]{:S(2)}) collective-permute-start(bf16[32,1152]{1,0:T(8,128)(2,1)S(1)} %get-tuple-element.107), channel_id=1, source_target_pairs={{0,28},{4,24},{8,20},{12,16},{16,12},{20,8},{24,4},{28,0},{1,29},{... | collective-permute-start | bytes 221192 | tf_op jit(solution)/shard_map/ppermute | solution.py:21
  65.2 0.2 collective-permute-start.25
  65.4 6.3 %collective-permute-done.21.refs_1_ = bf16[32,1152]{1,0:T(8,128)(2,1)S(1)} collective-permute-done((bf16[32,1152]{1,0:T(8,128)(2,1)S(1)}, bf16[32,1152]{1,0:T(8,128)(2,1)S(1)}, u32[]{:S(2)}, u32[]{:S(2)}) %collective-permute-start.21) | collective-permute-done | bytes 73760 | tf_op jit(solution)/shard_map/ppermute | solution.py:21
  71.7 0.0 collective-permute-done.22.refs_2_
  71.8 1.5 %shard_map.100 = bf16[1,64,4,1152]{3,2,1,0:T(4,128)(2,1)} custom-call(s32[64]{0:T(128)S(1)} %copy-done.7, bf16[128,1152]{1,0:T(8,128)(2,1)S(1)} %shard_map.98.refs_0_, bf16[64,1152]{1,0:T(8,128)(2,1)S(1)} %collective-permute-done.25.refs_1_, bf16[32,1152]{1,0:T(8,128)(2,1)S(1)} %get-tuple-element.110.refs_2_, ...), custom_call_target="tpu_custom_call" | custom-call | flops 1000000000 | bytes 1048576 | tf_op jit(solution)/shard_map/pallas_call | solution.py:353
  (23 shorter events, 0.1 us)
Async XLA Ops:
  0.0 2.7 %copy-start.4 = (bf16[288,1152]{1,0:T(8,128)(2,1)S(1)}, bf16[288,1152]{1,0:T(8,128)(2,1)}, u32[]{:S(2)}) copy-start(bf16[288,1152]{1,0:T(8,128)(2,1)} %refs_3_.1) | copy-start | bytes 1990660
  2.1 4.8 %collective-permute-start = (bf16[128,1152]{1,0:T(8,128)(2,1)}, bf16[128,1152]{1,0:T(8,128)(2,1)S(1)}, u32[]{:S(2)}, u32[]{:S(2)}) collective-permute-start(bf16[128,1152]{1,0:T(8,128)(2,1)} %get-tuple-element.60), channel_id=1, source_target_pairs={{0,4},{4,0},{8,12},{12,8},{16,20},{20,16},{24,28},{28,24},{1,5},{5... | collective-permute-start | bytes 884744 | tf_op jit(solution)/shard_map/ppermute | solution.py:21
  2.7 4.2 %copy-start.6 = (bf16[128,1152]{1,0:T(8,128)(2,1)S(1)}, bf16[128,1152]{1,0:T(8,128)(2,1)}, u32[]{:S(2)}) copy-start(bf16[128,1152]{1,0:T(8,128)(2,1)} %get-tuple-element.59.own_hbm) | copy-start | bytes 884740
  2.8 12.7 %collective-permute-start.4 = (bf16[144,1152]{1,0:T(8,128)(2,1)S(1)}, bf16[144,1152]{1,0:T(8,128)(2,1)S(1)}, u32[]{:S(2)}, u32[]{:S(2)}) collective-permute-start(bf16[144,1152]{1,0:T(8,128)(2,1)S(1)} %shard_map.87), channel_id=1, source_target_pairs={{0,1},{1,0},{2,3},{3,2},{4,5},{5,4},{6,7},{7,6},{8,9},{9,8},{10,11... | collective-permute-start | bytes 995336 | tf_op jit(solution)/shard_map/ppermute | solution.py:21
  5.4 10.1 %collective-permute-start.5 = (bf16[144,1152]{1,0:T(8,128)(2,1)S(1)}, bf16[144,1152]{1,0:T(8,128)(2,1)S(1)}, u32[]{:S(2)}, u32[]{:S(2)}) collective-permute-start(bf16[144,1152]{1,0:T(8,128)(2,1)S(1)} %shard_map.87), channel_id=1, source_target_pairs={{0,2},{1,3},{2,0},{3,1},{4,6},{5,7},{6,4},{7,5},{8,10},{9,11},{10,... | collective-permute-start | bytes 995336 | tf_op jit(solution)/shard_map/ppermute | solution.py:21
  6.9 8.0 %copy-start.1 = (s32[1,4,16]{2,1,0:T(4,128)S(1)}, s32[1,4,16]{2,1,0:T(4,128)}, u32[]{:S(2)}) copy-start(s32[1,4,16]{2,1,0:T(4,128)} %table_ref.13) | copy-start | bytes 772
  6.9 8.0 %copy-start.5 = (bf16[1,4,3,1152]{3,1,2,0:T(4,128)(2,1)S(1)}, bf16[1,4,3,1152]{3,1,2,0:T(4,128)(2,1)}, u32[]{:S(2)}) copy-start(bf16[1,4,3,1152]{3,1,2,0:T(4,128)(2,1)} %param.12) | copy-start | bytes 82948
  7.0 7.9 %collective-permute-start.1 = (bf16[64,1152]{1,0:T(8,128)(2,1)S(1)}, bf16[64,1152]{1,0:T(8,128)(2,1)S(1)}, u32[]{:S(2)}, u32[]{:S(2)}) collective-permute-start(bf16[64,1152]{1,0:T(8,128)(2,1)S(1)} %get-tuple-element.62), channel_id=1, source_target_pairs={{0,8},{4,12},{8,0},{12,4},{16,24},{20,28},{24,16},{28,20},{1,9},{5... | collective-permute-start | bytes 442376 | tf_op jit(solution)/shard_map/ppermute | solution.py:21
  8.7 14.0 %collective-permute-start.2 = (bf16[64,1152]{1,0:T(8,128)(2,1)S(1)}, bf16[64,1152]{1,0:T(8,128)(2,1)S(1)}, u32[]{:S(2)}, u32[]{:S(2)}) collective-permute-start(bf16[64,1152]{1,0:T(8,128)(2,1)S(1)} %get-tuple-element.65), channel_id=1, source_target_pairs={{0,16},{4,20},{8,24},{12,28},{16,0},{20,4},{24,8},{28,12},{1,17},{... | collective-permute-start | bytes 442376 | tf_op jit(solution)/shard_map/ppermute | solution.py:21
  11.3 11.4 %collective-permute-start.3 = (bf16[64,1152]{1,0:T(8,128)(2,1)S(1)}, bf16[64,1152]{1,0:T(8,128)(2,1)S(1)}, u32[]{:S(2)}, u32[]{:S(2)}) collective-permute-start(bf16[64,1152]{1,0:T(8,128)(2,1)S(1)} %get-tuple-element.66), channel_id=1, source_target_pairs={{0,24},{4,28},{8,16},{12,20},{16,8},{20,12},{24,0},{28,4},{1,25},{... | collective-permute-start | bytes 442376 | tf_op jit(solution)/shard_map/ppermute | solution.py:21
  15.5 8.1 %collective-permute-start.6 = (bf16[128,1152]{1,0:T(8,128)(2,1)S(1)}, bf16[128,1152]{1,0:T(8,128)(2,1)S(1)}, u32[]{:S(2)}, u32[]{:S(2)}) collective-permute-start(bf16[128,1152]{1,0:T(8,128)(2,1)S(1)} %shard_map.84.refs_0_), channel_id=1, source_target_pairs={{0,1},{1,0},{2,3},{3,2},{4,5},{5,4},{6,7},{7,6},{8,9},{9,8},{10,11... | collective-permute-start | bytes 884744 | tf_op jit(solution)/shard_map/ppermute | solution.py:21
  16.1 7.9 %collective-permute-start.7 = (bf16[128,1152]{1,0:T(8,128)(2,1)S(1)}, bf16[128,1152]{1,0:T(8,128)(2,1)S(1)}, u32[]{:S(2)}, u32[]{:S(2)}) collective-permute-start(bf16[128,1152]{1,0:T(8,128)(2,1)S(1)} %shard_map.84.refs_0_), channel_id=1, source_target_pairs={{0,2},{1,3},{2,0},{3,1},{4,6},{5,7},{6,4},{7,5},{8,10},{9,11},{10,... | collective-permute-start | bytes 884744 | tf_op jit(solution)/shard_map/ppermute | solution.py:21
  23.2 8.9 %copy-start = (bf16[1152,3,288]{0,2,1:T(8,128)(2,1)S(1)}, bf16[1152,3,288]{0,2,1:T(8,128)(2,1)}, u32[]{:S(2)}) copy-start(bf16[1152,3,288]{0,2,1:T(8,128)(2,1)} %param.13) | copy-start | bytes 5971972
  23.2 8.9 %copy-start.2 = (f32[2,72]{1,0:T(2,128)S(1)}, f32[2,72]{1,0:T(2,128)}, u32[]{:S(2)}) copy-start(f32[2,72]{1,0:T(2,128)} %gain_ref.5) | copy-start | bytes 1732
  24.0 6.7 %collective-permute-start.10 = (bf16[64,1152]{1,0:T(8,128)(2,1)S(1)}, bf16[64,1152]{1,0:T(8,128)(2,1)S(1)}, u32[]{:S(2)}, u32[]{:S(2)}) collective-permute-start(bf16[64,1152]{1,0:T(8,128)(2,1)S(1)} %get-tuple-element.72), channel_id=1, source_target_pairs={{0,1},{1,0},{2,3},{3,2},{4,5},{5,4},{6,7},{7,6},{8,9},{9,8},{10,11... | collective-permute-start | bytes 442376 | tf_op jit(solution)/shard_map/ppermute | solution.py:21
  25.4 6.7 %collective-permute-start.9 = (bf16[64,1152]{1,0:T(8,128)(2,1)S(1)}, bf16[64,1152]{1,0:T(8,128)(2,1)S(1)}, u32[]{:S(2)}, u32[]{:S(2)}) collective-permute-start(bf16[64,1152]{1,0:T(8,128)(2,1)S(1)} %get-tuple-element.71), channel_id=1, source_target_pairs={{0,2},{1,3},{2,0},{3,1},{4,6},{5,7},{6,4},{7,5},{8,10},{9,11},{10,... | collective-permute-start | bytes 442376 | tf_op jit(solution)/shard_map/ppermute | solution.py:21
  26.9 10.2 %collective-permute-start.8 = (bf16[128,1152]{1,0:T(8,128)(2,1)S(1)}, bf16[128,1152]{1,0:T(8,128)(2,1)S(1)}, u32[]{:S(2)}, u32[]{:S(2)}) collective-permute-start(bf16[128,1152]{1,0:T(8,128)(2,1)S(1)} %shard_map.86.refs_0_), channel_id=1, source_target_pairs={{0,1},{1,0},{2,3},{3,2},{4,5},{5,4},{6,7},{7,6},{8,9},{9,8},{10,11... | collective-permute-start | bytes 884744 | tf_op jit(solution)/shard_map/ppermute | solution.py:21
  27.5 14.1 %collective-permute-start.11 = (bf16[128,1152]{1,0:T(8,128)(2,1)S(1)}, bf16[128,1152]{1,0:T(8,128)(2,1)S(1)}, u32[]{:S(2)}, u32[]{:S(2)}) collective-permute-start(bf16[128,1152]{1,0:T(8,128)(2,1)S(1)} %shard_map.86.refs_0_), channel_id=1, source_target_pairs={{0,2},{1,3},{2,0},{3,1},{4,6},{5,7},{6,4},{7,5},{8,10},{9,11},{10,... | collective-permute-start | bytes 884744 | tf_op jit(solution)/shard_map/ppermute | solution.py:21
  28.1 13.5 %collective-permute-start.12 = (bf16[128,1152]{1,0:T(8,128)(2,1)S(1)}, bf16[128,1152]{1,0:T(8,128)(2,1)S(1)}, u32[]{:S(2)}, u32[]{:S(2)}) collective-permute-start(bf16[128,1152]{1,0:T(8,128)(2,1)S(1)} %shard_map.86.refs_0_), channel_id=1, source_target_pairs={{0,3},{1,2},{2,1},{3,0},{4,7},{5,6},{6,5},{7,4},{8,11},{9,10},{10,... | collective-permute-start | bytes 884744 | tf_op jit(solution)/shard_map/ppermute | solution.py:21
  33.5 2.4 %copy-start.3 = (s32[1,4]{1,0:T(1,128)S(1)}, s32[1,4]{1,0:T(1,128)}, u32[]{:S(2)}) copy-start(s32[1,4]{1,0:T(1,128)} %length_ref.3) | copy-start | bytes 52
  35.3 7.1 %collective-permute-start.13 = (bf16[144,1152]{1,0:T(8,128)(2,1)S(1)}, bf16[144,1152]{1,0:T(8,128)(2,1)S(1)}, u32[]{:S(2)}, u32[]{:S(2)}) collective-permute-start(bf16[144,1152]{1,0:T(8,128)(2,1)S(1)} %collective-permute-done.4.refs_4_), channel_id=1, source_target_pairs={{0,4},{4,0},{8,12},{12,8},{16,20},{20,16},{24,28},{28,24},{1,5},{5... | collective-permute-start | bytes 995336 | tf_op jit(solution)/shard_map/ppermute | solution.py:21
  35.4 7.0 %collective-permute-start.14 = (bf16[144,1152]{1,0:T(8,128)(2,1)S(1)}, bf16[144,1152]{1,0:T(8,128)(2,1)S(1)}, u32[]{:S(2)}, u32[]{:S(2)}) collective-permute-start(bf16[144,1152]{1,0:T(8,128)(2,1)S(1)} %collective-permute-done.5.refs_6_), channel_id=1, source_target_pairs={{0,4},{4,0},{8,12},{12,8},{16,20},{20,16},{24,28},{28,24},{1,5},{5... | collective-permute-start | bytes 995336 | tf_op jit(solution)/shard_map/ppermute | solution.py:21
  39.2 10.9 %collective-permute-start.18 = (bf16[144,1152]{1,0:T(8,128)(2,1)S(1)}, bf16[144,1152]{1,0:T(8,128)(2,1)S(1)}, u32[]{:S(2)}, u32[]{:S(2)}) collective-permute-start(bf16[144,1152]{1,0:T(8,128)(2,1)S(1)} %collective-permute-done.5.refs_6_), channel_id=1, source_target_pairs={{0,1},{1,0},{2,3},{3,2},{4,5},{5,4},{6,7},{7,6},{8,9},{9,8},{10,11... | collective-permute-start | bytes 995336 | tf_op jit(solution)/shard_map/ppermute | solution.py:21
  46.5 6.9 %collective-permute-start.15 = (bf16[288,256]{1,0:T(8,128)(2,1)S(1)}, bf16[288,256]{1,0:T(8,128)(2,1)S(1)}, u32[]{:S(2)}, u32[]{:S(2)}) collective-permute-start(bf16[288,256]{1,0:T(8,128)(2,1)S(1)} %get-tuple-element.96), channel_id=1, source_target_pairs={{0,1},{1,0},{2,3},{3,2},{4,5},{5,4},{6,7},{7,6},{8,9},{9,8},{10,11... | collective-permute-start | bytes 442376 | tf_op jit(solution)/shard_map/ppermute | solution.py:21
  48.1 6.2 %collective-permute-start.16 = (bf16[288,256]{1,0:T(8,128)(2,1)S(1)}, bf16[288,256]{1,0:T(8,128)(2,1)S(1)}, u32[]{:S(2)}, u32[]{:S(2)}) collective-permute-start(bf16[288,256]{1,0:T(8,128)(2,1)S(1)} %get-tuple-element.97), channel_id=1, source_target_pairs={{0,2},{1,3},{2,0},{3,1},{4,6},{5,7},{6,4},{7,5},{8,10},{9,11},{10,... | collective-permute-start | bytes 442376 | tf_op jit(solution)/shard_map/ppermute | solution.py:21
  48.7 7.7 %collective-permute-start.17 = (bf16[288,256]{1,0:T(8,128)(2,1)S(1)}, bf16[288,256]{1,0:T(8,128)(2,1)S(1)}, u32[]{:S(2)}, u32[]{:S(2)}) collective-permute-start(bf16[288,256]{1,0:T(8,128)(2,1)S(1)} %get-tuple-element.102), channel_id=1, source_target_pairs={{0,3},{1,2},{2,1},{3,0},{4,7},{5,6},{6,5},{7,4},{8,11},{9,10},{10,... | collective-permute-start | bytes 442376 | tf_op jit(solution)/shard_map/ppermute | solution.py:21
  50.1 6.3 %collective-permute-start.19 = (bf16[144,1152]{1,0:T(8,128)(2,1)S(1)}, bf16[144,1152]{1,0:T(8,128)(2,1)S(1)}, u32[]{:S(2)}, u32[]{:S(2)}) collective-permute-start(bf16[144,1152]{1,0:T(8,128)(2,1)S(1)} %collective-permute-done.18.refs_1_), channel_id=1, source_target_pairs={{0,4},{4,0},{8,12},{12,8},{16,20},{20,16},{24,28},{28,24},{1,5},{5... | collective-permute-start | bytes 995336 | tf_op jit(solution)/shard_map/ppermute | solution.py:21
  57.1 8.2 %collective-permute-start.24 = (bf16[64,1152]{1,0:T(8,128)(2,1)S(1)}, bf16[64,1152]{1,0:T(8,128)(2,1)S(1)}, u32[]{:S(2)}, u32[]{:S(2)}) collective-permute-start(bf16[64,1152]{1,0:T(8,128)(2,1)S(1)} %get-tuple-element.109), channel_id=1, source_target_pairs={{0,8},{4,12},{8,0},{12,4},{16,24},{20,28},{24,16},{28,20},{1,9},{5... | collective-permute-start | bytes 442376 | tf_op jit(solution)/shard_map/ppermute | solution.py:21
  58.7 6.7 %collective-permute-start.20 = (bf16[32,1152]{1,0:T(8,128)(2,1)S(1)}, bf16[32,1152]{1,0:T(8,128)(2,1)S(1)}, u32[]{:S(2)}, u32[]{:S(2)}) collective-permute-start(bf16[32,1152]{1,0:T(8,128)(2,1)S(1)} %get-tuple-element.104), channel_id=1, source_target_pairs={{0,16},{4,20},{8,24},{12,28},{16,0},{20,4},{24,8},{28,12},{1,17},{... | collective-permute-start | bytes 221192 | tf_op jit(solution)/shard_map/ppermute | solution.py:21
  61.3 10.4 %collective-permute-start.21 = (bf16[32,1152]{1,0:T(8,128)(2,1)S(1)}, bf16[32,1152]{1,0:T(8,128)(2,1)S(1)}, u32[]{:S(2)}, u32[]{:S(2)}) collective-permute-start(bf16[32,1152]{1,0:T(8,128)(2,1)S(1)} %get-tuple-element.105), channel_id=1, source_target_pairs={{0,20},{4,16},{8,28},{12,24},{16,4},{20,0},{24,12},{28,8},{1,21},{... | collective-permute-start | bytes 221192 | tf_op jit(solution)/shard_map/ppermute | solution.py:21
  61.3 10.4 %collective-permute-start.22 = (bf16[32,1152]{1,0:T(8,128)(2,1)S(1)}, bf16[32,1152]{1,0:T(8,128)(2,1)S(1)}, u32[]{:S(2)}, u32[]{:S(2)}) collective-permute-start(bf16[32,1152]{1,0:T(8,128)(2,1)S(1)} %get-tuple-element.106), channel_id=1, source_target_pairs={{0,24},{4,28},{8,16},{12,20},{16,8},{20,12},{24,0},{28,4},{1,25},{... | collective-permute-start | bytes 221192 | tf_op jit(solution)/shard_map/ppermute | solution.py:21
  62.5 9.2 %collective-permute-start.23 = (bf16[32,1152]{1,0:T(8,128)(2,1)S(1)}, bf16[32,1152]{1,0:T(8,128)(2,1)S(1)}, u32[]{:S(2)}, u32[]{:S(2)}) collective-permute-start(bf16[32,1152]{1,0:T(8,128)(2,1)S(1)} %get-tuple-element.107), channel_id=1, source_target_pairs={{0,28},{4,24},{8,20},{12,16},{16,12},{20,8},{24,4},{28,0},{1,29},{... | collective-permute-start | bytes 221192 | tf_op jit(solution)/shard_map/ppermute | solution.py:21
  65.2 6.5 %copy-start.7 = (s32[64]{0:T(128)S(1)}, s32[64]{0:T(128)}, u32[]{:S(2)}) copy-start(s32[64]{0:T(128)} %get-tuple-element.58.slot_ref) | copy-start | bytes 772
  65.2 6.5 %collective-permute-start.25 = (bf16[64,1152]{1,0:T(8,128)(2,1)S(1)}, bf16[64,1152]{1,0:T(8,128)(2,1)S(1)}, u32[]{:S(2)}, u32[]{:S(2)}) collective-permute-start(bf16[64,1152]{1,0:T(8,128)(2,1)S(1)} %shard_map.99), channel_id=1, source_target_pairs={{0,4},{4,0},{8,12},{12,8},{16,20},{20,16},{24,28},{28,24},{1,5},{5... | collective-permute-start | bytes 442376 | tf_op jit(solution)/shard_map/ppermute | solution.py:21

commit v6 on v5

--- a/solution.py
+++ b/solution.py
@@ -182,12 +182,17 @@
 ):
     out_ref = refs[-1]
     clips, _, clip_tokens = out_ref.shape
+    one_hot_ref, refs = (refs[0], refs[1:]) if len(refs[0].shape) == 2 else (None, refs)
+    columns = slice(first, first + stacked_ref.shape[1])
     code = token_codes(
         clips * clip_tokens, group_rows, per_peer, piece_rows, owner_ref, place_ref, table_ref
     )[:, first : first + stacked_ref.shape[1]]
     position = lax.broadcasted_iota(jnp.int32, (clip_tokens, 1), 0)
     for clip in range(clips):
-        chosen = jnp.where(code == position + clip * clip_tokens, 1.0, 0.0).astype(BF16)
+        if one_hot_ref is not None:
+            chosen = one_hot_ref[clip * clip_tokens : (clip + 1) * clip_tokens, columns]
+        else:
+            chosen = jnp.where(code == position + clip * clip_tokens, 1.0, 0.0).astype(BF16)
         picked = lax.dot_general(
             stacked_ref[...], chosen, (((1,), (1,)), ((), ())), preferred_element_type=F32
         )
@@ -474,7 +479,7 @@
         (gathered,) = call(
             functools.partial(gather_kernel, first, group_rows, per_peer, piece_rows),
             [owner_place, place, clip_pieces],
-            list(arrays),
+            [arrays[0], *one_hot, *arrays[1:]],
             [((clips_here, 3 * head_width, clip_tokens), BF16)],
             limit=16 if clip_tokens <= 256 else 48,
             flops=3 * 10**9,

time: 74.3 us -> 74.7 us (level); the launches traced: 73.3 us -> 74.5 us
  waiting for transfers between devices: 22.2 us -> 23.5 us
    ppermute x26, waiting for transfers between devices: 22.2 us -> 23.5 us  [send(): return lax.ppermute(array, axis, [(i, i ^ mask) for i in range(count)])]
  transfers between devices with their start and end apart: 26 -> 26, of which waited for: 11 -> 10; matrix products, arithmetic and copies ran while one was open for 0% -> 0% of each run, Pallas kernels for 21% -> 20%
where the time goes in v6:
time: 74.7 us; the launch traced here: 74.5 us
  starting transfers between devices  31.5 us (42%)
  waiting for transfers between devices  23.5 us (31%)
  Pallas kernels  19.2 us (26%)
    ppermute x26, starting transfers between devices, send(): return lax.ppermute(array, axis, [(i, i ^ mask) for i in range(count)])  31.5 us
    ppermute x26, waiting for transfers between devices, send(): return lax.ppermute(array, axis, [(i, i ^ mask) for i in range(count)])  23.5 us
    pallas_call x19, Pallas kernels, call(): pl.pallas_call(kernel, in_specs=[smem] * len(scalars) + (where if isinsta...  19.2 us
  transfers between devices with their start and end apart: 26, of which 10 were waited for; matrix products, arithmetic and copies ran while one was open for 0% of the time, Pallas kernels for 20%

profile of v6, /device:TPU:0, one launch (start us, length us, event | category | flops | bytes accessed | tf_op | source)
XLA Modules:
  0.0 74.5 jit_solution(6992069561465619335)
XLA Ops:
  0.0 2.1 %shard_map.82 = (s32[64]{0:T(128)}, bf16[128,1152]{1,0:T(8,128)(2,1)}, bf16[128,1152]{1,0:T(8,128)(2,1)}) custom-call(s32[1]{0:T(128)} %bitcast.place_ref.owner_ref, s32[1,64]{1,0:T(1,128)} %owner_hbm.1, bf16[1,64,4,1152]{3,2,1,0:T(4,128)(2,1)} %token_hbm.1), custom_call_target="tpu_custom_call" | custom-call | flops 30000001024 | bytes 1048576 | tf_op jit(solution)/shard_map/pallas_call | solution.py:358
  2.1 0.5 collective-permute-start
  2.7 0.1 shard_map.87
  2.8 2.6 %collective-permute-start.4 = (bf16[144,1152]{1,0:T(8,128)(2,1)S(1)}, bf16[144,1152]{1,0:T(8,128)(2,1)S(1)}, u32[]{:S(2)}, u32[]{:S(2)}) collective-permute-start(bf16[144,1152]{1,0:T(8,128)(2,1)S(1)} %shard_map.87), channel_id=1, source_target_pairs={{0,1},{1,0},{2,3},{3,2},{4,5},{5,4},{6,7},{7,6},{8,9},{9,8},{10,11... | collective-permute-start | bytes 995336 | tf_op jit(solution)/shard_map/ppermute | solution.py:21
  5.4 1.5 %collective-permute-start.5 = (bf16[144,1152]{1,0:T(8,128)(2,1)S(1)}, bf16[144,1152]{1,0:T(8,128)(2,1)S(1)}, u32[]{:S(2)}, u32[]{:S(2)}) collective-permute-start(bf16[144,1152]{1,0:T(8,128)(2,1)S(1)} %shard_map.87), channel_id=1, source_target_pairs={{0,2},{1,3},{2,0},{3,1},{4,6},{5,7},{6,4},{7,5},{8,10},{9,11},{10,... | collective-permute-start | bytes 995336 | tf_op jit(solution)/shard_map/ppermute | solution.py:21
  6.9 0.0 collective-permute-done.other_ref
  6.9 0.1 shard_map.83
  7.0 1.6 %collective-permute-start.1 = (bf16[64,1152]{1,0:T(8,128)(2,1)S(1)}, bf16[64,1152]{1,0:T(8,128)(2,1)S(1)}, u32[]{:S(2)}, u32[]{:S(2)}) collective-permute-start(bf16[64,1152]{1,0:T(8,128)(2,1)S(1)} %get-tuple-element.62), channel_id=1, source_target_pairs={{0,8},{4,12},{8,0},{12,4},{16,24},{20,28},{24,16},{28,20},{1,9},{5... | collective-permute-start | bytes 442376 | tf_op jit(solution)/shard_map/ppermute | solution.py:21
  8.7 2.6 %collective-permute-start.2 = (bf16[64,1152]{1,0:T(8,128)(2,1)S(1)}, bf16[64,1152]{1,0:T(8,128)(2,1)S(1)}, u32[]{:S(2)}, u32[]{:S(2)}) collective-permute-start(bf16[64,1152]{1,0:T(8,128)(2,1)S(1)} %get-tuple-element.65), channel_id=1, source_target_pairs={{0,16},{4,20},{8,24},{12,28},{16,0},{20,4},{24,8},{28,12},{1,17},{... | collective-permute-start | bytes 442376 | tf_op jit(solution)/shard_map/ppermute | solution.py:21
  11.3 0.2 collective-permute-start.3
  11.5 3.4 %collective-permute-done.1.refs_1_ = bf16[64,1152]{1,0:T(8,128)(2,1)S(1)} collective-permute-done((bf16[64,1152]{1,0:T(8,128)(2,1)S(1)}, bf16[64,1152]{1,0:T(8,128)(2,1)S(1)}, u32[]{:S(2)}, u32[]{:S(2)}) %collective-permute-start.1) | collective-permute-done | bytes 147488 | tf_op jit(solution)/shard_map/ppermute | solution.py:21
  14.9 0.6 shard_map.84.refs_0_
  15.5 0.0 collective-permute-done.4.refs_4_
  15.5 0.0 collective-permute-done.5.refs_6_
  15.5 0.6 collective-permute-start.6
  16.1 1.5 %collective-permute-start.7 = (bf16[128,1152]{1,0:T(8,128)(2,1)S(1)}, bf16[128,1152]{1,0:T(8,128)(2,1)S(1)}, u32[]{:S(2)}, u32[]{:S(2)}) collective-permute-start(bf16[128,1152]{1,0:T(8,128)(2,1)S(1)} %shard_map.84.refs_0_), channel_id=1, source_target_pairs={{0,2},{1,3},{2,0},{3,1},{4,6},{5,7},{6,4},{7,5},{8,10},{9,11},{10,... | collective-permute-start | bytes 884744 | tf_op jit(solution)/shard_map/ppermute | solution.py:21
  17.6 1.1 %shard_map.85.refs_0_.refs_2_ = bf16[1024,1024]{1,0:T(8,128)(2,1)S(1)} custom-call(s32[1]{0:T(128)} %bitcast.place_ref.owner_ref, s32[1]{0:T(128)} %bitcast.2.place_ref, s32[1,4,16]{2,1,0:T(4,128)S(1)} %copy-done.1), custom_call_target="tpu_custom_call" | custom-call | flops 1000000000 | bytes 1048576 | tf_op jit(solution)/shard_map/pallas_call | solution.py:358
  18.7 4.0 %collective-permute-done.2.refs_0_.refs_2_ = bf16[64,1152]{1,0:T(8,128)(2,1)S(1)} collective-permute-done((bf16[64,1152]{1,0:T(8,128)(2,1)S(1)}, bf16[64,1152]{1,0:T(8,128)(2,1)S(1)}, u32[]{:S(2)}, u32[]{:S(2)}) %collective-permute-start.2) | collective-permute-done | bytes 147488 | tf_op jit(solution)/shard_map/ppermute | solution.py:21
  22.7 0.0 collective-permute-done.3.refs_1_.refs_3_
  22.7 0.6 shard_map.86.refs_0_
  23.2 0.0 copy-start
  23.2 0.0 copy-start.2
  23.3 0.3 collective-permute-done.6.refs_0_.refs_1_
  23.6 0.4 collective-permute-done.7.refs_1_.refs_2_
  24.0 1.4 %collective-permute-start.10 = (bf16[64,1152]{1,0:T(8,128)(2,1)S(1)}, bf16[64,1152]{1,0:T(8,128)(2,1)S(1)}, u32[]{:S(2)}, u32[]{:S(2)}) collective-permute-start(bf16[64,1152]{1,0:T(8,128)(2,1)S(1)} %get-tuple-element.72), channel_id=1, source_target_pairs={{0,1},{1,0},{2,3},{3,2},{4,5},{5,4},{6,7},{7,6},{8,9},{9,8},{10,11... | collective-permute-start | bytes 442376 | tf_op jit(solution)/shard_map/ppermute | solution.py:21
  25.4 1.5 %collective-permute-start.9 = (bf16[64,1152]{1,0:T(8,128)(2,1)S(1)}, bf16[64,1152]{1,0:T(8,128)(2,1)S(1)}, u32[]{:S(2)}, u32[]{:S(2)}) collective-permute-start(bf16[64,1152]{1,0:T(8,128)(2,1)S(1)} %get-tuple-element.71), channel_id=1, source_target_pairs={{0,2},{1,3},{2,0},{3,1},{4,6},{5,7},{6,4},{7,5},{8,10},{9,11},{10,... | collective-permute-start | bytes 442376 | tf_op jit(solution)/shard_map/ppermute | solution.py:21
  26.9 0.6 collective-permute-start.8
  27.5 0.6 collective-permute-start.11
  28.1 2.3 %collective-permute-start.12 = (bf16[128,1152]{1,0:T(8,128)(2,1)S(1)}, bf16[128,1152]{1,0:T(8,128)(2,1)S(1)}, u32[]{:S(2)}, u32[]{:S(2)}) collective-permute-start(bf16[128,1152]{1,0:T(8,128)(2,1)S(1)} %shard_map.86.refs_0_), channel_id=1, source_target_pairs={{0,3},{1,2},{2,1},{3,0},{4,7},{5,6},{6,5},{7,4},{8,11},{9,10},{10,... | collective-permute-start | bytes 884744 | tf_op jit(solution)/shard_map/ppermute | solution.py:21
  30.4 0.3 collective-permute-done.10.refs_4_
  30.7 1.4 %collective-permute-done.9.refs_3_ = bf16[64,1152]{1,0:T(8,128)(2,1)S(1)} collective-permute-done((bf16[64,1152]{1,0:T(8,128)(2,1)S(1)}, bf16[64,1152]{1,0:T(8,128)(2,1)S(1)}, u32[]{:S(2)}, u32[]{:S(2)}) %collective-permute-start.9) | collective-permute-done | bytes 147488 | tf_op jit(solution)/shard_map/ppermute | solution.py:21
  32.1 1.4 %shard_map.89.stacked_ref = bf16[864,512]{1,0:T(8,128)(2,1)S(1)} custom-call(bf16[864,1152]{1,0:T(8,128)(2,1)S(1)} %bitcast.9, f32[2,72]{1,0:T(2,128)S(1)} %copy-done.2, bf16[128,1152]{1,0:T(8,128)(2,1)S(1)} %shard_map.84.refs_0_, bf16[128,1152]{1,0:T(8,128)(2,1)S(1)} %collective-permute-done.6.refs_0_.refs_1_, ...), custom_call_target="tpu_custom_call" | custom-call | flops 3000000000 | bytes 1048576 | tf_op jit(solution)/shard_map/pallas_call | solution.py:358
  33.5 0.0 copy-start.3
  33.5 1.7 %shard_map.90.refs_1_ = bf16[4,864,256]{2,1,0:T(8,128)(2,1)S(1)} custom-call(s32[1]{0:T(128)} %bitcast.place_ref.owner_ref, s32[1]{0:T(128)} %bitcast.2.place_ref, s32[1,4,16]{2,1,0:T(4,128)S(1)} %copy-done.1, bf16[864,512]{1,0:T(8,128)(2,1)S(1)} %shard_map.89.stacked_ref, bf16[1024,1024]{1,0:T(8,128)(2,1)S(1)} %shard_map.85.refs_0_.refs_2_), custom_call_target="tpu_custom_call" | custom-call | flops 3000000000 | bytes 1048576 | tf_op jit(solution)/shard_map/pallas_call | solution.py:358
  35.2 0.1 collective-permute-start.13
  35.3 0.5 collective-permute-start.14
  35.8 1.3 %shard_map.91 = (bf16[256,1152]{1,0:T(8,128)(2,1)S(1)}, bf16[256,1152]{1,0:T(8,128)(2,1)S(1)}) custom-call(s32[1,4]{1,0:T(1,128)S(1)} %copy-done.3, s32[1]{0:T(128)} %bitcast.place_ref.owner_ref, s32[1]{0:T(128)} %bitcast.2.place_ref, s32[1,4,16]{2,1,0:T(4,128)S(1)} %copy-done.1, bf16[3,4,1152]{2,1,0:T(4,128)(2,1)S(1)} %bitcast.14, ...), custom_call_target="tpu_custom_call" | custom-call | flops 1000000000 | bytes 1048576 | tf_op jit(solution)/shard_map/pallas_call | solution.py:358
  37.0 0.0 collective-permute-done.8.refs_1_
  37.0 0.8 %shard_map.92.stacked_ref = bf16[864,256]{1,0:T(8,128)(2,1)S(1)} custom-call(bf16[864,1152]{1,0:T(8,128)(2,1)S(1)} %bitcast.10, f32[2,72]{1,0:T(2,128)S(1)} %copy-done.2, bf16[128,1152]{1,0:T(8,128)(2,1)S(1)} %shard_map.86.refs_0_, bf16[128,1152]{1,0:T(8,128)(2,1)S(1)} %collective-permute-done.8.refs_1_), custom_call_target="tpu_custom_call" | custom-call | flops 3000000000 | bytes 1048576 | tf_op jit(solution)/shard_map/pallas_call | solution.py:358
  37.8 1.3 %shard_map.93.refs_0_ = bf16[4,864,256]{2,1,0:T(8,128)(2,1)S(1)} custom-call(s32[1]{0:T(128)} %bitcast.place_ref.owner_ref, s32[1]{0:T(128)} %bitcast.2.place_ref, s32[1,4,16]{2,1,0:T(4,128)S(1)} %copy-done.1, bf16[864,256]{1,0:T(8,128)(2,1)S(1)} %shard_map.92.stacked_ref, bf16[1024,1024]{1,0:T(8,128)(2,1)S(1)} %shard_map.85.refs_0_.refs_2_, ...), custom_call_target="tpu_custom_call" | custom-call | flops 3000000000 | bytes 1048576 | tf_op jit(solution)/shard_map/pallas_call | solution.py:358
  39.1 1.5 %collective-permute-start.18 = (bf16[144,1152]{1,0:T(8,128)(2,1)S(1)}, bf16[144,1152]{1,0:T(8,128)(2,1)S(1)}, u32[]{:S(2)}, u32[]{:S(2)}) collective-permute-start(bf16[144,1152]{1,0:T(8,128)(2,1)S(1)} %collective-permute-done.5.refs_6_), channel_id=1, source_target_pairs={{0,1},{1,0},{2,3},{3,2},{4,5},{5,4},{6,7},{7,6},{8,9},{9,8},{10,11... | collective-permute-start | bytes 995336 | tf_op jit(solution)/shard_map/ppermute | solution.py:21
  40.6 1.0 %collective-permute-done.11.refs_0_ = bf16[128,1152]{1,0:T(8,128)(2,1)S(1)} collective-permute-done((bf16[128,1152]{1,0:T(8,128)(2,1)S(1)}, bf16[128,1152]{1,0:T(8,128)(2,1)S(1)}, u32[]{:S(2)}, u32[]{:S(2)}) %collective-permute-start.11) | collective-permute-done | bytes 294944 | tf_op jit(solution)/shard_map/ppermute | solution.py:21
  41.6 0.0 collective-permute-done.12.refs_1_
  41.6 0.8 %shard_map.94.refs_1_ = bf16[864,256]{1,0:T(8,128)(2,1)S(1)} custom-call(bf16[864,1152]{1,0:T(8,128)(2,1)S(1)} %bitcast.11, f32[2,72]{1,0:T(2,128)S(1)} %copy-done.2, bf16[128,1152]{1,0:T(8,128)(2,1)S(1)} %collective-permute-done.11.refs_0_, bf16[128,1152]{1,0:T(8,128)(2,1)S(1)} %collective-permute-done.12.refs_1_), custom_call_target="tpu_custom_call" | custom-call | flops 100000000 | bytes 1048576 | tf_op jit(solution)/shard_map/pallas_call | solution.py:358
  42.4 0.0 collective-permute-done.13.refs_5_
  42.4 4.1 %shard_map.95 = (bf16[288,256]{1,0:T(8,128)(2,1)S(1)}, bf16[288,256]{1,0:T(8,128)(2,1)S(1)}, bf16[288,256]{1,0:T(8,128)(2,1)S(1)}, bf16[288,256]{1,0:T(8,128)(2,1)S(1)}) custom-call(s32[1,4]{1,0:T(1,128)S(1)} %copy-done.3, s32[1]{0:T(128)} %bitcast.place_ref.owner_ref, s32[1]{0:T(128)} %bitcast.2.place_ref, s32[1,4,16]{2,1,0:T(4,128)S(1)} %copy-done.1, ...), custom_call_target="tpu_custom_call" | custom-call | flops 100000000 | bytes 1048576 | tf_op jit(solution)/shard_map/pallas_call | solution.py:358
  46.6 1.5 %collective-permute-start.15 = (bf16[288,256]{1,0:T(8,128)(2,1)S(1)}, bf16[288,256]{1,0:T(8,128)(2,1)S(1)}, u32[]{:S(2)}, u32[]{:S(2)}) collective-permute-start(bf16[288,256]{1,0:T(8,128)(2,1)S(1)} %get-tuple-element.96), channel_id=1, source_target_pairs={{0,1},{1,0},{2,3},{3,2},{4,5},{5,4},{6,7},{7,6},{8,9},{9,8},{10,11... | collective-permute-start | bytes 442376 | tf_op jit(solution)/shard_map/ppermute | solution.py:21
  48.1 0.7 collective-permute-start.16
  48.8 1.3 %collective-permute-start.17 = (bf16[288,256]{1,0:T(8,128)(2,1)S(1)}, bf16[288,256]{1,0:T(8,128)(2,1)S(1)}, u32[]{:S(2)}, u32[]{:S(2)}) collective-permute-start(bf16[288,256]{1,0:T(8,128)(2,1)S(1)} %get-tuple-element.102), channel_id=1, source_target_pairs={{0,3},{1,2},{2,1},{3,0},{4,7},{5,6},{6,5},{7,4},{8,11},{9,10},{10,... | collective-permute-start | bytes 442376 | tf_op jit(solution)/shard_map/ppermute | solution.py:21
  50.1 3.3 %collective-permute-done.15.refs_1_ = bf16[288,256]{1,0:T(8,128)(2,1)S(1)} collective-permute-done((bf16[288,256]{1,0:T(8,128)(2,1)S(1)}, bf16[288,256]{1,0:T(8,128)(2,1)S(1)}, u32[]{:S(2)}, u32[]{:S(2)}) %collective-permute-start.15) | collective-permute-done | bytes 147488 | tf_op jit(solution)/shard_map/ppermute | solution.py:21
  53.4 3.0 %collective-permute-done.16.refs_2_ = bf16[288,256]{1,0:T(8,128)(2,1)S(1)} collective-permute-done((bf16[288,256]{1,0:T(8,128)(2,1)S(1)}, bf16[288,256]{1,0:T(8,128)(2,1)S(1)}, u32[]{:S(2)}, u32[]{:S(2)}) %collective-permute-start.16) | collective-permute-done | bytes 147488 | tf_op jit(solution)/shard_map/ppermute | solution.py:21
  56.4 1.2 %shard_map.96.partial_ref = f32[256,1152]{1,0:T(8,128)S(1)} custom-call(s32[1]{0:T(128)} %bitcast.1.core_ref, bf16[288,256]{1,0:T(8,128)(2,1)S(1)} %get-tuple-element.95.refs_0_, bf16[288,256]{1,0:T(8,128)(2,1)S(1)} %collective-permute-done.15.refs_1_, bf16[288,256]{1,0:T(8,128)(2,1)S(1)} %collective-permute-done.16.refs_2_, ...), custom_call_target="tpu_custom_call" | custom-call | flops 10000000000 | bytes 1048576 | tf_op jit(solution)/shard_map/pallas_call | solution.py:358
  57.6 0.0 collective-permute-done.17.refs_0_
  57.6 0.6 shard_map.97
  58.3 1.7 %collective-permute-start.24 = (bf16[64,1152]{1,0:T(8,128)(2,1)S(1)}, bf16[64,1152]{1,0:T(8,128)(2,1)S(1)}, u32[]{:S(2)}, u32[]{:S(2)}) collective-permute-start(bf16[64,1152]{1,0:T(8,128)(2,1)S(1)} %get-tuple-element.109), channel_id=1, source_target_pairs={{0,8},{4,12},{8,0},{12,4},{16,24},{20,28},{24,16},{28,20},{1,9},{5... | collective-permute-start | bytes 442376 | tf_op jit(solution)/shard_map/ppermute | solution.py:21
  59.9 2.6 %collective-permute-start.20 = (bf16[32,1152]{1,0:T(8,128)(2,1)S(1)}, bf16[32,1152]{1,0:T(8,128)(2,1)S(1)}, u32[]{:S(2)}, u32[]{:S(2)}) collective-permute-start(bf16[32,1152]{1,0:T(8,128)(2,1)S(1)} %get-tuple-element.104), channel_id=1, source_target_pairs={{0,16},{4,20},{8,24},{12,28},{16,0},{20,4},{24,8},{28,12},{1,17},{... | collective-permute-start | bytes 221192 | tf_op jit(solution)/shard_map/ppermute | solution.py:21
  62.5 0.0 collective-permute-start.21
  62.5 0.2 collective-permute-start.22
  62.7 3.4 %collective-permute-start.23 = (bf16[32,1152]{1,0:T(8,128)(2,1)S(1)}, bf16[32,1152]{1,0:T(8,128)(2,1)S(1)}, u32[]{:S(2)}, u32[]{:S(2)}) collective-permute-start(bf16[32,1152]{1,0:T(8,128)(2,1)S(1)} %get-tuple-element.107), channel_id=1, source_target_pairs={{0,28},{4,24},{8,20},{12,16},{16,12},{20,8},{24,4},{28,0},{1,29},{... | collective-permute-start | bytes 221192 | tf_op jit(solution)/shard_map/ppermute | solution.py:21
  66.2 0.4 collective-permute-start.25
  66.6 0.0 collective-permute-done.20.refs_0_
  66.6 6.3 %collective-permute-done.21.refs_1_ = bf16[32,1152]{1,0:T(8,128)(2,1)S(1)} collective-permute-done((bf16[32,1152]{1,0:T(8,128)(2,1)S(1)}, bf16[32,1152]{1,0:T(8,128)(2,1)S(1)}, u32[]{:S(2)}, u32[]{:S(2)}) %collective-permute-start.21) | collective-permute-done | bytes 73760 | tf_op jit(solution)/shard_map/ppermute | solution.py:21
  73.0 0.0 collective-permute-done.25.refs_1_
  73.0 1.5 %shard_map.100 = bf16[1,64,4,1152]{3,2,1,0:T(4,128)(2,1)} custom-call(s32[64]{0:T(128)S(1)} %copy-done.7, bf16[128,1152]{1,0:T(8,128)(2,1)S(1)} %shard_map.98.refs_0_, bf16[64,1152]{1,0:T(8,128)(2,1)S(1)} %collective-permute-done.25.refs_1_, bf16[32,1152]{1,0:T(8,128)(2,1)S(1)} %get-tuple-element.110.refs_2_, ...), custom_call_target="tpu_custom_call" | custom-call | flops 1000000000 | bytes 1048576 | tf_op jit(solution)/shard_map/pallas_call | solution.py:358
  (23 shorter events, 0.1 us)
Async XLA Ops:
  0.0 2.7 %copy-start.4 = (bf16[288,1152]{1,0:T(8,128)(2,1)S(1)}, bf16[288,1152]{1,0:T(8,128)(2,1)}, u32[]{:S(2)}) copy-start(bf16[288,1152]{1,0:T(8,128)(2,1)} %refs_3_.1) | copy-start | bytes 1990660
  2.1 4.8 %collective-permute-start = (bf16[128,1152]{1,0:T(8,128)(2,1)}, bf16[128,1152]{1,0:T(8,128)(2,1)S(1)}, u32[]{:S(2)}, u32[]{:S(2)}) collective-permute-start(bf16[128,1152]{1,0:T(8,128)(2,1)} %get-tuple-element.60), channel_id=1, source_target_pairs={{0,4},{4,0},{8,12},{12,8},{16,20},{20,16},{24,28},{28,24},{1,5},{5... | collective-permute-start | bytes 884744 | tf_op jit(solution)/shard_map/ppermute | solution.py:21
  2.7 4.2 %copy-start.6 = (bf16[128,1152]{1,0:T(8,128)(2,1)S(1)}, bf16[128,1152]{1,0:T(8,128)(2,1)}, u32[]{:S(2)}) copy-start(bf16[128,1152]{1,0:T(8,128)(2,1)} %get-tuple-element.59.own_hbm) | copy-start | bytes 884740
  2.8 12.7 %collective-permute-start.4 = (bf16[144,1152]{1,0:T(8,128)(2,1)S(1)}, bf16[144,1152]{1,0:T(8,128)(2,1)S(1)}, u32[]{:S(2)}, u32[]{:S(2)}) collective-permute-start(bf16[144,1152]{1,0:T(8,128)(2,1)S(1)} %shard_map.87), channel_id=1, source_target_pairs={{0,1},{1,0},{2,3},{3,2},{4,5},{5,4},{6,7},{7,6},{8,9},{9,8},{10,11... | collective-permute-start | bytes 995336 | tf_op jit(solution)/shard_map/ppermute | solution.py:21
  5.4 10.1 %collective-permute-start.5 = (bf16[144,1152]{1,0:T(8,128)(2,1)S(1)}, bf16[144,1152]{1,0:T(8,128)(2,1)S(1)}, u32[]{:S(2)}, u32[]{:S(2)}) collective-permute-start(bf16[144,1152]{1,0:T(8,128)(2,1)S(1)} %shard_map.87), channel_id=1, source_target_pairs={{0,2},{1,3},{2,0},{3,1},{4,6},{5,7},{6,4},{7,5},{8,10},{9,11},{10,... | collective-permute-start | bytes 995336 | tf_op jit(solution)/shard_map/ppermute | solution.py:21
  6.9 8.0 %copy-start.1 = (s32[1,4,16]{2,1,0:T(4,128)S(1)}, s32[1,4,16]{2,1,0:T(4,128)}, u32[]{:S(2)}) copy-start(s32[1,4,16]{2,1,0:T(4,128)} %table_ref.13) | copy-start | bytes 772
  6.9 8.0 %copy-start.5 = (bf16[1,4,3,1152]{3,1,2,0:T(4,128)(2,1)S(1)}, bf16[1,4,3,1152]{3,1,2,0:T(4,128)(2,1)}, u32[]{:S(2)}) copy-start(bf16[1,4,3,1152]{3,1,2,0:T(4,128)(2,1)} %param.12) | copy-start | bytes 82948
  7.0 7.9 %collective-permute-start.1 = (bf16[64,1152]{1,0:T(8,128)(2,1)S(1)}, bf16[64,1152]{1,0:T(8,128)(2,1)S(1)}, u32[]{:S(2)}, u32[]{:S(2)}) collective-permute-start(bf16[64,1152]{1,0:T(8,128)(2,1)S(1)} %get-tuple-element.62), channel_id=1, source_target_pairs={{0,8},{4,12},{8,0},{12,4},{16,24},{20,28},{24,16},{28,20},{1,9},{5... | collective-permute-start | bytes 442376 | tf_op jit(solution)/shard_map/ppermute | solution.py:21
  8.7 14.0 %collective-permute-start.2 = (bf16[64,1152]{1,0:T(8,128)(2,1)S(1)}, bf16[64,1152]{1,0:T(8,128)(2,1)S(1)}, u32[]{:S(2)}, u32[]{:S(2)}) collective-permute-start(bf16[64,1152]{1,0:T(8,128)(2,1)S(1)} %get-tuple-element.65), channel_id=1, source_target_pairs={{0,16},{4,20},{8,24},{12,28},{16,0},{20,4},{24,8},{28,12},{1,17},{... | collective-permute-start | bytes 442376 | tf_op jit(solution)/shard_map/ppermute | solution.py:21
  11.3 11.4 %collective-permute-start.3 = (bf16[64,1152]{1,0:T(8,128)(2,1)S(1)}, bf16[64,1152]{1,0:T(8,128)(2,1)S(1)}, u32[]{:S(2)}, u32[]{:S(2)}) collective-permute-start(bf16[64,1152]{1,0:T(8,128)(2,1)S(1)} %get-tuple-element.66), channel_id=1, source_target_pairs={{0,24},{4,28},{8,16},{12,20},{16,8},{20,12},{24,0},{28,4},{1,25},{... | collective-permute-start | bytes 442376 | tf_op jit(solution)/shard_map/ppermute | solution.py:21
  15.5 8.1 %collective-permute-start.6 = (bf16[128,1152]{1,0:T(8,128)(2,1)S(1)}, bf16[128,1152]{1,0:T(8,128)(2,1)S(1)}, u32[]{:S(2)}, u32[]{:S(2)}) collective-permute-start(bf16[128,1152]{1,0:T(8,128)(2,1)S(1)} %shard_map.84.refs_0_), channel_id=1, source_target_pairs={{0,1},{1,0},{2,3},{3,2},{4,5},{5,4},{6,7},{7,6},{8,9},{9,8},{10,11... | collective-permute-start | bytes 884744 | tf_op jit(solution)/shard_map/ppermute | solution.py:21
  16.1 7.9 %collective-permute-start.7 = (bf16[128,1152]{1,0:T(8,128)(2,1)S(1)}, bf16[128,1152]{1,0:T(8,128)(2,1)S(1)}, u32[]{:S(2)}, u32[]{:S(2)}) collective-permute-start(bf16[128,1152]{1,0:T(8,128)(2,1)S(1)} %shard_map.84.refs_0_), channel_id=1, source_target_pairs={{0,2},{1,3},{2,0},{3,1},{4,6},{5,7},{6,4},{7,5},{8,10},{9,11},{10,... | collective-permute-start | bytes 884744 | tf_op jit(solution)/shard_map/ppermute | solution.py:21
  23.2 8.9 %copy-start = (bf16[1152,3,288]{0,2,1:T(8,128)(2,1)S(1)}, bf16[1152,3,288]{0,2,1:T(8,128)(2,1)}, u32[]{:S(2)}) copy-start(bf16[1152,3,288]{0,2,1:T(8,128)(2,1)} %param.13) | copy-start | bytes 5971972
  23.2 8.9 %copy-start.2 = (f32[2,72]{1,0:T(2,128)S(1)}, f32[2,72]{1,0:T(2,128)}, u32[]{:S(2)}) copy-start(f32[2,72]{1,0:T(2,128)} %gain_ref.5) | copy-start | bytes 1732
  24.0 6.7 %collective-permute-start.10 = (bf16[64,1152]{1,0:T(8,128)(2,1)S(1)}, bf16[64,1152]{1,0:T(8,128)(2,1)S(1)}, u32[]{:S(2)}, u32[]{:S(2)}) collective-permute-start(bf16[64,1152]{1,0:T(8,128)(2,1)S(1)} %get-tuple-element.72), channel_id=1, source_target_pairs={{0,1},{1,0},{2,3},{3,2},{4,5},{5,4},{6,7},{7,6},{8,9},{9,8},{10,11... | collective-permute-start | bytes 442376 | tf_op jit(solution)/shard_map/ppermute | solution.py:21
  25.4 6.7 %collective-permute-start.9 = (bf16[64,1152]{1,0:T(8,128)(2,1)S(1)}, bf16[64,1152]{1,0:T(8,128)(2,1)S(1)}, u32[]{:S(2)}, u32[]{:S(2)}) collective-permute-start(bf16[64,1152]{1,0:T(8,128)(2,1)S(1)} %get-tuple-element.71), channel_id=1, source_target_pairs={{0,2},{1,3},{2,0},{3,1},{4,6},{5,7},{6,4},{7,5},{8,10},{9,11},{10,... | collective-permute-start | bytes 442376 | tf_op jit(solution)/shard_map/ppermute | solution.py:21
  26.9 10.1 %collective-permute-start.8 = (bf16[128,1152]{1,0:T(8,128)(2,1)S(1)}, bf16[128,1152]{1,0:T(8,128)(2,1)S(1)}, u32[]{:S(2)}, u32[]{:S(2)}) collective-permute-start(bf16[128,1152]{1,0:T(8,128)(2,1)S(1)} %shard_map.86.refs_0_), channel_id=1, source_target_pairs={{0,1},{1,0},{2,3},{3,2},{4,5},{5,4},{6,7},{7,6},{8,9},{9,8},{10,11... | collective-permute-start | bytes 884744 | tf_op jit(solution)/shard_map/ppermute | solution.py:21
  27.5 14.1 %collective-permute-start.11 = (bf16[128,1152]{1,0:T(8,128)(2,1)S(1)}, bf16[128,1152]{1,0:T(8,128)(2,1)S(1)}, u32[]{:S(2)}, u32[]{:S(2)}) collective-permute-start(bf16[128,1152]{1,0:T(8,128)(2,1)S(1)} %shard_map.86.refs_0_), channel_id=1, source_target_pairs={{0,2},{1,3},{2,0},{3,1},{4,6},{5,7},{6,4},{7,5},{8,10},{9,11},{10,... | collective-permute-start | bytes 884744 | tf_op jit(solution)/shard_map/ppermute | solution.py:21
  28.1 13.5 %collective-permute-start.12 = (bf16[128,1152]{1,0:T(8,128)(2,1)S(1)}, bf16[128,1152]{1,0:T(8,128)(2,1)S(1)}, u32[]{:S(2)}, u32[]{:S(2)}) collective-permute-start(bf16[128,1152]{1,0:T(8,128)(2,1)S(1)} %shard_map.86.refs_0_), channel_id=1, source_target_pairs={{0,3},{1,2},{2,1},{3,0},{4,7},{5,6},{6,5},{7,4},{8,11},{9,10},{10,... | collective-permute-start | bytes 884744 | tf_op jit(solution)/shard_map/ppermute | solution.py:21
  33.5 2.3 %copy-start.3 = (s32[1,4]{1,0:T(1,128)S(1)}, s32[1,4]{1,0:T(1,128)}, u32[]{:S(2)}) copy-start(s32[1,4]{1,0:T(1,128)} %length_ref.3) | copy-start | bytes 52
  35.2 7.2 %collective-permute-start.13 = (bf16[144,1152]{1,0:T(8,128)(2,1)S(1)}, bf16[144,1152]{1,0:T(8,128)(2,1)S(1)}, u32[]{:S(2)}, u32[]{:S(2)}) collective-permute-start(bf16[144,1152]{1,0:T(8,128)(2,1)S(1)} %collective-permute-done.4.refs_4_), channel_id=1, source_target_pairs={{0,4},{4,0},{8,12},{12,8},{16,20},{20,16},{24,28},{28,24},{1,5},{5... | collective-permute-start | bytes 995336 | tf_op jit(solution)/shard_map/ppermute | solution.py:21
  35.3 7.1 %collective-permute-start.14 = (bf16[144,1152]{1,0:T(8,128)(2,1)S(1)}, bf16[144,1152]{1,0:T(8,128)(2,1)S(1)}, u32[]{:S(2)}, u32[]{:S(2)}) collective-permute-start(bf16[144,1152]{1,0:T(8,128)(2,1)S(1)} %collective-permute-done.5.refs_6_), channel_id=1, source_target_pairs={{0,4},{4,0},{8,12},{12,8},{16,20},{20,16},{24,28},{28,24},{1,5},{5... | collective-permute-start | bytes 995336 | tf_op jit(solution)/shard_map/ppermute | solution.py:21
  39.1 11.0 %collective-permute-start.18 = (bf16[144,1152]{1,0:T(8,128)(2,1)S(1)}, bf16[144,1152]{1,0:T(8,128)(2,1)S(1)}, u32[]{:S(2)}, u32[]{:S(2)}) collective-permute-start(bf16[144,1152]{1,0:T(8,128)(2,1)S(1)} %collective-permute-done.5.refs_6_), channel_id=1, source_target_pairs={{0,1},{1,0},{2,3},{3,2},{4,5},{5,4},{6,7},{7,6},{8,9},{9,8},{10,11... | collective-permute-start | bytes 995336 | tf_op jit(solution)/shard_map/ppermute | solution.py:21
  46.6 6.9 %collective-permute-start.15 = (bf16[288,256]{1,0:T(8,128)(2,1)S(1)}, bf16[288,256]{1,0:T(8,128)(2,1)S(1)}, u32[]{:S(2)}, u32[]{:S(2)}) collective-permute-start(bf16[288,256]{1,0:T(8,128)(2,1)S(1)} %get-tuple-element.96), channel_id=1, source_target_pairs={{0,1},{1,0},{2,3},{3,2},{4,5},{5,4},{6,7},{7,6},{8,9},{9,8},{10,11... | collective-permute-start | bytes 442376 | tf_op jit(solution)/shard_map/ppermute | solution.py:21
  48.1 8.3 %collective-permute-start.16 = (bf16[288,256]{1,0:T(8,128)(2,1)S(1)}, bf16[288,256]{1,0:T(8,128)(2,1)S(1)}, u32[]{:S(2)}, u32[]{:S(2)}) collective-permute-start(bf16[288,256]{1,0:T(8,128)(2,1)S(1)} %get-tuple-element.97), channel_id=1, source_target_pairs={{0,2},{1,3},{2,0},{3,1},{4,6},{5,7},{6,4},{7,5},{8,10},{9,11},{10,... | collective-permute-start | bytes 442376 | tf_op jit(solution)/shard_map/ppermute | solution.py:21
  48.8 8.9 %collective-permute-start.17 = (bf16[288,256]{1,0:T(8,128)(2,1)S(1)}, bf16[288,256]{1,0:T(8,128)(2,1)S(1)}, u32[]{:S(2)}, u32[]{:S(2)}) collective-permute-start(bf16[288,256]{1,0:T(8,128)(2,1)S(1)} %get-tuple-element.102), channel_id=1, source_target_pairs={{0,3},{1,2},{2,1},{3,0},{4,7},{5,6},{6,5},{7,4},{8,11},{9,10},{10,... | collective-permute-start | bytes 442376 | tf_op jit(solution)/shard_map/ppermute | solution.py:21
  50.1 7.5 %collective-permute-start.19 = (bf16[144,1152]{1,0:T(8,128)(2,1)S(1)}, bf16[144,1152]{1,0:T(8,128)(2,1)S(1)}, u32[]{:S(2)}, u32[]{:S(2)}) collective-permute-start(bf16[144,1152]{1,0:T(8,128)(2,1)S(1)} %collective-permute-done.18.refs_1_), channel_id=1, source_target_pairs={{0,4},{4,0},{8,12},{12,8},{16,20},{20,16},{24,28},{28,24},{1,5},{5... | collective-permute-start | bytes 995336 | tf_op jit(solution)/shard_map/ppermute | solution.py:21
  58.3 7.9 %collective-permute-start.24 = (bf16[64,1152]{1,0:T(8,128)(2,1)S(1)}, bf16[64,1152]{1,0:T(8,128)(2,1)S(1)}, u32[]{:S(2)}, u32[]{:S(2)}) collective-permute-start(bf16[64,1152]{1,0:T(8,128)(2,1)S(1)} %get-tuple-element.109), channel_id=1, source_target_pairs={{0,8},{4,12},{8,0},{12,4},{16,24},{20,28},{24,16},{28,20},{1,9},{5... | collective-permute-start | bytes 442376 | tf_op jit(solution)/shard_map/ppermute | solution.py:21
  59.9 6.6 %collective-permute-start.20 = (bf16[32,1152]{1,0:T(8,128)(2,1)S(1)}, bf16[32,1152]{1,0:T(8,128)(2,1)S(1)}, u32[]{:S(2)}, u32[]{:S(2)}) collective-permute-start(bf16[32,1152]{1,0:T(8,128)(2,1)S(1)} %get-tuple-element.104), channel_id=1, source_target_pairs={{0,16},{4,20},{8,24},{12,28},{16,0},{20,4},{24,8},{28,12},{1,17},{... | collective-permute-start | bytes 221192 | tf_op jit(solution)/shard_map/ppermute | solution.py:21
  62.5 10.4 %collective-permute-start.21 = (bf16[32,1152]{1,0:T(8,128)(2,1)S(1)}, bf16[32,1152]{1,0:T(8,128)(2,1)S(1)}, u32[]{:S(2)}, u32[]{:S(2)}) collective-permute-start(bf16[32,1152]{1,0:T(8,128)(2,1)S(1)} %get-tuple-element.105), channel_id=1, source_target_pairs={{0,20},{4,16},{8,28},{12,24},{16,4},{20,0},{24,12},{28,8},{1,21},{... | collective-permute-start | bytes 221192 | tf_op jit(solution)/shard_map/ppermute | solution.py:21
  62.5 10.4 %collective-permute-start.22 = (bf16[32,1152]{1,0:T(8,128)(2,1)S(1)}, bf16[32,1152]{1,0:T(8,128)(2,1)S(1)}, u32[]{:S(2)}, u32[]{:S(2)}) collective-permute-start(bf16[32,1152]{1,0:T(8,128)(2,1)S(1)} %get-tuple-element.106), channel_id=1, source_target_pairs={{0,24},{4,28},{8,16},{12,20},{16,8},{20,12},{24,0},{28,4},{1,25},{... | collective-permute-start | bytes 221192 | tf_op jit(solution)/shard_map/ppermute | solution.py:21
  62.7 10.2 %collective-permute-start.23 = (bf16[32,1152]{1,0:T(8,128)(2,1)S(1)}, bf16[32,1152]{1,0:T(8,128)(2,1)S(1)}, u32[]{:S(2)}, u32[]{:S(2)}) collective-permute-start(bf16[32,1152]{1,0:T(8,128)(2,1)S(1)} %get-tuple-element.107), channel_id=1, source_target_pairs={{0,28},{4,24},{8,20},{12,16},{16,12},{20,8},{24,4},{28,0},{1,29},{... | collective-permute-start | bytes 221192 | tf_op jit(solution)/shard_map/ppermute | solution.py:21
  66.2 6.8 %copy-start.7 = (s32[64]{0:T(128)S(1)}, s32[64]{0:T(128)}, u32[]{:S(2)}) copy-start(s32[64]{0:T(128)} %get-tuple-element.58.slot_ref) | copy-start | bytes 772
  66.2 6.8 %collective-permute-start.25 = (bf16[64,1152]{1,0:T(8,128)(2,1)S(1)}, bf16[64,1152]{1,0:T(8,128)(2,1)S(1)}, u32[]{:S(2)}, u32[]{:S(2)}) collective-permute-start(bf16[64,1152]{1,0:T(8,128)(2,1)S(1)} %shard_map.99), channel_id=1, source_target_pairs={{0,4},{4,0},{8,12},{12,8},{16,20},{20,16},{24,28},{28,24},{1,5},{5... | collective-permute-start | bytes 442376 | tf_op jit(solution)/shard_map/ppermute | solution.py:21
